TPU v7x, 32 devices: a whole 2x2x4 slice. The times are simulated.
32 devices in a mesh: runs: 2 (over y), space: 4 (over z), spec: 4 (over x, core).
Axes of the slice: x: 2, y: 2, z: 4, core: 2. Of those that a mesh axis runs over, the one named last changes fastest.
Arguments:
- spectrum: float32 [36, 36, 1024], P('spec', None, ('runs', 'space')), parts along dimension 2, may hold values from 0.012 to 6.01, as said below
- courant: float32 [36, 36, 512], P('spec', None, 'space'), may hold values from 0.1 to 0.9
- refraction: float32 [36, 36, 512], P('spec', None, 'space'), may hold values from -0.4 to 0.4
- growth: float32 [36, 1024], P(None, ('runs', 'space')), parts along dimension 1, may hold values from 0 to 0.5
- dissip: float32 [36], replicated, may hold values from 0.5 to 2
- upwind: int32 [36, 512], P('spec', 'space'), may hold values from 0 to 511, as said below
- send_order: int32 [512], P('space'), may hold values from 0 to 511, as said below
Outputs:
- energy_out: float32 [36, 36, 1024], P('spec', None, ('runs', 'space')), parts along dimension 2
- series: float32 [12, 1024], P(None, ('runs', 'space')), parts along dimension 1
There are 2 independent parts, one for each index of `runs`. A program takes and returns all parts, laid end to end along the dimension named above; an argument that names none is the same for every part. Nothing has to cross between parts.
Inputs may be any that keep to these rules, and one draw needn't show every extreme that they name: Each point and its upwind point lie within 16 positions of each other in the cyclic order of points; offsets of exactly 16 and - 16 occur. `send_order`: entries s * 128 to (s + 1) * 128 - 1 are a permutation of the points of tile s. `spectrum`: positive energies.
All inputs are finite; a program needn't handle non-finite values.
Results may differ from a plain program's by a relative error of at most 0.0001.
Values sent between devices are 32-bit elements; how exact they have to be, the bound alone decides.
No kernel may reach another device: no remote copies, remote signals or barrier semaphores. Data moves between devices by JAX's collectives and lax.ppermute only.
A program may use at most 64 MiB of HBM per device.

v0:
```python
import jax
import jax.numpy as jnp
from jax import lax
from jax.sharding import PartitionSpec as P

STEPS = 6


def passed_along(block, axis, distance):
    devices = range(lax.axis_size(axis))
    route = [((i - distance) % len(devices), i) for i in devices]
    return lax.ppermute(block, axis, route)


def padded_2(cells, sides, width):
    for axis, dim in sides:
        count = lax.axis_size(axis)
        head = lax.slice_in_dim(cells, 0, width, axis=dim)
        tail = lax.slice_in_dim(cells, cells.shape[dim] - width, cells.shape[dim], axis=dim)
        cells = jnp.concatenate(
            [
                lax.ppermute(tail, axis, [(i, (i + 1) % count) for i in range(count)]),
                cells,
                lax.ppermute(head, axis, [((i + 1) % count, i) for i in range(count)]),
            ],
            axis=dim,
        )
    return cells


def frequency_table(count):
    return 0.035 * jnp.float32(1.1) ** jnp.arange(count, dtype=jnp.float32)


def upwind_matrix(local_up, width):
    columns = jnp.arange(width, dtype=jnp.int32)[None, :, None]
    return (local_up[:, None, :] == columns).astype(jnp.float32)


def advect(padded, courant, energy, selector):
    upstream = jnp.einsum("gfw,gwp->gfp", padded, selector, precision=lax.Precision.HIGHEST)
    return energy + courant * (upstream - energy)


def apply_source(turned, growth, dissip, total, bins):
    mean_energy = total / bins
    return turned * (1.0 + growth)[None] / (1.0 + dissip[:, None] * mean_energy[None, :])[None]


def field_pair(zeroth, first, bins):
    return jnp.stack([4.0 * jnp.sqrt(zeroth / bins), zeroth / first])


def arrange(fields, send_local, tiles):
    ordered = jnp.take(fields, send_local, axis=1)
    return ordered.reshape(fields.shape[0], tiles, fields.shape[1] // tiles)


def on_device(spectrum, courant, refraction, growth, dissip, upwind, send_order):
    groups, nfreq, npt = spectrum.shape
    tiles = lax.axis_size("space")
    tile = lax.axis_index("space")
    spec_count = lax.axis_size("spec")
    total_points = npt * tiles
    reach = npt // 8
    bins = groups * spec_count * nfreq
    freqs = frequency_table(nfreq)
    send_local = send_order - tile * npt
    hour_fields = []
    local_up = jnp.mod(upwind - tile * npt + reach, total_points)
    selector = upwind_matrix(local_up, npt + 2 * reach)
    prev_rate = passed_along(refraction[-1:], "spec", 1)
    rates = jnp.concatenate([prev_rate, refraction], axis=0)
    energy = spectrum
    for hour in range(STEPS):
        padded = padded_2(energy, (("space", 2),), reach)
        moved = advect(padded, courant, energy, selector)
        extended = padded_2(moved, (("spec", 0),), 1)
        flux = jnp.maximum(rates, 0.0) * extended[:-1] + jnp.minimum(rates, 0.0) * extended[1:]
        turned = moved - flux[1:] + flux[:-1]
        total = lax.psum(jnp.sum(turned, axis=(0, 1)), "spec")
        energy = apply_source(turned, growth, dissip, total, bins)
        zeroth_part = jnp.sum(energy, axis=(0, 1))
        first_part = jnp.sum(energy * freqs[None, :, None], axis=(0, 1))
        zeroth, first = lax.psum((zeroth_part, first_part), "spec")
        hour_fields.append(field_pair(zeroth, first, bins))
    stacked = jnp.stack(hour_fields).transpose(1, 0, 2).reshape(2 * STEPS, npt)
    series = lax.all_to_all(
        arrange(stacked, send_local, tiles), "space", split_axis=1, concat_axis=1, tiled=True
    ).reshape(2 * STEPS, npt)
    return (energy, series)


def solution(mesh):
    placed = (
        P("spec", None, ("runs", "space")),
        P("spec", None, "space"),
        P("spec", None, "space"),
        P(None, ("runs", "space")),
        P(),
        P("spec", "space"),
        P("space"),
    )
    return jax.shard_map(
        on_device,
        mesh=mesh,
        in_specs=placed,
        out_specs=(P("spec", None, ("runs", "space")), P(None, ("runs", "space"))),
        check_vma=False,
    )
```

profile of v0, /device:TPU:0, one launch (start us, length us, event | category | flops | bytes accessed | tf_op | source)
XLA Modules:
  0.0 155.2 jit_solution(9932668744062366996)
XLA Ops:
  1.8 3.1 %collective-permute-start = (f32[9,36,16]{2,1,0:T(8,128)S(1)}, f32[9,36,16]{2,1,0:T(8,128)S(1)}, u32[]{:S(2)}, u32[]{:S(2)}) collective-permute-start(f32[9,36,16]{2,1,0:T(8,128)S(1)} %get-tuple-element.61), channel_id=1, source_target_pairs={{0,4},{4,8},{8,12},{12,0},{1,5},{5,9},{9,13},{13,1},{2,6},{6,10},{... | collective-permute-start | bytes 62216 | tf_op jit(solution)/shard_map/ppermute | solution.py:22
  4.9 2.1 %collective-permute-start.1 = (f32[9,36,16]{2,1,0:T(8,128)S(1)}, f32[9,36,16]{2,1,0:T(8,128)S(1)}, u32[]{:S(2)}, u32[]{:S(2)}) collective-permute-start(f32[9,36,16]{2,1,0:T(8,128)S(1)} %get-tuple-element.62), channel_id=1, source_target_pairs={{4,0},{8,4},{12,8},{0,12},{5,1},{9,5},{13,9},{1,13},{6,2},{10,6},{... | collective-permute-start | bytes 62216 | tf_op jit(solution)/shard_map/ppermute | solution.py:24
  7.8 2.5 %collective-permute-done.2 = f32[1,36,128]{2,1,0:T(8,128)S(1)} collective-permute-done((f32[1,36,128]{2,1,0:T(8,128)S(1)}, f32[1,36,128]{2,1,0:T(8,128)S(1)}, u32[]{:S(2)}, u32[]{:S(2)}) %collective-permute-start.2) | collective-permute-done | bytes 18464 | tf_op jit(solution)/shard_map/ppermute | solution.py:12
  10.2 2.2 %collective-permute-done = f32[9,36,16]{2,1,0:T(8,128)S(1)} collective-permute-done((f32[9,36,16]{2,1,0:T(8,128)S(1)}, f32[9,36,16]{2,1,0:T(8,128)S(1)}, u32[]{:S(2)}, u32[]{:S(2)}) %collective-permute-start) | collective-permute-done | bytes 20768 | tf_op jit(solution)/shard_map/ppermute | solution.py:22
  12.5 2.5 %collective-permute-done.1 = f32[9,36,16]{2,1,0:T(8,128)S(1)} collective-permute-done((f32[9,36,16]{2,1,0:T(8,128)S(1)}, f32[9,36,16]{2,1,0:T(8,128)S(1)}, u32[]{:S(2)}, u32[]{:S(2)}) %collective-permute-start.1) | collective-permute-done | bytes 20768 | tf_op jit(solution)/shard_map/ppermute | solution.py:24
  15.6 1.7 %collective-permute-start.4 = (f32[1,36,128]{2,1,0:T(8,128)S(1)}, f32[1,36,128]{2,1,0:T(8,128)S(1)}, u32[]{:S(2)}, u32[]{:S(2)}) collective-permute-start(f32[1,36,128]{2,1,0:T(8,128)S(1)} %get-tuple-element.59), channel_id=1, source_target_pairs={{1,0},{2,1},{3,2},{0,3},{5,4},{6,5},{7,6},{4,7},{9,8},{10,9},{11,1... | collective-permute-start | bytes 55304 | tf_op jit(solution)/shard_map/ppermute | solution.py:24
  19.0 7.4 %psum.126 = f32[128]{0:T(128)S(1)} all-reduce(f32[128]{0:T(128)S(1)} %fusion.61), channel_id=1, replica_groups=mesh['runs'=2,'space'=4,'spec'=4] {'spec'}, use_global_device_ids=true, to_apply=%region_1.2 | all-reduce | flops 128 | bytes 1024 | tf_op jit(solution)/shard_map/psum | solution.py:81
  28.4 2.7 %collective-permute-start.6 = (f32[9,36,16]{2,1,0:T(8,128)S(1)}, f32[9,36,16]{2,1,0:T(8,128)S(1)}, u32[]{:S(2)}, u32[]{:S(2)}) collective-permute-start(f32[9,36,16]{2,1,0:T(8,128)S(1)} %get-tuple-element.58), channel_id=1, source_target_pairs={{4,0},{8,4},{12,8},{0,12},{5,1},{9,5},{13,9},{1,13},{6,2},{10,6},{... | collective-permute-start | bytes 62216 | tf_op jit(solution)/shard_map/ppermute | solution.py:24
  31.1 5.6 %collective-permute-done.5 = f32[9,36,16]{2,1,0:T(8,128)S(1)} collective-permute-done((f32[9,36,16]{2,1,0:T(8,128)S(1)}, f32[9,36,16]{2,1,0:T(8,128)S(1)}, u32[]{:S(2)}, u32[]{:S(2)}) %collective-permute-start.5) | collective-permute-done | bytes 20768 | tf_op jit(solution)/shard_map/ppermute | solution.py:22
  38.6 1.7 %collective-permute-start.8 = (f32[1,36,128]{2,1,0:T(8,128)S(1)}, f32[1,36,128]{2,1,0:T(8,128)S(1)}, u32[]{:S(2)}, u32[]{:S(2)}) collective-permute-start(f32[1,36,128]{2,1,0:T(8,128)S(1)} %get-tuple-element.55), channel_id=1, source_target_pairs={{1,0},{2,1},{3,2},{0,3},{5,4},{6,5},{7,6},{4,7},{9,8},{10,9},{11,1... | collective-permute-start | bytes 55304 | tf_op jit(solution)/shard_map/ppermute | solution.py:24
  41.9 7.4 %psum.127 = f32[128]{0:T(128)S(1)} all-reduce(f32[128]{0:T(128)S(1)} %fusion.62), channel_id=1, replica_groups=mesh['runs'=2,'space'=4,'spec'=4] {'spec'}, use_global_device_ids=true, to_apply=%region_3.4 | all-reduce | flops 128 | bytes 1024 | tf_op jit(solution)/shard_map/psum | solution.py:81
  49.5 2.1 %collective-permute-start.10 = (f32[9,36,16]{2,1,0:T(8,128)S(1)}, f32[9,36,16]{2,1,0:T(8,128)S(1)}, u32[]{:S(2)}, u32[]{:S(2)}) collective-permute-start(f32[9,36,16]{2,1,0:T(8,128)S(1)} %get-tuple-element.54), channel_id=1, source_target_pairs={{4,0},{8,4},{12,8},{0,12},{5,1},{9,5},{13,9},{1,13},{6,2},{10,6},{... | collective-permute-start | bytes 62216 | tf_op jit(solution)/shard_map/ppermute | solution.py:24
  51.7 4.9 %collective-permute-done.10 = f32[9,36,16]{2,1,0:T(8,128)S(1)} collective-permute-done((f32[9,36,16]{2,1,0:T(8,128)S(1)}, f32[9,36,16]{2,1,0:T(8,128)S(1)}, u32[]{:S(2)}, u32[]{:S(2)}) %collective-permute-start.10) | collective-permute-done | bytes 20768 | tf_op jit(solution)/shard_map/ppermute | solution.py:24
  56.6 3.5 %collective-permute-done.9 = f32[9,36,16]{2,1,0:T(8,128)S(1)} collective-permute-done((f32[9,36,16]{2,1,0:T(8,128)S(1)}, f32[9,36,16]{2,1,0:T(8,128)S(1)}, u32[]{:S(2)}, u32[]{:S(2)}) %collective-permute-start.9) | collective-permute-done | bytes 20768 | tf_op jit(solution)/shard_map/ppermute | solution.py:22
  60.7 1.7 %collective-permute-start.12 = (f32[1,36,128]{2,1,0:T(8,128)S(1)}, f32[1,36,128]{2,1,0:T(8,128)S(1)}, u32[]{:S(2)}, u32[]{:S(2)}) collective-permute-start(f32[1,36,128]{2,1,0:T(8,128)S(1)} %get-tuple-element.51), channel_id=1, source_target_pairs={{1,0},{2,1},{3,2},{0,3},{5,4},{6,5},{7,6},{4,7},{9,8},{10,9},{11,1... | collective-permute-start | bytes 55304 | tf_op jit(solution)/shard_map/ppermute | solution.py:24
  64.0 7.4 %psum.128 = f32[128]{0:T(128)S(1)} all-reduce(f32[128]{0:T(128)S(1)} %fusion.63), channel_id=1, replica_groups=mesh['runs'=2,'space'=4,'spec'=4] {'spec'}, use_global_device_ids=true, to_apply=%region_5.6 | all-reduce | flops 128 | bytes 1024 | tf_op jit(solution)/shard_map/psum | solution.py:81
  72.6 2.9 %collective-permute-start.14 = (f32[9,36,16]{2,1,0:T(8,128)S(1)}, f32[9,36,16]{2,1,0:T(8,128)S(1)}, u32[]{:S(2)}, u32[]{:S(2)}) collective-permute-start(f32[9,36,16]{2,1,0:T(8,128)S(1)} %get-tuple-element.50), channel_id=1, source_target_pairs={{4,0},{8,4},{12,8},{0,12},{5,1},{9,5},{13,9},{1,13},{6,2},{10,6},{... | collective-permute-start | bytes 62216 | tf_op jit(solution)/shard_map/ppermute | solution.py:24
  75.5 5.3 %collective-permute-done.13 = f32[9,36,16]{2,1,0:T(8,128)S(1)} collective-permute-done((f32[9,36,16]{2,1,0:T(8,128)S(1)}, f32[9,36,16]{2,1,0:T(8,128)S(1)}, u32[]{:S(2)}, u32[]{:S(2)}) %collective-permute-start.13) | collective-permute-done | bytes 20768 | tf_op jit(solution)/shard_map/ppermute | solution.py:22
  82.4 1.7 %collective-permute-start.16 = (f32[1,36,128]{2,1,0:T(8,128)S(1)}, f32[1,36,128]{2,1,0:T(8,128)S(1)}, u32[]{:S(2)}, u32[]{:S(2)}) collective-permute-start(f32[1,36,128]{2,1,0:T(8,128)S(1)} %get-tuple-element.47), channel_id=1, source_target_pairs={{1,0},{2,1},{3,2},{0,3},{5,4},{6,5},{7,6},{4,7},{9,8},{10,9},{11,1... | collective-permute-start | bytes 55304 | tf_op jit(solution)/shard_map/ppermute | solution.py:24
  85.7 7.4 %psum.129 = f32[128]{0:T(128)S(1)} all-reduce(f32[128]{0:T(128)S(1)} %fusion.64), channel_id=1, replica_groups=mesh['runs'=2,'space'=4,'spec'=4] {'spec'}, use_global_device_ids=true, to_apply=%region_7.8 | all-reduce | flops 128 | bytes 1024 | tf_op jit(solution)/shard_map/psum | solution.py:81
  93.8 3.5 %collective-permute-start.18 = (f32[9,36,16]{2,1,0:T(8,128)S(1)}, f32[9,36,16]{2,1,0:T(8,128)S(1)}, u32[]{:S(2)}, u32[]{:S(2)}) collective-permute-start(f32[9,36,16]{2,1,0:T(8,128)S(1)} %get-tuple-element.46), channel_id=1, source_target_pairs={{4,0},{8,4},{12,8},{0,12},{5,1},{9,5},{13,9},{1,13},{6,2},{10,6},{... | collective-permute-start | bytes 62216 | tf_op jit(solution)/shard_map/ppermute | solution.py:24
  97.2 5.4 %collective-permute-done.17 = f32[9,36,16]{2,1,0:T(8,128)S(1)} collective-permute-done((f32[9,36,16]{2,1,0:T(8,128)S(1)}, f32[9,36,16]{2,1,0:T(8,128)S(1)}, u32[]{:S(2)}, u32[]{:S(2)}) %collective-permute-start.17) | collective-permute-done | bytes 20768 | tf_op jit(solution)/shard_map/ppermute | solution.py:22
  103.6 1.7 %collective-permute-start.20 = (f32[1,36,128]{2,1,0:T(8,128)S(1)}, f32[1,36,128]{2,1,0:T(8,128)S(1)}, u32[]{:S(2)}, u32[]{:S(2)}) collective-permute-start(f32[1,36,128]{2,1,0:T(8,128)S(1)} %get-tuple-element.43), channel_id=1, source_target_pairs={{1,0},{2,1},{3,2},{0,3},{5,4},{6,5},{7,6},{4,7},{9,8},{10,9},{11,1... | collective-permute-start | bytes 55304 | tf_op jit(solution)/shard_map/ppermute | solution.py:24
  107.0 7.4 %psum.130 = f32[128]{0:T(128)S(1)} all-reduce(f32[128]{0:T(128)S(1)} %fusion.65), channel_id=1, replica_groups=mesh['runs'=2,'space'=4,'spec'=4] {'spec'}, use_global_device_ids=true, to_apply=%region_9.10 | all-reduce | flops 128 | bytes 1024 | tf_op jit(solution)/shard_map/psum | solution.py:81
  114.6 1.8 %collective-permute-start.21 = (f32[9,36,16]{2,1,0:T(8,128)S(1)}, f32[9,36,16]{2,1,0:T(8,128)S(1)}, u32[]{:S(2)}, u32[]{:S(2)}) collective-permute-start(f32[9,36,16]{2,1,0:T(8,128)S(1)} %get-tuple-element.41), channel_id=1, source_target_pairs={{0,4},{4,8},{8,12},{12,0},{1,5},{5,9},{9,13},{13,1},{2,6},{6,10},{... | collective-permute-start | bytes 62216 | tf_op jit(solution)/shard_map/ppermute | solution.py:22
  116.4 2.1 %collective-permute-start.22 = (f32[9,36,16]{2,1,0:T(8,128)S(1)}, f32[9,36,16]{2,1,0:T(8,128)S(1)}, u32[]{:S(2)}, u32[]{:S(2)}) collective-permute-start(f32[9,36,16]{2,1,0:T(8,128)S(1)} %get-tuple-element.42), channel_id=1, source_target_pairs={{4,0},{8,4},{12,8},{0,12},{5,1},{9,5},{13,9},{1,13},{6,2},{10,6},{... | collective-permute-start | bytes 62216 | tf_op jit(solution)/shard_map/ppermute | solution.py:24
  118.5 5.3 %collective-permute-done.21 = f32[9,36,16]{2,1,0:T(8,128)S(1)} collective-permute-done((f32[9,36,16]{2,1,0:T(8,128)S(1)}, f32[9,36,16]{2,1,0:T(8,128)S(1)}, u32[]{:S(2)}, u32[]{:S(2)}) %collective-permute-start.21) | collective-permute-done | bytes 20768 | tf_op jit(solution)/shard_map/ppermute | solution.py:22
  123.7 1.6 %collective-permute-done.22 = f32[9,36,16]{2,1,0:T(8,128)S(1)} collective-permute-done((f32[9,36,16]{2,1,0:T(8,128)S(1)}, f32[9,36,16]{2,1,0:T(8,128)S(1)}, u32[]{:S(2)}, u32[]{:S(2)}) %collective-permute-start.22) | collective-permute-done | bytes 20768 | tf_op jit(solution)/shard_map/ppermute | solution.py:24
  126.0 1.7 %collective-permute-start.24 = (f32[1,36,128]{2,1,0:T(8,128)S(1)}, f32[1,36,128]{2,1,0:T(8,128)S(1)}, u32[]{:S(2)}, u32[]{:S(2)}) collective-permute-start(f32[1,36,128]{2,1,0:T(8,128)S(1)} %get-tuple-element.39), channel_id=1, source_target_pairs={{1,0},{2,1},{3,2},{0,3},{5,4},{6,5},{7,6},{4,7},{9,8},{10,9},{11,1... | collective-permute-start | bytes 55304 | tf_op jit(solution)/shard_map/ppermute | solution.py:24
  129.3 7.4 %psum.131 = f32[128]{0:T(128)S(1)} all-reduce(f32[128]{0:T(128)S(1)} %fusion.66), channel_id=1, replica_groups=mesh['runs'=2,'space'=4,'spec'=4] {'spec'}, use_global_device_ids=true, to_apply=%region_11.12 | all-reduce | flops 128 | bytes 1024 | tf_op jit(solution)/shard_map/psum | solution.py:81
  137.7 5.7 %all-reduce = (f32[128]{0:T(128)S(1)}, f32[128]{0:T(128)S(1)}, f32[128]{0:T(128)S(1)}, f32[128]{0:T(128)S(1)}, f32[128]{0:T(128)S(1)}, /*index=5*/f32[128]{0:T(1...) all-reduce(f32[128]{0:T(128)S(1)} %get-tuple-element.22, ...), channel_id=1, replica_groups=mesh['runs'=2,'space'=4,'spec'=4] {'spec'}, use_global_device_ids=true, to_apply=%region_13.14 | all-reduce | flops 1536 | bytes 12288 | tf_op jit(solution)/shard_map/psum | solution.py:85
  144.5 8.7 %all_to_all.5 = f32[4,1,384]{2,1,0:T(1,128)S(1)} all-to-all(f32[4,1,384]{2,1,0:T(1,128)S(1)} %reshape.198), channel_id=1, replica_groups=mesh['runs'=2,'space'=4,'spec'=4] {'space'}, dimensions={0} | all-to-all | bytes 12288 | tf_op jit(solution)/shard_map/all_to_all | solution.py:88
  (118 shorter events, 26.3 us)
Async XLA Ops:
  0.6 6.4 %copy-start.2 = (f32[9,36,128]{2,1,0:T(8,128)S(1)}, f32[9,36,128]{2,1,0:T(8,128)}, u32[]{:S(2)}) copy-start(f32[9,36,128]{2,1,0:T(8,128)} %param.9) | copy-start | bytes 497668
  0.6 14.3 %copy-start = (f32[9,36,128]{2,1,0:T(8,128)S(1)}, f32[9,36,128]{2,1,0:T(8,128)}, u32[]{:S(2)}) copy-start(f32[9,36,128]{2,1,0:T(8,128)} %param.8) | copy-start | bytes 497668
  0.6 14.3 %copy-start.1 = (f32[9,36,128]{2,1,0:T(8,128)S(1)}, f32[9,36,128]{2,1,0:T(8,128)}, u32[]{:S(2)}) copy-start(f32[9,36,128]{2,1,0:T(8,128)} %param.7) | copy-start | bytes 497668
  1.8 10.6 %collective-permute-start = (f32[9,36,16]{2,1,0:T(8,128)S(1)}, f32[9,36,16]{2,1,0:T(8,128)S(1)}, u32[]{:S(2)}, u32[]{:S(2)}) collective-permute-start(f32[9,36,16]{2,1,0:T(8,128)S(1)} %get-tuple-element.61), channel_id=1, source_target_pairs={{0,4},{4,8},{8,12},{12,0},{1,5},{5,9},{9,13},{13,1},{2,6},{6,10},{... | collective-permute-start | bytes 62216 | tf_op jit(solution)/shard_map/ppermute | solution.py:22
  4.9 2.1 %copy-start.3 = (f32[36,128]{1,0:T(8,128)S(1)}, f32[36,128]{1,0:T(8,128)}, u32[]{:S(2)}) copy-start(f32[36,128]{1,0:T(8,128)} %param.10) | copy-start | bytes 55300
  4.9 10.0 %collective-permute-start.1 = (f32[9,36,16]{2,1,0:T(8,128)S(1)}, f32[9,36,16]{2,1,0:T(8,128)S(1)}, u32[]{:S(2)}, u32[]{:S(2)}) collective-permute-start(f32[9,36,16]{2,1,0:T(8,128)S(1)} %get-tuple-element.62), channel_id=1, source_target_pairs={{4,0},{8,4},{12,8},{0,12},{5,1},{9,5},{13,9},{1,13},{6,2},{10,6},{... | collective-permute-start | bytes 62216 | tf_op jit(solution)/shard_map/ppermute | solution.py:24
  7.0 3.2 %collective-permute-start.2 = (f32[1,36,128]{2,1,0:T(8,128)S(1)}, f32[1,36,128]{2,1,0:T(8,128)S(1)}, u32[]{:S(2)}, u32[]{:S(2)}) collective-permute-start(f32[1,36,128]{2,1,0:T(8,128)S(1)} %slice.137), channel_id=1, source_target_pairs={{3,0},{0,1},{1,2},{2,3},{7,4},{4,5},{5,6},{6,7},{11,8},{8,9},{9,10... | collective-permute-start | bytes 55304 | tf_op jit(solution)/shard_map/ppermute | solution.py:12
  7.0 0.7 copy-start.5
  15.5 3.3 %collective-permute-start.3 = (f32[1,36,128]{2,1,0:T(8,128)S(1)}, f32[1,36,128]{2,1,0:T(8,128)S(1)}, u32[]{:S(2)}, u32[]{:S(2)}) collective-permute-start(f32[1,36,128]{2,1,0:T(8,128)S(1)} %get-tuple-element.60), channel_id=1, source_target_pairs={{0,1},{1,2},{2,3},{3,0},{4,5},{5,6},{6,7},{7,4},{8,9},{9,10},{10,1... | collective-permute-start | bytes 55304 | tf_op jit(solution)/shard_map/ppermute | solution.py:22
  15.6 3.2 %collective-permute-start.4 = (f32[1,36,128]{2,1,0:T(8,128)S(1)}, f32[1,36,128]{2,1,0:T(8,128)S(1)}, u32[]{:S(2)}, u32[]{:S(2)}) collective-permute-start(f32[1,36,128]{2,1,0:T(8,128)S(1)} %get-tuple-element.59), channel_id=1, source_target_pairs={{1,0},{2,1},{3,2},{0,3},{5,4},{6,5},{7,6},{4,7},{9,8},{10,9},{11,1... | collective-permute-start | bytes 55304 | tf_op jit(solution)/shard_map/ppermute | solution.py:24
  26.3 0.7 copy-start.4
  27.2 9.4 %collective-permute-start.5 = (f32[9,36,16]{2,1,0:T(8,128)S(1)}, f32[9,36,16]{2,1,0:T(8,128)S(1)}, u32[]{:S(2)}, u32[]{:S(2)}) collective-permute-start(f32[9,36,16]{2,1,0:T(8,128)S(1)} %get-tuple-element.57), channel_id=1, source_target_pairs={{0,4},{4,8},{8,12},{12,0},{1,5},{5,9},{9,13},{13,1},{2,6},{6,10},{... | collective-permute-start | bytes 62216 | tf_op jit(solution)/shard_map/ppermute | solution.py:22
  28.4 9.5 %collective-permute-start.6 = (f32[9,36,16]{2,1,0:T(8,128)S(1)}, f32[9,36,16]{2,1,0:T(8,128)S(1)}, u32[]{:S(2)}, u32[]{:S(2)}) collective-permute-start(f32[9,36,16]{2,1,0:T(8,128)S(1)} %get-tuple-element.58), channel_id=1, source_target_pairs={{4,0},{8,4},{12,8},{0,12},{5,1},{9,5},{13,9},{1,13},{6,2},{10,6},{... | collective-permute-start | bytes 62216 | tf_op jit(solution)/shard_map/ppermute | solution.py:24
  38.5 3.3 %collective-permute-start.7 = (f32[1,36,128]{2,1,0:T(8,128)S(1)}, f32[1,36,128]{2,1,0:T(8,128)S(1)}, u32[]{:S(2)}, u32[]{:S(2)}) collective-permute-start(f32[1,36,128]{2,1,0:T(8,128)S(1)} %get-tuple-element.56), channel_id=1, source_target_pairs={{0,1},{1,2},{2,3},{3,0},{4,5},{5,6},{6,7},{7,4},{8,9},{9,10},{10,1... | collective-permute-start | bytes 55304 | tf_op jit(solution)/shard_map/ppermute | solution.py:22
  38.6 3.2 %collective-permute-start.8 = (f32[1,36,128]{2,1,0:T(8,128)S(1)}, f32[1,36,128]{2,1,0:T(8,128)S(1)}, u32[]{:S(2)}, u32[]{:S(2)}) collective-permute-start(f32[1,36,128]{2,1,0:T(8,128)S(1)} %get-tuple-element.55), channel_id=1, source_target_pairs={{1,0},{2,1},{3,2},{0,3},{5,4},{6,5},{7,6},{4,7},{9,8},{10,9},{11,1... | collective-permute-start | bytes 55304 | tf_op jit(solution)/shard_map/ppermute | solution.py:24
  49.5 7.0 %collective-permute-start.10 = (f32[9,36,16]{2,1,0:T(8,128)S(1)}, f32[9,36,16]{2,1,0:T(8,128)S(1)}, u32[]{:S(2)}, u32[]{:S(2)}) collective-permute-start(f32[9,36,16]{2,1,0:T(8,128)S(1)} %get-tuple-element.54), channel_id=1, source_target_pairs={{4,0},{8,4},{12,8},{0,12},{5,1},{9,5},{13,9},{1,13},{6,2},{10,6},{... | collective-permute-start | bytes 62216 | tf_op jit(solution)/shard_map/ppermute | solution.py:24
  51.7 8.4 %collective-permute-start.9 = (f32[9,36,16]{2,1,0:T(8,128)S(1)}, f32[9,36,16]{2,1,0:T(8,128)S(1)}, u32[]{:S(2)}, u32[]{:S(2)}) collective-permute-start(f32[9,36,16]{2,1,0:T(8,128)S(1)} %get-tuple-element.53), channel_id=1, source_target_pairs={{0,4},{4,8},{8,12},{12,0},{1,5},{5,9},{9,13},{13,1},{2,6},{6,10},{... | collective-permute-start | bytes 62216 | tf_op jit(solution)/shard_map/ppermute | solution.py:22
  60.6 3.3 %collective-permute-start.11 = (f32[1,36,128]{2,1,0:T(8,128)S(1)}, f32[1,36,128]{2,1,0:T(8,128)S(1)}, u32[]{:S(2)}, u32[]{:S(2)}) collective-permute-start(f32[1,36,128]{2,1,0:T(8,128)S(1)} %get-tuple-element.52), channel_id=1, source_target_pairs={{0,1},{1,2},{2,3},{3,0},{4,5},{5,6},{6,7},{7,4},{8,9},{9,10},{10,1... | collective-permute-start | bytes 55304 | tf_op jit(solution)/shard_map/ppermute | solution.py:22
  60.7 3.2 %collective-permute-start.12 = (f32[1,36,128]{2,1,0:T(8,128)S(1)}, f32[1,36,128]{2,1,0:T(8,128)S(1)}, u32[]{:S(2)}, u32[]{:S(2)}) collective-permute-start(f32[1,36,128]{2,1,0:T(8,128)S(1)} %get-tuple-element.51), channel_id=1, source_target_pairs={{1,0},{2,1},{3,2},{0,3},{5,4},{6,5},{7,6},{4,7},{9,8},{10,9},{11,1... | collective-permute-start | bytes 55304 | tf_op jit(solution)/shard_map/ppermute | solution.py:24
  71.7 9.2 %collective-permute-start.13 = (f32[9,36,16]{2,1,0:T(8,128)S(1)}, f32[9,36,16]{2,1,0:T(8,128)S(1)}, u32[]{:S(2)}, u32[]{:S(2)}) collective-permute-start(f32[9,36,16]{2,1,0:T(8,128)S(1)} %get-tuple-element.49), channel_id=1, source_target_pairs={{0,4},{4,8},{8,12},{12,0},{1,5},{5,9},{9,13},{13,1},{2,6},{6,10},{... | collective-permute-start | bytes 62216 | tf_op jit(solution)/shard_map/ppermute | solution.py:22
  72.6 9.1 %collective-permute-start.14 = (f32[9,36,16]{2,1,0:T(8,128)S(1)}, f32[9,36,16]{2,1,0:T(8,128)S(1)}, u32[]{:S(2)}, u32[]{:S(2)}) collective-permute-start(f32[9,36,16]{2,1,0:T(8,128)S(1)} %get-tuple-element.50), channel_id=1, source_target_pairs={{4,0},{8,4},{12,8},{0,12},{5,1},{9,5},{13,9},{1,13},{6,2},{10,6},{... | collective-permute-start | bytes 62216 | tf_op jit(solution)/shard_map/ppermute | solution.py:24
  82.3 3.3 %collective-permute-start.15 = (f32[1,36,128]{2,1,0:T(8,128)S(1)}, f32[1,36,128]{2,1,0:T(8,128)S(1)}, u32[]{:S(2)}, u32[]{:S(2)}) collective-permute-start(f32[1,36,128]{2,1,0:T(8,128)S(1)} %get-tuple-element.48), channel_id=1, source_target_pairs={{0,1},{1,2},{2,3},{3,0},{4,5},{5,6},{6,7},{7,4},{8,9},{9,10},{10,1... | collective-permute-start | bytes 55304 | tf_op jit(solution)/shard_map/ppermute | solution.py:22
  82.4 3.2 %collective-permute-start.16 = (f32[1,36,128]{2,1,0:T(8,128)S(1)}, f32[1,36,128]{2,1,0:T(8,128)S(1)}, u32[]{:S(2)}, u32[]{:S(2)}) collective-permute-start(f32[1,36,128]{2,1,0:T(8,128)S(1)} %get-tuple-element.47), channel_id=1, source_target_pairs={{1,0},{2,1},{3,2},{0,3},{5,4},{6,5},{7,6},{4,7},{9,8},{10,9},{11,1... | collective-permute-start | bytes 55304 | tf_op jit(solution)/shard_map/ppermute | solution.py:24
  93.3 9.2 %collective-permute-start.17 = (f32[9,36,16]{2,1,0:T(8,128)S(1)}, f32[9,36,16]{2,1,0:T(8,128)S(1)}, u32[]{:S(2)}, u32[]{:S(2)}) collective-permute-start(f32[9,36,16]{2,1,0:T(8,128)S(1)} %get-tuple-element.45), channel_id=1, source_target_pairs={{0,4},{4,8},{8,12},{12,0},{1,5},{5,9},{9,13},{13,1},{2,6},{6,10},{... | collective-permute-start | bytes 62216 | tf_op jit(solution)/shard_map/ppermute | solution.py:22
  93.8 9.2 %collective-permute-start.18 = (f32[9,36,16]{2,1,0:T(8,128)S(1)}, f32[9,36,16]{2,1,0:T(8,128)S(1)}, u32[]{:S(2)}, u32[]{:S(2)}) collective-permute-start(f32[9,36,16]{2,1,0:T(8,128)S(1)} %get-tuple-element.46), channel_id=1, source_target_pairs={{4,0},{8,4},{12,8},{0,12},{5,1},{9,5},{13,9},{1,13},{6,2},{10,6},{... | collective-permute-start | bytes 62216 | tf_op jit(solution)/shard_map/ppermute | solution.py:24
  103.6 1.8 %copy-start.6 = (s32[128]{0:T(128)S(1)}, s32[128]{0:T(128)}, u32[]{:S(2)}) copy-start(s32[128]{0:T(128)} %param.13) | copy-start | bytes 1540
  103.6 3.3 %collective-permute-start.19 = (f32[1,36,128]{2,1,0:T(8,128)S(1)}, f32[1,36,128]{2,1,0:T(8,128)S(1)}, u32[]{:S(2)}, u32[]{:S(2)}) collective-permute-start(f32[1,36,128]{2,1,0:T(8,128)S(1)} %get-tuple-element.44), channel_id=1, source_target_pairs={{0,1},{1,2},{2,3},{3,0},{4,5},{5,6},{6,7},{7,4},{8,9},{9,10},{10,1... | collective-permute-start | bytes 55304 | tf_op jit(solution)/shard_map/ppermute | solution.py:22
  103.6 3.2 %collective-permute-start.20 = (f32[1,36,128]{2,1,0:T(8,128)S(1)}, f32[1,36,128]{2,1,0:T(8,128)S(1)}, u32[]{:S(2)}, u32[]{:S(2)}) collective-permute-start(f32[1,36,128]{2,1,0:T(8,128)S(1)} %get-tuple-element.43), channel_id=1, source_target_pairs={{1,0},{2,1},{3,2},{0,3},{5,4},{6,5},{7,6},{4,7},{9,8},{10,9},{11,1... | collective-permute-start | bytes 55304 | tf_op jit(solution)/shard_map/ppermute | solution.py:24
  114.6 9.1 %collective-permute-start.21 = (f32[9,36,16]{2,1,0:T(8,128)S(1)}, f32[9,36,16]{2,1,0:T(8,128)S(1)}, u32[]{:S(2)}, u32[]{:S(2)}) collective-permute-start(f32[9,36,16]{2,1,0:T(8,128)S(1)} %get-tuple-element.41), channel_id=1, source_target_pairs={{0,4},{4,8},{8,12},{12,0},{1,5},{5,9},{9,13},{13,1},{2,6},{6,10},{... | collective-permute-start | bytes 62216 | tf_op jit(solution)/shard_map/ppermute | solution.py:22
  116.4 8.9 %collective-permute-start.22 = (f32[9,36,16]{2,1,0:T(8,128)S(1)}, f32[9,36,16]{2,1,0:T(8,128)S(1)}, u32[]{:S(2)}, u32[]{:S(2)}) collective-permute-start(f32[9,36,16]{2,1,0:T(8,128)S(1)} %get-tuple-element.42), channel_id=1, source_target_pairs={{4,0},{8,4},{12,8},{0,12},{5,1},{9,5},{13,9},{1,13},{6,2},{10,6},{... | collective-permute-start | bytes 62216 | tf_op jit(solution)/shard_map/ppermute | solution.py:24
  125.9 3.3 %collective-permute-start.23 = (f32[1,36,128]{2,1,0:T(8,128)S(1)}, f32[1,36,128]{2,1,0:T(8,128)S(1)}, u32[]{:S(2)}, u32[]{:S(2)}) collective-permute-start(f32[1,36,128]{2,1,0:T(8,128)S(1)} %get-tuple-element.40), channel_id=1, source_target_pairs={{0,1},{1,2},{2,3},{3,0},{4,5},{5,6},{6,7},{7,4},{8,9},{9,10},{10,1... | collective-permute-start | bytes 55304 | tf_op jit(solution)/shard_map/ppermute | solution.py:22
  126.0 3.2 %collective-permute-start.24 = (f32[1,36,128]{2,1,0:T(8,128)S(1)}, f32[1,36,128]{2,1,0:T(8,128)S(1)}, u32[]{:S(2)}, u32[]{:S(2)}) collective-permute-start(f32[1,36,128]{2,1,0:T(8,128)S(1)} %get-tuple-element.39), channel_id=1, source_target_pairs={{1,0},{2,1},{3,2},{0,3},{5,4},{6,5},{7,6},{4,7},{9,8},{10,9},{11,1... | collective-permute-start | bytes 55304 | tf_op jit(solution)/shard_map/ppermute | solution.py:24
where the time goes:
time: 156 us; the launch traced here: 155 us
  blocking collectives  58.7 us (38%)
  waiting for transfers between devices  50 us (32%)
  starting transfers between devices  33.6 us (22%)
  local copies, waits for them, and re-layouts  5.42 us (3%)
  matrix products  3.35 us (2%)
  other arithmetic  3.18 us (2%)
    psum x6, blocking collectives, on_device(): total = lax.psum(jnp.sum(turned, axis=(0, 1)), 'spec')  44.2 us
    ppermute x12, waiting for transfers between devices, padded_2(): lax.ppermute(tail, axis, [(i, (i + 1) % count) for i in range(count)])  35.8 us
    ppermute x12, starting transfers between devices, padded_2(): lax.ppermute(head, axis, [((i + 1) % count, i) for i in range(count)])  25.8 us
    ppermute x12, waiting for transfers between devices, padded_2(): lax.ppermute(head, axis, [((i + 1) % count, i) for i in range(count)])  11.7 us
    all_to_all x1, blocking collectives, on_device(): lax.all_to_all(arrange(stacked, send_local, tiles), 'space', split_axis=1...  8.73 us
    ppermute x12, starting transfers between devices, padded_2(): lax.ppermute(tail, axis, [(i, (i + 1) % count) for i in range(count)])  7.8 us
    psum x1, blocking collectives, on_device(): zeroth, first = lax.psum((zeroth_part, first_part), 'spec')  5.73 us
    dot_general x6, matrix products, advect(): jnp.einsum('gfw,gwp->gfp', padded, selector, precision=lax.Precision.HIGH...  3.35 us
  transfers between devices with their start and end apart: 25, of which 19 were waited for; matrix products, arithmetic and copies ran while one was open for 0% of the time, Pallas kernels for 0%

commit v1 on v0

v1 whole, which is shorter than its diff:
```python
import functools

import jax
import jax.numpy as jnp
from jax import lax
from jax.experimental import pallas as pl
from jax.experimental.pallas import tpu as pltpu
from jax.sharding import PartitionSpec as P

STEPS = 6
ROWS = 40
F32 = jnp.float32


def frequency_table(count):
    return 0.035 * jnp.float32(1.1) ** jnp.arange(count, dtype=jnp.float32)


def subtile_of(s, k, n):
    return jnp.where(s % 2 == 0, k, n - 1 - k)


def far_route(tiles, n):
    route = []
    for s in range(tiles):
        for k in range(n):
            q = k if s % 2 == 0 else n - 1 - k
            at = s * n + q
            to = (at - 1 if q % 2 == 0 else at + 1) % (tiles * n)
            ts, tq = divmod(to, n)
            route.append((s * n + k, ts * n + (tq if ts % 2 == 0 else n - 1 - tq)))
    return route


def lanes(shape):
    return lax.broadcasted_iota(jnp.int32, shape, len(shape) - 1)


class Spot:
    def __init__(self, n, npt):
        self.n, self.sub, self.npt = n, npt // n, npt
        self.s, self.k = lax.axis_index("space"), lax.axis_index("spec")
        self.q = subtile_of(self.s, self.k, n)
        self.qn = self.q ^ 1
        self.qf = n - 1 - self.q
        self.even = self.q % 2 == 0

    def shift(self, to, frm):
        return ((to - frm + self.n) % self.n) * self.sub

    def block(self, shape):
        return lanes(shape) // self.sub


def move(x, amount):
    return pltpu.roll(x, amount, 1)


def offsets(upwind, s, npt, total, reach):
    own = s * npt + lanes(upwind.shape)
    return (jnp.mod(upwind - own + reach, total) - reach).astype(F32)


def pack_kernel(n, total, reach, e_ref, c_ref, r_ref, u_ref, *rest):
    outs, v = rest[: n - 1], rest[n - 1]
    dirs, nfreq, npt = e_ref.shape
    at = Spot(n, npt)
    off = offsets(u_ref[...], at.s, npt, total, reach)
    for a, ref in enumerate((e_ref, c_ref, r_ref)):
        for j in range(dirs):
            v[a * dirs + j, :nfreq, :] = ref[j]
            v[a * dirs + j, nfreq:, :] = (
                jnp.broadcast_to(off[j : j + 1], (ROWS - nfreq, npt)) if a == 0 else jnp.zeros((ROWS - nfreq, npt), F32)
            )
    block = at.block((ROWS, npt))
    for d in range(1, n):
        to = subtile_of(at.s, at.k ^ d, n)
        for g in range(outs[0].shape[0]):
            row = None
            for i in range(n):
                if n * g + i >= 3 * dirs:
                    continue
                piece = move(v[n * g + i], at.shift(i, to))
                row = piece if row is None else jnp.where(block == i, piece, row)
            outs[d - 1][g] = row


def half_mask(at, shape, q, first):
    lane = lanes(shape)
    start = q * at.sub + jnp.where(first, 0, at.sub // 2)
    return (lane >= start) & (lane < start + at.sub // 2)


def packed(at, pieces, block):
    row = None
    for i, piece in enumerate(pieces):
        piece = move(piece, at.shift(i, at.q))
        row = piece if row is None else jnp.where(block == i, piece, row)
    return row


def spread_kernel(n, total, reach, e_ref, c_ref, r_ref, u_ref, g_ref, *rest):
    msgs = rest[: n - 1]
    eo, co, ro, near, far = rest[n - 1 :]
    dirs, nfreq, npt = e_ref.shape
    at = Spot(n, npt)
    off = offsets(u_ref[...], at.s, npt, total, reach)
    for out, ref in ((eo, e_ref), (co, c_ref), (ro, r_ref)):
        for j in range(dirs):
            out[dirs * at.k + j, :nfreq, :] = ref[j]
            out[dirs * at.k + j, nfreq:, :] = jnp.broadcast_to(off[j : j + 1], (ROWS - nfreq, npt))
    for d in range(1, n):
        b = at.k ^ d
        for a, out in enumerate((eo, co, ro)):
            for j in range(dirs):
                p = a * dirs + j
                out[dirs * b + j] = move(msgs[d - 1][p // n], at.shift(at.q, p % n))
    shape = (ROWS, npt)
    block = at.block(shape)
    half = at.sub // 2
    groups = n * dirs // n
    masks = {}
    for name, first in (("near", jnp.logical_not(at.even)), ("far", at.even)):
        masks[name] = (half_mask(at, shape, at.q, first), jnp.where(first, half, npt - half))
    for g in range(groups):
        row = packed(at, [eo[n * g + i] for i in range(n)], block)
        near[g] = row
        far[g] = row
        for name, out in (("near", near), ("far", far)):
            mask, amount = masks[name]
            out[groups + g] = packed(
                at, [jnp.where(mask, co[n * g + i], move(ro[n * g + i], amount)) for i in range(n)], block
            )
    far[2 * groups, :nfreq, :] = g_ref[...]
    far[2 * groups, nfreq:, :] = jnp.zeros((ROWS - nfreq, npt), F32)


def window(at, e, near, far, ew, ndir, block):
    def slab(g, _):
        for i in range(at.n):
            d = at.n * g + i
            x = jnp.where(block == at.qn, move(near[g], at.shift(at.qn, i)), e[d])
            ew[d] = jnp.where(block == at.qf, move(far[g], at.shift(at.qf, i)), x)
        return 0

    lax.fori_loop(0, ndir // at.n, slab, 0)


def hour(e, c, r, idx, out, m0s, grow1, dissip, freqs, bins, nfreq, factor):
    ndir, rows, npt = e.shape

    def moved(d):
        x = e[d]
        if factor is not None:
            x = x * factor
        index = jnp.broadcast_to(idx[pl.ds(d, 1), :], (rows, npt))
        up = jnp.take_along_axis(x, index, axis=1)
        return x + c[d] * (up - x)

    def flux(d, here, there):
        rate = r[d]
        return jnp.maximum(rate, 0.0) * here + jnp.minimum(rate, 0.0) * there

    first = moved(0)
    m0s[...] = first
    last = moved(ndir - 1)

    def body(d, carry):
        here, before, total = carry
        there = moved(d + 1)
        f = flux(d, here, there)
        turned = here - f + before
        out[d] = turned
        return there, f, total + turned

    here, before, total = lax.fori_loop(
        0, ndir - 1, body, (first, flux(ndir - 1, last, first), jnp.zeros((rows, npt), F32)), unroll=5
    )
    f = flux(ndir - 1, here, m0s[...])
    turned = here - f + before
    out[ndir - 1] = turned
    total = total + turned
    live = lax.broadcasted_iota(jnp.int32, (rows, npt), 0) < nfreq
    total = jnp.where(live, total, 0.0)
    mean = jnp.sum(total, axis=0, keepdims=True) / bins
    factor = grow1 / (1.0 + dissip * mean)
    part = jnp.where(live, factor * total, 0.0)
    zeroth = jnp.sum(part, axis=0, keepdims=True)
    first_moment = jnp.sum(part * freqs, axis=0, keepdims=True)
    return factor, 4.0 * jnp.sqrt(zeroth / bins), zeroth / first_moment


def phase_kernel(n, stage, bins, nfreq, fields_before, *refs):
    refs = list(refs)
    take = lambda count: [refs.pop(0) for _ in range(count)]
    e, near, far, dissip_ref, freqs_ref = take(5)
    if stage == 0:
        ci, ri, g_ref = take(3)
    else:
        cw, rw, idx, gw = take(4)
        old = take(fields_before)
    if stage == 0:
        cw, rw, idx, gw = take(4)
    fields = take(1)[0]
    if stage < 2:
        eo, msg = take(2)
    else:
        eo = take(1)[0]
        backs = take(n - 1)
    ew, et, m0s = take(3)
    ndir, rows, npt = e.shape
    at = Spot(n, npt)
    shape = (rows, npt)
    block = at.block(shape)
    groups = ndir // n
    window(at, e, near, far, ew, ndir, block)
    if stage == 0:
        half = at.sub // 2
        nfirst, ffirst = at.even, jnp.logical_not(at.even)
        nmask, fmask = half_mask(at, shape, at.qn, nfirst), half_mask(at, shape, at.qf, ffirst)
        nback, fback = jnp.where(nfirst, npt - half, half), jnp.where(ffirst, npt - half, half)

        def slab(g, _):
            for i in range(n):
                d = n * g + i
                pn = move(near[groups + g], at.shift(at.qn, i))
                pf = move(far[groups + g], at.shift(at.qf, i))
                cw[d] = jnp.where(nmask, pn, jnp.where(fmask, pf, ci[d]))
                rw[d] = jnp.where(nmask, move(pn, nback), jnp.where(fmask, move(pf, fback), ri[d]))
                idx[pl.ds(d, 1), :] = (lanes((1, npt)) + ew[d, nfreq : nfreq + 1, :].astype(jnp.int32)) & (npt - 1)
            return 0

        lax.fori_loop(0, groups, slab, 0)
        gw[:nfreq, :] = 1.0 + jnp.where(block[:nfreq] == at.qf, far[2 * groups, :nfreq, :], g_ref[...])
        gw[nfreq:, :] = jnp.ones((rows - nfreq, npt), F32)
    grow1, dissip, freqs = gw[...], dissip_ref[...], freqs_ref[...]
    fa, ha, pa = hour(ew, cw, rw, idx, et, m0s, grow1, dissip, freqs, bins, nfreq, None)
    fb, hb, pb = hour(et, cw, rw, idx, ew, m0s, grow1, dissip, freqs, bins, nfreq, fa)
    if stage < 2:
        fields[...] = jnp.concatenate([ha, hb, pa, pb], axis=0)

        def slab(g, _):
            row = None
            for i in range(n):
                x = ew[n * g + i] * fb
                eo[n * g + i] = x
                piece = move(x, at.shift(i, at.q))
                row = piece if row is None else jnp.where(block == i, piece, row)
            msg[g] = row
            return 0

        lax.fori_loop(0, groups, slab, 0)
    else:
        dirs = ndir // n
        h = [o[:2] for o in old] + [ha, hb]
        p = [o[2:] for o in old] + [pa, pb]
        every = jnp.concatenate(h + p + [jnp.zeros((16 - 2 * STEPS, npt), F32)], axis=0)
        fields[...] = every
        for j in range(dirs):
            eo[j] = ew[dirs * at.k + j] * fb
        m0s[...] = jnp.zeros(shape, F32)
        m0s[:16, :] = every
        tail = m0s[...]
        for d in range(1, n):
            b = at.k ^ d
            for g in range(backs[0].shape[0]):
                row = None
                for i in range(n):
                    j = n * g + i
                    if j > dirs:
                        continue
                    x = ew[dirs * b + j] * fb if j < dirs else tail
                    piece = move(x, at.shift(i, at.q))
                    row = piece if row is None else jnp.where(block == i, piece, row)
                backs[d - 1][g] = row


def join_kernel(n, nfreq, e_ref, f_ref, order_ref, *rest):
    msgs = rest[: n - 1]
    out, series = rest[n - 1 :]
    dirs, rows, npt = e_ref.shape
    at = Spot(n, npt)
    shape = (rows, npt)
    block = at.block(shape)
    fields = f_ref[...]
    qs = [subtile_of(at.s, at.k ^ d, n) for d in range(1, n)]
    for j in range(dirs + 1):
        x = e_ref[j] if j < dirs else None
        for d in range(1, n):
            piece = move(msgs[d - 1][j // n], at.shift(qs[d - 1], j % n))
            if j < dirs:
                x = jnp.where(block == qs[d - 1], piece, x)
            else:
                fields = jnp.where(block[:16] == qs[d - 1], piece[:16], fields)
        if j < dirs:
            out[j] = x[:nfreq]
    index = jnp.broadcast_to((order_ref[...] - at.s * npt).reshape(1, npt), (16, npt))
    series[...] = jnp.take_along_axis(fields, index, axis=1)


def hand_kernel(tiles, own_ref, *rest):
    others, out = rest[:-1], rest[-1]
    rows, npt = out.shape
    share = npt // tiles
    s = lax.axis_index("space")
    block = lanes((16, npt)) // share
    x = own_ref[...]
    for d in range(1, tiles):
        frm = (s - d + tiles) % tiles
        piece = move(others[d - 1][...], ((frm - s + tiles) % tiles) * share)
        x = jnp.where(block == frm, piece, x)
    out[...] = x[:rows]


def call(kernel, outs, scratch, *args):
    vm = pl.BlockSpec(memory_space=pltpu.VMEM)
    return pl.pallas_call(
        kernel,
        out_shape=[jax.ShapeDtypeStruct(shape, dtype) for shape, dtype in outs],
        in_specs=[vm] * len(args),
        out_specs=[vm] * len(outs),
        scratch_shapes=[pltpu.VMEM(shape, F32) for shape in scratch],
        compiler_params=pltpu.CompilerParams(vmem_limit_bytes=40 * 2**20),
    )(*args)


def on_device(spectrum, courant, refraction, growth, dissip, upwind, send_order):
    dirs, nfreq, npt = spectrum.shape
    tiles, n = lax.axis_size("space"), lax.axis_size("spec")
    total, reach = npt * tiles, npt // 8
    ndir = dirs * n
    bins = ndir * nfreq
    groups = ndir // n
    peers = range(1, n)
    swap = lambda x, d: lax.ppermute(x, "spec", [(k, k ^ d) for k in range(n)])
    near_to = lambda x: swap(x, 1)
    route = far_route(tiles, n)
    far_to = lambda x: lax.ppermute(x, ("space", "spec"), route)
    wide = lambda v: jnp.pad(jnp.broadcast_to(v[:, None], (nfreq, npt)), ((0, ROWS - nfreq), (0, 0)))
    freqs, dissip = wide(frequency_table(nfreq)), wide(dissip)
    field = (ROWS, npt)
    state = ((ndir, *field), F32)

    slabs = -(-3 * dirs // n)
    sent = call(
        functools.partial(pack_kernel, n, total, reach),
        [((slabs, *field), F32)] * (n - 1),
        [(3 * dirs, *field)],
        spectrum, courant, refraction, upwind,
    )
    got = [swap(x, d) for d, x in zip(peers, sent)]
    e, c, r, near, far = call(
        functools.partial(spread_kernel, n, total, reach),
        [state] * 3 + [((2 * groups, *field), F32), ((2 * groups + 1, *field), F32)],
        [],
        spectrum, courant, refraction, upwind, growth, *got,
    )
    scratch = [(ndir, *field), (ndir, *field), field]
    phase = lambda stage, before, outs, *args: call(
        functools.partial(phase_kernel, n, stage, bins, nfreq, before), outs, scratch, *args
    )
    c, r, idx, gw, f0, e, msg = phase(
        0, 0,
        [state, state, ((ndir + (-ndir) % 8, npt), jnp.int32), (field, F32), ((4, npt), F32), state, ((groups, *field), F32)],
        e, near_to(near), far_to(far), dissip, freqs, c, r, growth,
    )
    f1, e, msg = phase(
        1, 1, [((4, npt), F32), state, ((groups, *field), F32)],
        e, near_to(msg), far_to(msg), dissip, freqs, c, r, idx, gw, f0,
    )
    back = (-(-(dirs + 1) // n), *field)
    fields, own, *backs = phase(
        2, 2, [((16, npt), F32), ((dirs, *field), F32)] + [(back, F32)] * (n - 1),
        e, near_to(msg), far_to(msg), dissip, freqs, c, r, idx, gw, f0, f1,
    )
    energy, ordered = call(
        functools.partial(join_kernel, n, nfreq),
        [((dirs, nfreq, npt), F32), ((16, npt), F32)],
        [],
        own, fields, send_order, *[swap(x, d) for d, x in zip(peers, backs)],
    )
    if tiles <= 4:
        others = [lax.ppermute(ordered, "space", [(t, (t + d) % tiles) for t in range(tiles)]) for d in range(1, tiles)]
        (series,) = call(functools.partial(hand_kernel, tiles), [((2 * STEPS, npt), F32)], [], ordered, *others)
    else:
        parts = ordered[: 2 * STEPS].reshape(2 * STEPS, tiles, npt // tiles)
        series = lax.all_to_all(parts, "space", split_axis=1, concat_axis=1, tiled=True).reshape(2 * STEPS, npt)
    return (energy, series)


def solution(mesh):
    placed = (
        P("spec", None, ("runs", "space")),
        P("spec", None, "space"),
        P("spec", None, "space"),
        P(None, ("runs", "space")),
        P(),
        P("spec", "space"),
        P("space"),
    )
    return jax.shard_map(
        on_device,
        mesh=mesh,
        in_specs=placed,
        out_specs=(P("spec", None, ("runs", "space")), P(None, ("runs", "space"))),
        check_vma=False,
    )
```

time: 156 us -> 72.3 us (0.46)
  blocking collectives: 58.7 us -> 0 us
  waiting for transfers between devices: 50 us -> 27.3 us
  Pallas kernels: 0 us -> 16.7 us
  starting transfers between devices: 33.6 us -> 23.1 us
  matrix products: 3.35 us -> 0 us
  other arithmetic: 3.18 us -> 0.01 us
    psum x7 -> x0, blocking collectives: 50 us -> none  [the longest x6 44.2 us: on_device(): total = lax.psum(jnp.sum(turned, axis=(0, 1)), 'spec')]
    ppermute x25 -> x15, waiting for transfers between devices: 50 us -> 27.3 us  [the longest x9 12.2 us: on_device(): swap = lambda x, d: lax.ppermute(x, 'spec', [(k, k ^ d) for k in range(n)])]
    pallas_call x0 -> x7, Pallas kernels: none -> 16.7 us  [call(): pl.pallas_call(kernel, out_shape=[jax.ShapeDtypeStruct(shape, dtype) for...]
    ppermute x25 -> x15, starting transfers between devices: 33.6 us -> 23.1 us  [the longest x3 11.3 us: on_device(): far_to = lambda x: lax.ppermute(x, ('space', 'spec'), route)]
    all_to_all x1 -> x0, blocking collectives: 8.73 us -> none  [on_device(): lax.all_to_all(arrange(stacked, send_local, tiles), 'space', split_axis=1...]
    dot_general x6 -> x0, matrix products: 3.35 us -> none  [advect(): jnp.einsum('gfw,gwp->gfp', padded, selector, precision=lax.Precision.HIGH...]
    unnamed x17 -> x14, local copies, waits for them, and re-layouts: 1.52 us -> 4.12 us
    slice x13 -> x0, local copies, waits for them, and re-layouts: 1.74 us -> none  [the longest x6 1.7 us: padded_2(): lax.slice_in_dim(cells, cells.shape[dim] - width, cells.shape[dim], axis=...]
  transfers between devices with their start and end apart: 25 -> 15, of which waited for: 19 -> 10; matrix products, arithmetic and copies ran while one was open for 0% -> 0% of each run, Pallas kernels for 0% -> 0%
where the time goes in v1:
time: 72.3 us; the launch traced here: 72 us
  waiting for transfers between devices  27.3 us (38%)
  starting transfers between devices  23.1 us (32%)
  Pallas kernels  16.7 us (23%)
  local copies, waits for them, and re-layouts  4.27 us (6%)
  between operations  0.74 us (1%)
    pallas_call x7, Pallas kernels, call(): pl.pallas_call(kernel, out_shape=[jax.ShapeDtypeStruct(shape, dtype) for...  16.7 us
    ppermute x9, waiting for transfers between devices, on_device(): swap = lambda x, d: lax.ppermute(x, 'spec', [(k, k ^ d) for k in range(n)])  12.2 us
    ppermute x3, waiting for transfers between devices, on_device(): far_to = lambda x: lax.ppermute(x, ('space', 'spec'), route)  11.7 us
    ppermute x3, starting transfers between devices, on_device(): far_to = lambda x: lax.ppermute(x, ('space', 'spec'), route)  11.3 us
    ppermute x3, starting transfers between devices, on_device(): lax.ppermute(ordered, 'space', [(t, (t + d) % tiles) for t in range(tiles)])  6.73 us
    ppermute x9, starting transfers between devices, on_device(): swap = lambda x, d: lax.ppermute(x, 'spec', [(k, k ^ d) for k in range(n)])  5.08 us
    unnamed x14, local copies, waits for them, and re-layouts  4.12 us
    ppermute x3, waiting for transfers between devices, on_device(): lax.ppermute(ordered, 'space', [(t, (t + d) % tiles) for t in range(tiles)])  3.42 us
  transfers between devices with their start and end apart: 15, of which 10 were waited for; matrix products, arithmetic and copies ran while one was open for 0% of the time, Pallas kernels for 0%

profile of v1, /device:TPU:0, one launch (start us, length us, event | category | flops | bytes accessed | tf_op | source)
XLA Modules:
  0.0 72.0 jit_solution(12112879334886182340)
XLA Ops:
  0.6 0.9 %copy-done = f32[9,36,128]{2,1,0:T(8,128)S(1)} copy-done((f32[9,36,128]{2,1,0:T(8,128)S(1)}, f32[9,36,128]{2,1,0:T(8,128)}, u32[]{:S(2)}) %copy-start) | copy-done | bytes 165912
  1.6 0.9 %copy-done.1 = f32[9,36,128]{2,1,0:T(8,128)S(1)} copy-done((f32[9,36,128]{2,1,0:T(8,128)S(1)}, f32[9,36,128]{2,1,0:T(8,128)}, u32[]{:S(2)}) %copy-start.1) | copy-done | bytes 165912
  2.5 0.9 %copy-done.2 = f32[9,36,128]{2,1,0:T(8,128)S(1)} copy-done((f32[9,36,128]{2,1,0:T(8,128)S(1)}, f32[9,36,128]{2,1,0:T(8,128)}, u32[]{:S(2)}) %copy-start.2) | copy-done | bytes 165912
  3.4 0.7 copy-done.4
  4.1 0.5 shard_map.86
  4.6 0.5 collective-permute-start
  5.1 2.6 %collective-permute-start.1 = (f32[7,40,128]{2,1,0:T(8,128)S(1)}, f32[7,40,128]{2,1,0:T(8,128)S(1)}, u32[]{:S(2)}, u32[]{:S(2)}) collective-permute-start(f32[7,40,128]{2,1,0:T(8,128)S(1)} %get-tuple-element.28), channel_id=1, source_target_pairs={{0,2},{1,3},{2,0},{3,1},{4,6},{5,7},{6,4},{7,5},{8,10},{9,11},{10,... | collective-permute-start | bytes 430088 | tf_op jit(solution)/shard_map/ppermute | solution.py:335
  7.8 4.5 %collective-permute-done.1.rest_1_ = f32[7,40,128]{2,1,0:T(8,128)S(1)} collective-permute-done((f32[7,40,128]{2,1,0:T(8,128)S(1)}, f32[7,40,128]{2,1,0:T(8,128)S(1)}, u32[]{:S(2)}, u32[]{:S(2)}) %collective-permute-start.1) | collective-permute-done | bytes 143392 | tf_op jit(solution)/shard_map/ppermute | solution.py:335
  12.3 2.5 %collective-permute-done.2.rest_2_ = f32[7,40,128]{2,1,0:T(8,128)S(1)} collective-permute-done((f32[7,40,128]{2,1,0:T(8,128)S(1)}, f32[7,40,128]{2,1,0:T(8,128)S(1)}, u32[]{:S(2)}, u32[]{:S(2)}) %collective-permute-start.2) | collective-permute-done | bytes 143392 | tf_op jit(solution)/shard_map/ppermute | solution.py:335
  14.9 2.3 %shard_map.87 = (f32[36,40,128]{2,1,0:T(8,128)S(1)}, f32[36,40,128]{2,1,0:T(8,128)S(1)}, f32[36,40,128]{2,1,0:T(8,128)S(1)}, f32[18,40,128]{2,1,0:T(8,128)S(1)}, f32[19,40,128]{2,1,0:T(8,128)S(1)}) custom-call(f32[9,36,128]{2,1,0:T(8,128)S(1)} %copy-done, f32[9,36,128]{2,1,0:T(8,128)S(1)} %copy-done.1, f32[9,36,128]{2,1,0:T(8,128)S(1)} %copy-done.2, ...), custom_call_target="tpu_custom_call" | custom-call | tf_op jit(solution)/shard_map/pallas_call | solution.py:317
  17.2 3.7 %collective-permute-start.4 = (f32[19,40,128]{2,1,0:T(8,128)S(1)}, f32[19,40,128]{2,1,0:T(8,128)S(1)}, u32[]{:S(2)}, u32[]{:S(2)}) collective-permute-start(f32[19,40,128]{2,1,0:T(8,128)S(1)} %get-tuple-element.32), channel_id=1, source_target_pairs={{0,12},{1,2},{2,1},{3,7},{4,8},{5,6},{6,5},{7,3},{8,4},{9,10},{10,... | collective-permute-start | bytes 1167368 | tf_op jit(solution)/shard_map/ppermute | solution.py:338
  21.0 1.6 %collective-permute-done.3.refs_1_ = f32[18,40,128]{2,1,0:T(8,128)S(1)} collective-permute-done((f32[18,40,128]{2,1,0:T(8,128)S(1)}, f32[18,40,128]{2,1,0:T(8,128)S(1)}, u32[]{:S(2)}, u32[]{:S(2)}) %collective-permute-start.3) | collective-permute-done | bytes 368672 | tf_op jit(solution)/shard_map/ppermute | solution.py:335
  22.6 4.3 %collective-permute-done.4.refs_2_ = f32[19,40,128]{2,1,0:T(8,128)S(1)} collective-permute-done((f32[19,40,128]{2,1,0:T(8,128)S(1)}, f32[19,40,128]{2,1,0:T(8,128)S(1)}, u32[]{:S(2)}, u32[]{:S(2)}) %collective-permute-start.4) | collective-permute-done | bytes 389152 | tf_op jit(solution)/shard_map/ppermute | solution.py:338
  27.0 5.4 %shard_map.88 = (f32[36,40,128]{2,1,0:T(8,128)S(1)}, f32[36,40,128]{2,1,0:T(8,128)S(1)}, s32[40,128]{1,0:T(8,128)S(1)}, f32[40,128]{1,0:T(8,128)S(1)}, f32[4,128...) custom-call(f32[36,40,128]{2,1,0:T(8,128)S(1)} %get-tuple-element.30.refs_0_, ...), custom_call_target="tpu_custom_call" | custom-call | tf_op jit(solution)/shard_map/pallas_call | solution.py:317
  32.4 3.7 %collective-permute-start.6 = (f32[9,40,128]{2,1,0:T(8,128)S(1)}, f32[9,40,128]{2,1,0:T(8,128)S(1)}, u32[]{:S(2)}, u32[]{:S(2)}) collective-permute-start(f32[9,40,128]{2,1,0:T(8,128)S(1)} %get-tuple-element.36), channel_id=1, source_target_pairs={{0,12},{1,2},{2,1},{3,7},{4,8},{5,6},{6,5},{7,3},{8,4},{9,10},{10,... | collective-permute-start | bytes 552968 | tf_op jit(solution)/shard_map/ppermute | solution.py:338
  36.1 3.7 %collective-permute-done.6.refs_2_ = f32[9,40,128]{2,1,0:T(8,128)S(1)} collective-permute-done((f32[9,40,128]{2,1,0:T(8,128)S(1)}, f32[9,40,128]{2,1,0:T(8,128)S(1)}, u32[]{:S(2)}, u32[]{:S(2)}) %collective-permute-start.6) | collective-permute-done | bytes 184352 | tf_op jit(solution)/shard_map/ppermute | solution.py:338
  39.8 3.8 %shard_map.89 = (f32[4,128]{1,0:T(4,128)S(1)}, f32[36,40,128]{2,1,0:T(8,128)S(1)}, f32[9,40,128]{2,1,0:T(8,128)S(1)}) custom-call(f32[36,40,128]{2,1,0:T(8,128)S(1)} %get-tuple-element.35.refs_0_, f32[9,40,128]{2,1,0:T(8,128)S(1)} %collective-permute-done.5.refs_1_, f32[9,40,128]{2,1,0:T(8,128)S(1)} %collective-permute-done.6.refs_2_, ...), custom_call_target="tpu_custom_call" | custom-call | tf_op jit(solution)/shard_map/pallas_call | solution.py:317
  43.6 3.8 %collective-permute-start.8 = (f32[9,40,128]{2,1,0:T(8,128)S(1)}, f32[9,40,128]{2,1,0:T(8,128)S(1)}, u32[]{:S(2)}, u32[]{:S(2)}) collective-permute-start(f32[9,40,128]{2,1,0:T(8,128)S(1)} %get-tuple-element.43), channel_id=1, source_target_pairs={{0,12},{1,2},{2,1},{3,7},{4,8},{5,6},{6,5},{7,3},{8,4},{9,10},{10,... | collective-permute-start | bytes 552968 | tf_op jit(solution)/shard_map/ppermute | solution.py:338
  47.4 3.7 %collective-permute-done.8.refs_2_ = f32[9,40,128]{2,1,0:T(8,128)S(1)} collective-permute-done((f32[9,40,128]{2,1,0:T(8,128)S(1)}, f32[9,40,128]{2,1,0:T(8,128)S(1)}, u32[]{:S(2)}, u32[]{:S(2)}) %collective-permute-start.8) | collective-permute-done | bytes 184352 | tf_op jit(solution)/shard_map/ppermute | solution.py:338
  51.1 3.1 %shard_map.90 = (f32[16,128]{1,0:T(8,128)S(1)}, f32[9,40,128]{2,1,0:T(8,128)S(1)}, f32[3,40,128]{2,1,0:T(8,128)S(1)}, f32[3,40,128]{2,1,0:T(8,128)S(1)}, f32[3,40,128]{2,1,0:T(8,128)S(1)}) custom-call(f32[36,40,128]{2,1,0:T(8,128)S(1)} %get-tuple-element.42.refs_0_, f32[9,40,128]{2,1,0:T(8,128)S(1)} %collective-permute-done.7.refs_1_, ...), custom_call_target="tpu_custom_call" | custom-call | tf_op jit(solution)/shard_map/pallas_call | solution.py:317
  54.3 0.1 collective-permute-start.9
  54.4 1.8 %collective-permute-start.11 = (f32[3,40,128]{2,1,0:T(8,128)S(1)}, f32[3,40,128]{2,1,0:T(8,128)S(1)}, u32[]{:S(2)}, u32[]{:S(2)}) collective-permute-start(f32[3,40,128]{2,1,0:T(8,128)S(1)} %get-tuple-element.49), channel_id=1, source_target_pairs={{0,3},{1,2},{2,1},{3,0},{4,7},{5,6},{6,5},{7,4},{8,11},{9,10},{10,... | collective-permute-start | bytes 184328 | tf_op jit(solution)/shard_map/ppermute | solution.py:335
  56.2 3.0 %collective-permute-done.10.rest_1_ = f32[3,40,128]{2,1,0:T(8,128)S(1)} collective-permute-done((f32[3,40,128]{2,1,0:T(8,128)S(1)}, f32[3,40,128]{2,1,0:T(8,128)S(1)}, u32[]{:S(2)}, u32[]{:S(2)}) %collective-permute-start.10) | collective-permute-done | bytes 61472 | tf_op jit(solution)/shard_map/ppermute | solution.py:335
  59.2 0.4 collective-permute-done.11.rest_2_
  59.6 0.7 copy-done.5
  60.3 0.9 %shard_map.91 = (f32[9,36,128]{2,1,0:T(8,128)}, f32[16,128]{1,0:T(8,128)S(1)}) custom-call(f32[9,40,128]{2,1,0:T(8,128)S(1)} %get-tuple-element.45.e_ref, f32[16,128]{1,0:T(8,128)S(1)} %get-tuple-element.46.f_ref, s32[128]{0:T(128)S(1)} %copy-done.5, f32[3,40,128]{2,1,0:T(8,128)S(1)} %collective-permute-done.9.rest_0_, ...), custom_call_target="tpu_custom_call" | custom-call | tf_op jit(solution)/shard_map/pallas_call | solution.py:317
  61.2 3.7 %collective-permute-start.14 = (f32[16,128]{1,0:T(8,128)S(1)}, f32[16,128]{1,0:T(8,128)S(1)}, u32[]{:S(2)}, u32[]{:S(2)}) collective-permute-start(f32[16,128]{1,0:T(8,128)S(1)} %get-tuple-element.51.own_ref), channel_id=1, source_target_pairs={{0,12},{4,0},{8,4},{12,8},{1,13},{5,1},{9,5},{13,9},{2,14},{6,2},{... | collective-permute-start | bytes 24584 | tf_op jit(solution)/shard_map/ppermute | solution.py:383
  64.9 1.0 %collective-permute-start.13 = (f32[16,128]{1,0:T(8,128)S(1)}, f32[16,128]{1,0:T(8,128)S(1)}, u32[]{:S(2)}, u32[]{:S(2)}) collective-permute-start(f32[16,128]{1,0:T(8,128)S(1)} %get-tuple-element.51.own_ref), channel_id=1, source_target_pairs={{0,8},{4,12},{8,0},{12,4},{1,9},{5,13},{9,1},{13,5},{2,10},{6,14},... | collective-permute-start | bytes 24584 | tf_op jit(solution)/shard_map/ppermute | solution.py:383
  65.9 2.0 %collective-permute-start.12 = (f32[16,128]{1,0:T(8,128)S(1)}, f32[16,128]{1,0:T(8,128)S(1)}, u32[]{:S(2)}, u32[]{:S(2)}) collective-permute-start(f32[16,128]{1,0:T(8,128)S(1)} %get-tuple-element.51.own_ref), channel_id=1, source_target_pairs={{0,4},{4,8},{8,12},{12,0},{1,5},{5,9},{9,13},{13,1},{2,6},{6,10},{... | collective-permute-start | bytes 24584 | tf_op jit(solution)/shard_map/ppermute | solution.py:383
  67.9 1.5 %collective-permute-done.13.rest_1_ = f32[16,128]{1,0:T(8,128)S(1)} collective-permute-done((f32[16,128]{1,0:T(8,128)S(1)}, f32[16,128]{1,0:T(8,128)S(1)}, u32[]{:S(2)}, u32[]{:S(2)}) %collective-permute-start.13) | collective-permute-done | bytes 8224 | tf_op jit(solution)/shard_map/ppermute | solution.py:383
  69.5 1.9 %collective-permute-done.12.rest_0_ = f32[16,128]{1,0:T(8,128)S(1)} collective-permute-done((f32[16,128]{1,0:T(8,128)S(1)}, f32[16,128]{1,0:T(8,128)S(1)}, u32[]{:S(2)}, u32[]{:S(2)}) %collective-permute-start.12) | collective-permute-done | bytes 8224 | tf_op jit(solution)/shard_map/ppermute | solution.py:383
  71.4 0.7 shard_map.92
  (24 shorter events, 0.3 us)
Async XLA Ops:
  0.6 0.9 %copy-start = (f32[9,36,128]{2,1,0:T(8,128)S(1)}, f32[9,36,128]{2,1,0:T(8,128)}, u32[]{:S(2)}) copy-start(f32[9,36,128]{2,1,0:T(8,128)} %e_ref.3) | copy-start | bytes 497668
  1.6 0.9 %copy-start.1 = (f32[9,36,128]{2,1,0:T(8,128)S(1)}, f32[9,36,128]{2,1,0:T(8,128)}, u32[]{:S(2)}) copy-start(f32[9,36,128]{2,1,0:T(8,128)} %c_ref.3) | copy-start | bytes 497668
  2.5 0.9 %copy-start.2 = (f32[9,36,128]{2,1,0:T(8,128)S(1)}, f32[9,36,128]{2,1,0:T(8,128)}, u32[]{:S(2)}) copy-start(f32[9,36,128]{2,1,0:T(8,128)} %r_ref.3) | copy-start | bytes 497668
  3.4 0.7 copy-start.4
  4.1 10.8 %copy-start.3 = (f32[36,128]{1,0:T(8,128)S(1)}, f32[36,128]{1,0:T(8,128)}, u32[]{:S(2)}) copy-start(f32[36,128]{1,0:T(8,128)} %refs_7_.1) | copy-start | bytes 55300
  4.6 3.2 %collective-permute-start = (f32[7,40,128]{2,1,0:T(8,128)S(1)}, f32[7,40,128]{2,1,0:T(8,128)S(1)}, u32[]{:S(2)}, u32[]{:S(2)}) collective-permute-start(f32[7,40,128]{2,1,0:T(8,128)S(1)} %get-tuple-element.27), channel_id=1, source_target_pairs={{0,1},{1,0},{2,3},{3,2},{4,5},{5,4},{6,7},{7,6},{8,9},{9,8},{10,11... | collective-permute-start | bytes 430088 | tf_op jit(solution)/shard_map/ppermute | solution.py:335
  5.1 7.2 %collective-permute-start.1 = (f32[7,40,128]{2,1,0:T(8,128)S(1)}, f32[7,40,128]{2,1,0:T(8,128)S(1)}, u32[]{:S(2)}, u32[]{:S(2)}) collective-permute-start(f32[7,40,128]{2,1,0:T(8,128)S(1)} %get-tuple-element.28), channel_id=1, source_target_pairs={{0,2},{1,3},{2,0},{3,1},{4,6},{5,7},{6,4},{7,5},{8,10},{9,11},{10,... | collective-permute-start | bytes 430088 | tf_op jit(solution)/shard_map/ppermute | solution.py:335
  7.7 7.2 %collective-permute-start.2 = (f32[7,40,128]{2,1,0:T(8,128)S(1)}, f32[7,40,128]{2,1,0:T(8,128)S(1)}, u32[]{:S(2)}, u32[]{:S(2)}) collective-permute-start(f32[7,40,128]{2,1,0:T(8,128)S(1)} %get-tuple-element.29), channel_id=1, source_target_pairs={{0,3},{1,2},{2,1},{3,0},{4,7},{5,6},{6,5},{7,4},{8,11},{9,10},{10,... | collective-permute-start | bytes 430088 | tf_op jit(solution)/shard_map/ppermute | solution.py:335
  17.2 3.8 %copy-start.6 = (f32[36]{0:T(128)S(1)}, f32[36]{0:T(128)}, u32[]{:S(2)}) copy-start(f32[36]{0:T(128)} %param.11) | copy-start | bytes 436
  17.2 9.7 %collective-permute-start.4 = (f32[19,40,128]{2,1,0:T(8,128)S(1)}, f32[19,40,128]{2,1,0:T(8,128)S(1)}, u32[]{:S(2)}, u32[]{:S(2)}) collective-permute-start(f32[19,40,128]{2,1,0:T(8,128)S(1)} %get-tuple-element.32), channel_id=1, source_target_pairs={{0,12},{1,2},{2,1},{3,7},{4,8},{5,6},{6,5},{7,3},{8,4},{9,10},{10,... | collective-permute-start | bytes 1167368 | tf_op jit(solution)/shard_map/ppermute | solution.py:338
  20.9 1.7 %collective-permute-start.3 = (f32[18,40,128]{2,1,0:T(8,128)S(1)}, f32[18,40,128]{2,1,0:T(8,128)S(1)}, u32[]{:S(2)}, u32[]{:S(2)}) collective-permute-start(f32[18,40,128]{2,1,0:T(8,128)S(1)} %get-tuple-element.31), channel_id=1, source_target_pairs={{0,1},{1,0},{2,3},{3,2},{4,5},{5,4},{6,7},{7,6},{8,9},{9,8},{10,11... | collective-permute-start | bytes 1105928 | tf_op jit(solution)/shard_map/ppermute | solution.py:335
  32.4 7.4 %collective-permute-start.6 = (f32[9,40,128]{2,1,0:T(8,128)S(1)}, f32[9,40,128]{2,1,0:T(8,128)S(1)}, u32[]{:S(2)}, u32[]{:S(2)}) collective-permute-start(f32[9,40,128]{2,1,0:T(8,128)S(1)} %get-tuple-element.36), channel_id=1, source_target_pairs={{0,12},{1,2},{2,1},{3,7},{4,8},{5,6},{6,5},{7,3},{8,4},{9,10},{10,... | collective-permute-start | bytes 552968 | tf_op jit(solution)/shard_map/ppermute | solution.py:338
  36.1 3.7 %collective-permute-start.5 = (f32[9,40,128]{2,1,0:T(8,128)S(1)}, f32[9,40,128]{2,1,0:T(8,128)S(1)}, u32[]{:S(2)}, u32[]{:S(2)}) collective-permute-start(f32[9,40,128]{2,1,0:T(8,128)S(1)} %get-tuple-element.36), channel_id=1, source_target_pairs={{0,1},{1,0},{2,3},{3,2},{4,5},{5,4},{6,7},{7,6},{8,9},{9,8},{10,11... | collective-permute-start | bytes 552968 | tf_op jit(solution)/shard_map/ppermute | solution.py:335
  43.6 7.5 %collective-permute-start.8 = (f32[9,40,128]{2,1,0:T(8,128)S(1)}, f32[9,40,128]{2,1,0:T(8,128)S(1)}, u32[]{:S(2)}, u32[]{:S(2)}) collective-permute-start(f32[9,40,128]{2,1,0:T(8,128)S(1)} %get-tuple-element.43), channel_id=1, source_target_pairs={{0,12},{1,2},{2,1},{3,7},{4,8},{5,6},{6,5},{7,3},{8,4},{9,10},{10,... | collective-permute-start | bytes 552968 | tf_op jit(solution)/shard_map/ppermute | solution.py:338
  47.4 3.7 %collective-permute-start.7 = (f32[9,40,128]{2,1,0:T(8,128)S(1)}, f32[9,40,128]{2,1,0:T(8,128)S(1)}, u32[]{:S(2)}, u32[]{:S(2)}) collective-permute-start(f32[9,40,128]{2,1,0:T(8,128)S(1)} %get-tuple-element.43), channel_id=1, source_target_pairs={{0,1},{1,0},{2,3},{3,2},{4,5},{5,4},{6,7},{7,6},{8,9},{9,8},{10,11... | collective-permute-start | bytes 552968 | tf_op jit(solution)/shard_map/ppermute | solution.py:335
  54.3 1.9 %collective-permute-start.9 = (f32[3,40,128]{2,1,0:T(8,128)S(1)}, f32[3,40,128]{2,1,0:T(8,128)S(1)}, u32[]{:S(2)}, u32[]{:S(2)}) collective-permute-start(f32[3,40,128]{2,1,0:T(8,128)S(1)} %get-tuple-element.47), channel_id=1, source_target_pairs={{0,1},{1,0},{2,3},{3,2},{4,5},{5,4},{6,7},{7,6},{8,9},{9,8},{10,11... | collective-permute-start | bytes 184328 | tf_op jit(solution)/shard_map/ppermute | solution.py:335
  54.4 4.9 %collective-permute-start.10 = (f32[3,40,128]{2,1,0:T(8,128)S(1)}, f32[3,40,128]{2,1,0:T(8,128)S(1)}, u32[]{:S(2)}, u32[]{:S(2)}) collective-permute-start(f32[3,40,128]{2,1,0:T(8,128)S(1)} %get-tuple-element.48), channel_id=1, source_target_pairs={{0,2},{1,3},{2,0},{3,1},{4,6},{5,7},{6,4},{7,5},{8,10},{9,11},{10,... | collective-permute-start | bytes 184328 | tf_op jit(solution)/shard_map/ppermute | solution.py:335
  54.4 5.2 %collective-permute-start.11 = (f32[3,40,128]{2,1,0:T(8,128)S(1)}, f32[3,40,128]{2,1,0:T(8,128)S(1)}, u32[]{:S(2)}, u32[]{:S(2)}) collective-permute-start(f32[3,40,128]{2,1,0:T(8,128)S(1)} %get-tuple-element.49), channel_id=1, source_target_pairs={{0,3},{1,2},{2,1},{3,0},{4,7},{5,6},{6,5},{7,4},{8,11},{9,10},{10,... | collective-permute-start | bytes 184328 | tf_op jit(solution)/shard_map/ppermute | solution.py:335
  59.6 0.7 copy-start.5
  61.2 6.7 %collective-permute-start.14 = (f32[16,128]{1,0:T(8,128)S(1)}, f32[16,128]{1,0:T(8,128)S(1)}, u32[]{:S(2)}, u32[]{:S(2)}) collective-permute-start(f32[16,128]{1,0:T(8,128)S(1)} %get-tuple-element.51.own_ref), channel_id=1, source_target_pairs={{0,12},{4,0},{8,4},{12,8},{1,13},{5,1},{9,5},{13,9},{2,14},{6,2},{... | collective-permute-start | bytes 24584 | tf_op jit(solution)/shard_map/ppermute | solution.py:383
  64.9 4.5 %collective-permute-start.13 = (f32[16,128]{1,0:T(8,128)S(1)}, f32[16,128]{1,0:T(8,128)S(1)}, u32[]{:S(2)}, u32[]{:S(2)}) collective-permute-start(f32[16,128]{1,0:T(8,128)S(1)} %get-tuple-element.51.own_ref), channel_id=1, source_target_pairs={{0,8},{4,12},{8,0},{12,4},{1,9},{5,13},{9,1},{13,5},{2,10},{6,14},... | collective-permute-start | bytes 24584 | tf_op jit(solution)/shard_map/ppermute | solution.py:383
  65.9 5.4 %collective-permute-start.12 = (f32[16,128]{1,0:T(8,128)S(1)}, f32[16,128]{1,0:T(8,128)S(1)}, u32[]{:S(2)}, u32[]{:S(2)}) collective-permute-start(f32[16,128]{1,0:T(8,128)S(1)} %get-tuple-element.51.own_ref), channel_id=1, source_target_pairs={{0,4},{4,8},{8,12},{12,0},{1,5},{5,9},{9,13},{13,1},{2,6},{6,10},{... | collective-permute-start | bytes 24584 | tf_op jit(solution)/shard_map/ppermute | solution.py:383

commit v2 on v1

v2 whole, which is shorter than its diff:
```python
import functools

import jax
import jax.numpy as jnp
from jax import lax
from jax.experimental import pallas as pl
from jax.experimental.pallas import tpu as pltpu
from jax.sharding import PartitionSpec as P

STEPS = 6
ROWS = 40
F32 = jnp.float32


def frequency_table(count):
    return 0.035 * jnp.float32(1.1) ** jnp.arange(count, dtype=jnp.float32)


def subtile_of(s, k, n):
    return jnp.where(s % 2 == 0, k, n - 1 - k)


def far_route(tiles, n):
    route = []
    for s in range(tiles):
        for k in range(n):
            q = k if s % 2 == 0 else n - 1 - k
            at = s * n + q
            to = (at - 1 if q % 2 == 0 else at + 1) % (tiles * n)
            ts, tq = divmod(to, n)
            route.append((s * n + k, ts * n + (tq if ts % 2 == 0 else n - 1 - tq)))
    return route


def lanes(shape):
    return lax.broadcasted_iota(jnp.int32, shape, len(shape) - 1)


class Spot:
    def __init__(self, n, npt):
        self.n, self.sub, self.npt = n, npt // n, npt
        self.s, self.k = lax.axis_index("space"), lax.axis_index("spec")
        self.q = subtile_of(self.s, self.k, n)
        self.qn = self.q ^ 1
        self.qf = n - 1 - self.q
        self.even = self.q % 2 == 0

    def shift(self, to, frm):
        return ((to - frm + self.n) % self.n) * self.sub

    def block(self, shape):
        return lanes(shape) // self.sub


def move(x, amount):
    return pltpu.roll(x, amount, 1)


def offsets(upwind, s, npt, total, reach):
    own = s * npt + lanes(upwind.shape)
    return (jnp.mod(upwind - own + reach, total) - reach).astype(F32)


def pieces(dirs, n):
    full = (dirs - 1) // n
    where = []
    for b in range(n):
        where += [(full * b + j // n, j % n) for j in range(dirs - 1)] + [(full * n, b)]
    return where


def pack_kernel(n, total, reach, e_hbm, c_hbm, r_hbm, u_hbm, *rest):
    outs, (e_ref, c_ref, r_ref, u_ref, v, sem) = rest[:n], rest[n:]
    dirs, nfreq, npt = e_ref.shape
    copies = [
        pltpu.make_async_copy(x, y, sem.at[i])
        for i, (x, y) in enumerate(((e_hbm, e_ref), (c_hbm, c_ref), (r_hbm, r_ref), (u_hbm, u_ref)))
    ]
    for copy in copies:
        copy.start()
    for copy in copies:
        copy.wait()
    at = Spot(n, npt)
    off = offsets(u_ref[...], at.s, npt, total, reach)
    for a, ref in enumerate((e_ref, c_ref, r_ref)):
        for j in range(dirs):
            v[a * dirs + j, :nfreq, :] = ref[j]
            v[a * dirs + j, nfreq:, :] = jnp.broadcast_to(off[j : j + 1], (ROWS - nfreq, npt))
    block = at.block((ROWS, npt))
    full = (dirs - 1) // n
    last = [(at.k + a) % n for a in range(3)]
    for d in range(n):
        to = subtile_of(at.s, at.k ^ d, n)
        for a in range(3):
            for h in range(full):
                row = None
                for i in range(n):
                    piece = move(v[a * dirs + n * h + i], at.shift(i, to))
                    row = piece if row is None else jnp.where(block == i, piece, row)
                outs[d][full * a + h] = row
        row = None
        for a in range(3):
            piece = move(v[(a + 1) * dirs - 1], at.shift(last[a], to))
            row = piece if row is None else jnp.where(block == last[a], piece, row)
        outs[d][3 * full] = row


def spread_kernel(n, g_ref, *rest):
    msgs, (pe, pc, pr, near, far) = rest[:n], rest[n:]
    rows, npt = msgs[0].shape[1:]
    nfreq = g_ref.shape[0]
    at = Spot(n, npt)
    full = (msgs[0].shape[0] - 1) // 3
    block = at.block((rows, npt))
    half = at.sub // 2
    low = lanes((rows, npt)) % at.sub < half
    for a, out in enumerate((pe, pc, pr)):
        row = None
        for d in range(n):
            b = at.k ^ d
            for h in range(full):
                out[full * b + h] = msgs[d][full * a + h]
            left = msgs[d][3 * full]
            row = left if row is None else jnp.where(block == (b + a) % n, left, row)
        out[full * n] = move(row, npt - a * at.sub) if a else row
    slabs = full * n + 1
    for out, first in ((near, jnp.logical_not(at.even)), (far, at.even)):
        keep = jnp.logical_xor(low, jnp.logical_not(first))
        amount = jnp.where(first, half, npt - half)
        for g in range(slabs):
            out[g] = pe[g]
            out[slabs + g] = jnp.where(keep, pc[g], move(pr[g], amount))
    far[2 * slabs, :nfreq, :] = g_ref[...]
    far[2 * slabs, nfreq:, :] = jnp.zeros((rows - nfreq, npt), F32)


def window(at, own, near, far, base, nback, fback, out, where, block):
    dn, df = at.shift(at.qn, at.q), at.shift(at.qf, at.q)
    dn, df = (dn + nback) % at.npt, (df + fback) % at.npt
    step = (at.qn - at.q + at.n) % at.n
    for g in range(own.shape[0]):
        x, y, z = own[g], move(near[base + g], dn), move(far[base + g], df)
        for d, (slab, i) in enumerate(where):
            if slab == g:
                both = jnp.where(block == i, x, jnp.where(block == (i + step) % at.n, y, z))
                out[d] = move(both, at.shift(at.q, i))


def hour(e, c, r, idx, out, m0s, grow1, dissip, freqs, bins, nfreq, factor):
    ndir, rows, npt = e.shape

    def moved(d):
        x = e[d]
        if factor is not None:
            x = x * factor
        index = jnp.broadcast_to(idx[pl.ds(d, 1), :], (rows, npt))
        up = jnp.take_along_axis(x, index, axis=1)
        return x + c[d] * (up - x)

    def flux(d, here, there):
        rate = r[d]
        return rate * jnp.where(rate > 0.0, here, there)

    first = moved(0)
    m0s[...] = first
    last = moved(ndir - 1)

    def body(d, carry):
        here, before, total = carry
        there = moved(d + 1)
        f = flux(d, here, there)
        turned = here - f + before
        out[d] = turned
        return there, f, total + turned

    here, before, total = lax.fori_loop(
        0, ndir - 1, body, (first, flux(ndir - 1, last, first), jnp.zeros((rows, npt), F32)), unroll=True
    )
    f = flux(ndir - 1, here, m0s[...])
    turned = here - f + before
    out[ndir - 1] = turned
    total = total + turned
    live = lax.broadcasted_iota(jnp.int32, (rows, npt), 0) < nfreq
    total = jnp.where(live, total, 0.0)
    mean = jnp.sum(total, axis=0, keepdims=True) / bins
    factor = grow1 / (1.0 + dissip * mean)
    part = jnp.where(live, factor * total, 0.0)
    zeroth = jnp.sum(part, axis=0, keepdims=True)
    first_moment = jnp.sum(part * freqs, axis=0, keepdims=True)
    return factor, 4.0 * jnp.sqrt(zeroth / bins), zeroth / first_moment


def phase_kernel(n, stage, bins, nfreq, fields_before, *refs):
    refs = list(refs)
    take = lambda count: [refs.pop(0) for _ in range(count)]
    own, near, far, dissip_ref, freqs_ref = take(5)
    if stage == 0:
        pc, pr, g_ref = take(3)
    else:
        cw, rw, idx, gw = take(4)
        old = take(fields_before)
    if stage == 0:
        cw, rw, idx, gw = take(4)
    fields = take(1)[0]
    if stage < 2:
        msg = take(1)[0]
    else:
        eo = take(1)[0]
        backs = take(n - 1)
    ew, et, m0s = take(3)
    ndir, rows, npt = ew.shape
    dirs = ndir // n
    at = Spot(n, npt)
    shape = (rows, npt)
    block = at.block(shape)
    where = pieces(dirs, n)
    slabs = own.shape[0]
    window(at, own, near, far, 0, 0, 0, ew, where, block)
    if stage == 0:
        half = at.sub // 2
        nback, fback = jnp.where(at.even, npt - half, half), jnp.where(at.even, half, npt - half)
        window(at, pc, near, far, slabs, 0, 0, cw, where, block)
        window(at, pr, near, far, slabs, nback, fback, rw, where, block)
        m0s[...] = jnp.zeros(shape, F32)
        for d in range(ndir):
            m0s[d : d + 1, :] = ew[d, nfreq : nfreq + 1, :]
        idx[...] = (lanes(shape) + m0s[...].astype(jnp.int32)) & (npt - 1)
        gw[:nfreq, :] = 1.0 + jnp.where(block[:nfreq] == at.qf, far[2 * slabs, :nfreq, :], g_ref[...])
        gw[nfreq:, :] = jnp.ones((rows - nfreq, npt), F32)
    grow1, dissip, freqs = gw[...], dissip_ref[...], freqs_ref[...]
    fa, ha, pa = hour(ew, cw, rw, idx, et, m0s, grow1, dissip, freqs, bins, nfreq, None)
    fb, hb, pb = hour(et, cw, rw, idx, ew, m0s, grow1, dissip, freqs, bins, nfreq, fa)
    if stage < 2:
        fields[...] = jnp.concatenate([ha, hb, pa, pb], axis=0)
        for g in range(slabs):
            row = None
            for d, (slab, i) in enumerate(where):
                if slab == g:
                    piece = move(ew[d] * fb, at.shift(i, at.q))
                    row = piece if row is None else jnp.where(block == i, piece, row)
            msg[g] = row
    else:
        h = [o[:2] for o in old] + [ha, hb]
        p = [o[2:] for o in old] + [pa, pb]
        every = jnp.concatenate(h + p + [jnp.zeros((16 - 2 * STEPS, npt), F32)], axis=0)
        fields[...] = every
        for j in range(dirs):
            eo[j] = ew[dirs * at.k + j] * fb
        m0s[...] = jnp.zeros(shape, F32)
        m0s[:16, :] = every
        tail = m0s[...]
        for d in range(1, n):
            b = at.k ^ d
            for g in range(backs[0].shape[0]):
                row = None
                for i in range(n):
                    j = n * g + i
                    if j > dirs:
                        continue
                    x = ew[dirs * b + j] * fb if j < dirs else tail
                    piece = move(x, at.shift(i, at.q))
                    row = piece if row is None else jnp.where(block == i, piece, row)
                backs[d - 1][g] = row


def order_kernel(n, dirs, f_ref, order_ref, *rest):
    msgs, series = rest[: n - 1], rest[n - 1]
    rows, npt = f_ref.shape
    at = Spot(n, npt)
    block = at.block((rows, npt))
    fields = f_ref[...]
    for d in range(1, n):
        q = subtile_of(at.s, at.k ^ d, n)
        piece = move(msgs[d - 1][dirs // n, :rows, :], at.shift(q, dirs % n))
        fields = jnp.where(block == q, piece, fields)
    index = jnp.broadcast_to((order_ref[...] - at.s * npt).reshape(1, npt), (rows, npt))
    series[...] = jnp.take_along_axis(fields, index, axis=1)


def join_kernel(n, e_ref, *rest):
    msgs, out = rest[: n - 1], rest[n - 1]
    dirs, rows, npt = e_ref.shape
    nfreq = out.shape[1]
    at = Spot(n, npt)
    block = at.block((rows, npt))
    qs = [subtile_of(at.s, at.k ^ d, n) for d in range(1, n)]
    for j in range(dirs):
        x = e_ref[j]
        for d in range(1, n):
            piece = move(msgs[d - 1][j // n], at.shift(qs[d - 1], j % n))
            x = jnp.where(block == qs[d - 1], piece, x)
        out[j] = x[:nfreq]


def hand_kernel(tiles, own_ref, *rest):
    others, out = rest[:-1], rest[-1]
    rows, npt = out.shape
    share = npt // tiles
    s = lax.axis_index("space")
    block = lanes((16, npt)) // share
    x = own_ref[...]
    for d in range(1, tiles):
        frm = s ^ d
        piece = move(others[d - 1][...], ((frm - s + tiles) % tiles) * share)
        x = jnp.where(block == frm, piece, x)
    out[...] = x[:rows]


def call(kernel, outs, scratch, *args, hbm=0):
    vm = pl.BlockSpec(memory_space=pltpu.VMEM)
    return pl.pallas_call(
        kernel,
        out_shape=[jax.ShapeDtypeStruct(shape, dtype) for shape, dtype in outs],
        in_specs=[pl.BlockSpec(memory_space=pltpu.HBM)] * hbm + [vm] * (len(args) - hbm),
        out_specs=[vm] * len(outs),
        scratch_shapes=scratch,
        compiler_params=pltpu.CompilerParams(vmem_limit_bytes=(54600 if hbm else 40960) * 1024),
    )(*args)


def on_device(spectrum, courant, refraction, growth, dissip, upwind, send_order):
    dirs, nfreq, npt = spectrum.shape
    tiles, n = lax.axis_size("space"), lax.axis_size("spec")
    total, reach = npt * tiles, npt // 8
    ndir = dirs * n
    bins = ndir * nfreq
    full = (dirs - 1) // n
    slabs = full * n + 1
    peers = range(1, n)
    swap = lambda x, d: lax.ppermute(x, "spec", [(k, k ^ d) for k in range(n)])
    near_to = lambda x: swap(x, 1)
    route = far_route(tiles, n)
    far_to = lambda x: lax.ppermute(x, ("space", "spec"), route)
    wide = lambda v: jnp.pad(jnp.broadcast_to(v[:, None], (nfreq, npt)), ((0, ROWS - nfreq), (0, 0)))
    freqs, dissip = wide(frequency_table(nfreq)), wide(dissip)
    field = (ROWS, npt)
    state, packed = ((ndir, *field), F32), ((slabs, *field), F32)

    part = pltpu.VMEM(spectrum.shape, F32)
    sent = call(
        functools.partial(pack_kernel, n, total, reach),
        [((3 * full + 1, *field), F32)] * n,
        [part, part, part, pltpu.VMEM(upwind.shape, jnp.int32), pltpu.VMEM((3 * dirs, *field), F32), pltpu.SemaphoreType.DMA((4,))],
        spectrum, courant, refraction, upwind, hbm=4,
    )
    got = [sent[0]] + [swap(sent[d], d) for d in peers]
    e, c, r, near, far = call(
        functools.partial(spread_kernel, n),
        [packed] * 3 + [((2 * slabs, *field), F32), ((2 * slabs + 1, *field), F32)],
        [],
        growth, *got,
    )
    scratch = [pltpu.VMEM(shape, F32) for shape in ((ndir, *field), (ndir, *field), field)]
    phase = lambda stage, before, outs, *args: call(
        functools.partial(phase_kernel, n, stage, bins, nfreq, before), outs, scratch, *args
    )
    some = ((4, npt), F32)
    c, r, idx, gw, f0, e = phase(
        0, 0, [state, state, (field, jnp.int32), (field, F32), some, packed],
        e, near_to(near), far_to(far), dissip, freqs, c, r, growth,
    )
    f1, e = phase(1, 1, [some, packed], e, near_to(e), far_to(e), dissip, freqs, c, r, idx, gw, f0)
    back = ((-(-(dirs + 1) // n), *field), F32)
    fields, own, *backs = phase(
        2, 2, [((16, npt), F32), ((dirs, *field), F32)] + [back] * (n - 1),
        e, near_to(e), far_to(e), dissip, freqs, c, r, idx, gw, f0, f1,
    )
    backs = [swap(x, d) for d, x in zip(peers, backs)]
    (ordered,) = call(functools.partial(order_kernel, n, dirs), [((16, npt), F32)], [], fields, send_order, *backs)
    (energy,) = call(functools.partial(join_kernel, n), [(spectrum.shape, F32)], [], own, *backs)
    if tiles == 4:
        others = [lax.ppermute(ordered, "space", [(t, t ^ d) for t in range(tiles)]) for d in range(1, tiles)]
        (series,) = call(functools.partial(hand_kernel, tiles), [((2 * STEPS, npt), F32)], [], ordered, *others)
    else:
        parts = ordered[: 2 * STEPS].reshape(2 * STEPS, tiles, npt // tiles)
        series = lax.all_to_all(parts, "space", split_axis=1, concat_axis=1, tiled=True).reshape(2 * STEPS, npt)
    return (energy, series)


def solution(mesh):
    placed = (
        P("spec", None, ("runs", "space")),
        P("spec", None, "space"),
        P("spec", None, "space"),
        P(None, ("runs", "space")),
        P(),
        P("spec", "space"),
        P("space"),
    )
    return jax.shard_map(
        on_device,
        mesh=mesh,
        in_specs=placed,
        out_specs=(P("spec", None, ("runs", "space")), P(None, ("runs", "space"))),
        check_vma=False,
    )
```

time: 72.3 us -> 60.8 us (0.84)
  Pallas kernels: 16.7 us -> 11.3 us
  local copies, waits for them, and re-layouts: 4.27 us -> 0.85 us
  starting transfers between devices: 23.1 us -> 21.6 us
  waiting for transfers between devices: 27.3 us -> 26.1 us
    pallas_call x7 -> x8, Pallas kernels: 16.7 us -> 11.3 us  [call(): pl.pallas_call(kernel, out_shape=[jax.ShapeDtypeStruct(shape, dtype) for...]
    unnamed x14 -> x8, local copies, waits for them, and re-layouts: 4.12 us -> 0.71 us
    ppermute x3, starting transfers between devices: 6.73 us -> 5.28 us  [on_device(): lax.ppermute(ordered, 'space', [(t, t ^ d) for t in range(tiles)])]
    ppermute x3, waiting for transfers between devices: 3.42 us -> 2.29 us  [on_device(): lax.ppermute(ordered, 'space', [(t, t ^ d) for t in range(tiles)])]
  transfers between devices with their start and end apart: 15 -> 15, of which waited for: 10 -> 10; matrix products, arithmetic and copies ran while one was open for 0% -> 0% of each run, Pallas kernels for 0% -> 1%
where the time goes in v2:
time: 60.8 us; the launch traced here: 60.6 us
  waiting for transfers between devices  26.1 us (43%)
  starting transfers between devices  21.6 us (36%)
  Pallas kernels  11.3 us (19%)
  local copies, waits for them, and re-layouts  0.85 us (1%)
  between operations  0.74 us (1%)
    ppermute x9, waiting for transfers between devices, on_device(): swap = lambda x, d: lax.ppermute(x, 'spec', [(k, k ^ d) for k in range(n)])  12.2 us
    ppermute x3, waiting for transfers between devices, on_device(): far_to = lambda x: lax.ppermute(x, ('space', 'spec'), route)  11.7 us
    ppermute x3, starting transfers between devices, on_device(): far_to = lambda x: lax.ppermute(x, ('space', 'spec'), route)  11.3 us
    pallas_call x8, Pallas kernels, call(): pl.pallas_call(kernel, out_shape=[jax.ShapeDtypeStruct(shape, dtype) for...  11.3 us
    ppermute x3, starting transfers between devices, on_device(): lax.ppermute(ordered, 'space', [(t, t ^ d) for t in range(tiles)])  5.28 us
    ppermute x9, starting transfers between devices, on_device(): swap = lambda x, d: lax.ppermute(x, 'spec', [(k, k ^ d) for k in range(n)])  5.07 us
    ppermute x3, waiting for transfers between devices, on_device(): lax.ppermute(ordered, 'space', [(t, t ^ d) for t in range(tiles)])  2.29 us
  transfers between devices with their start and end apart: 15, of which 10 were waited for; matrix products, arithmetic and copies ran while one was open for 0% of the time, Pallas kernels for 1%

profile of v2, /device:TPU:0, one launch (start us, length us, event | category | flops | bytes accessed | tf_op | source)
XLA Modules:
  0.0 60.6 jit_solution(10860828805951415751)
XLA Ops:
  0.6 0.7 %copy-done.1 = s32[9,128]{1,0:T(8,128)S(1)} copy-done((s32[9,128]{1,0:T(8,128)S(1)}, s32[9,128]{1,0:T(8,128)}, u32[]{:S(2)}) %copy-start.1) | copy-done | bytes 4632
  1.3 1.8 %shard_map.86 = (f32[7,40,128]{2,1,0:T(8,128)S(1)}, f32[7,40,128]{2,1,0:T(8,128)S(1)}, f32[7,40,128]{2,1,0:T(8,128)S(1)}, f32[7,40,128]{2,1,0:T(8,128)S(1)}) custom-call(f32[9,36,128]{2,1,0:T(8,128)} %e_hbm.1, f32[9,36,128]{2,1,0:T(8,128)} %c_hbm.1, f32[9,36,128]{2,1,0:T(8,128)} %r_hbm.1, s32[9,128]{1,0:T(8,128)S(1)} %copy-done.1), custom_call_target="tpu_custom_call" | custom-call | tf_op jit(solution)/shard_map/pallas_call | solution.py:311
  3.1 0.5 collective-permute-start
  3.6 2.6 %collective-permute-start.1 = (f32[7,40,128]{2,1,0:T(8,128)S(1)}, f32[7,40,128]{2,1,0:T(8,128)S(1)}, u32[]{:S(2)}, u32[]{:S(2)}) collective-permute-start(f32[7,40,128]{2,1,0:T(8,128)S(1)} %get-tuple-element.26), channel_id=1, source_target_pairs={{0,2},{1,3},{2,0},{3,1},{4,6},{5,7},{6,4},{7,5},{8,10},{9,11},{10,... | collective-permute-start | bytes 430088 | tf_op jit(solution)/shard_map/ppermute | solution.py:330
  6.3 4.5 %collective-permute-done.1.rest_2_ = f32[7,40,128]{2,1,0:T(8,128)S(1)} collective-permute-done((f32[7,40,128]{2,1,0:T(8,128)S(1)}, f32[7,40,128]{2,1,0:T(8,128)S(1)}, u32[]{:S(2)}, u32[]{:S(2)}) %collective-permute-start.1) | collective-permute-done | bytes 143392 | tf_op jit(solution)/shard_map/ppermute | solution.py:330
  10.8 2.5 %collective-permute-done.2.rest_3_ = f32[7,40,128]{2,1,0:T(8,128)S(1)} collective-permute-done((f32[7,40,128]{2,1,0:T(8,128)S(1)}, f32[7,40,128]{2,1,0:T(8,128)S(1)}, u32[]{:S(2)}, u32[]{:S(2)}) %collective-permute-start.2) | collective-permute-done | bytes 143392 | tf_op jit(solution)/shard_map/ppermute | solution.py:330
  13.4 0.2 shard_map.87
  13.6 3.7 %collective-permute-start.4 = (f32[19,40,128]{2,1,0:T(8,128)S(1)}, f32[19,40,128]{2,1,0:T(8,128)S(1)}, u32[]{:S(2)}, u32[]{:S(2)}) collective-permute-start(f32[19,40,128]{2,1,0:T(8,128)S(1)} %get-tuple-element.30), channel_id=1, source_target_pairs={{0,12},{1,2},{2,1},{3,7},{4,8},{5,6},{6,5},{7,3},{8,4},{9,10},{10,... | collective-permute-start | bytes 1167368 | tf_op jit(solution)/shard_map/ppermute | solution.py:333
  17.4 1.6 %collective-permute-done.3.refs_1_ = f32[18,40,128]{2,1,0:T(8,128)S(1)} collective-permute-done((f32[18,40,128]{2,1,0:T(8,128)S(1)}, f32[18,40,128]{2,1,0:T(8,128)S(1)}, u32[]{:S(2)}, u32[]{:S(2)}) %collective-permute-start.3) | collective-permute-done | bytes 368672 | tf_op jit(solution)/shard_map/ppermute | solution.py:330
  19.0 4.3 %collective-permute-done.4.refs_2_ = f32[19,40,128]{2,1,0:T(8,128)S(1)} collective-permute-done((f32[19,40,128]{2,1,0:T(8,128)S(1)}, f32[19,40,128]{2,1,0:T(8,128)S(1)}, u32[]{:S(2)}, u32[]{:S(2)}) %collective-permute-start.4) | collective-permute-done | bytes 389152 | tf_op jit(solution)/shard_map/ppermute | solution.py:333
  23.3 0.1 pad.14.refs_4_
  23.4 0.1 pad.12.refs_3_
  23.5 3.6 %shard_map.88 = (f32[36,40,128]{2,1,0:T(8,128)S(1)}, f32[36,40,128]{2,1,0:T(8,128)S(1)}, s32[40,128]{1,0:T(8,128)S(1)}, f32[40,128]{1,0:T(8,128)S(1)}, f32[4,128]{1,0:T(4,128)S(1)}, /*index=5*/f32[9,40,128]{2,1,0:T(8,128)S(1)}) custom-call(f32[9,40,128]{2,1,0:T(8,128)S(1)} %get-tuple-element.28.refs_0_, f32[18,40,128]{2,1,0:T(8,128)S(1)} %collective-permute-done.3.refs_1_, ...), custom_call_target="tpu_custom_call" | custom-call | tf_op jit(solution)/shard_map/pallas_call | solution.py:311
  27.1 3.7 %collective-permute-start.6 = (f32[9,40,128]{2,1,0:T(8,128)S(1)}, f32[9,40,128]{2,1,0:T(8,128)S(1)}, u32[]{:S(2)}, u32[]{:S(2)}) collective-permute-start(f32[9,40,128]{2,1,0:T(8,128)S(1)} %get-tuple-element.33.refs_0_), channel_id=1, source_target_pairs={{0,12},{1,2},{2,1},{3,7},{4,8},{5,6},{6,5},{7,3},{8,4},{9,10},{10,... | collective-permute-start | bytes 552968 | tf_op jit(solution)/shard_map/ppermute | solution.py:333
  30.8 3.7 %collective-permute-done.6.refs_2_ = f32[9,40,128]{2,1,0:T(8,128)S(1)} collective-permute-done((f32[9,40,128]{2,1,0:T(8,128)S(1)}, f32[9,40,128]{2,1,0:T(8,128)S(1)}, u32[]{:S(2)}, u32[]{:S(2)}) %collective-permute-start.6) | collective-permute-done | bytes 184352 | tf_op jit(solution)/shard_map/ppermute | solution.py:333
  34.6 2.0 %shard_map.89 = (f32[4,128]{1,0:T(4,128)S(1)}, f32[9,40,128]{2,1,0:T(8,128)S(1)}) custom-call(f32[9,40,128]{2,1,0:T(8,128)S(1)} %get-tuple-element.33.refs_0_, f32[9,40,128]{2,1,0:T(8,128)S(1)} %collective-permute-done.5.refs_1_, f32[9,40,128]{2,1,0:T(8,128)S(1)} %collective-permute-done.6.refs_2_, f32[40,128]{1,0:T(8,128)S(1)} %pad.12.refs_3_, ...), custom_call_target="tpu_custom_call" | custom-call | tf_op jit(solution)/shard_map/pallas_call | solution.py:311
  36.6 3.8 %collective-permute-start.8 = (f32[9,40,128]{2,1,0:T(8,128)S(1)}, f32[9,40,128]{2,1,0:T(8,128)S(1)}, u32[]{:S(2)}, u32[]{:S(2)}) collective-permute-start(f32[9,40,128]{2,1,0:T(8,128)S(1)} %get-tuple-element.39.refs_0_), channel_id=1, source_target_pairs={{0,12},{1,2},{2,1},{3,7},{4,8},{5,6},{6,5},{7,3},{8,4},{9,10},{10,... | collective-permute-start | bytes 552968 | tf_op jit(solution)/shard_map/ppermute | solution.py:333
  40.4 3.7 %collective-permute-done.8.refs_2_ = f32[9,40,128]{2,1,0:T(8,128)S(1)} collective-permute-done((f32[9,40,128]{2,1,0:T(8,128)S(1)}, f32[9,40,128]{2,1,0:T(8,128)S(1)}, u32[]{:S(2)}, u32[]{:S(2)}) %collective-permute-start.8) | collective-permute-done | bytes 184352 | tf_op jit(solution)/shard_map/ppermute | solution.py:333
  44.1 1.9 %shard_map.90 = (f32[16,128]{1,0:T(8,128)S(1)}, f32[9,40,128]{2,1,0:T(8,128)S(1)}, f32[3,40,128]{2,1,0:T(8,128)S(1)}, f32[3,40,128]{2,1,0:T(8,128)S(1)}, f32[3,40,128]{2,1,0:T(8,128)S(1)}) custom-call(f32[9,40,128]{2,1,0:T(8,128)S(1)} %get-tuple-element.39.refs_0_, f32[9,40,128]{2,1,0:T(8,128)S(1)} %collective-permute-done.7.refs_1_, ...), custom_call_target="tpu_custom_call" | custom-call | tf_op jit(solution)/shard_map/pallas_call | solution.py:311
  46.0 0.1 collective-permute-start.9
  46.1 0.1 collective-permute-start.10
  46.1 1.8 %collective-permute-start.11 = (f32[3,40,128]{2,1,0:T(8,128)S(1)}, f32[3,40,128]{2,1,0:T(8,128)S(1)}, u32[]{:S(2)}, u32[]{:S(2)}) collective-permute-start(f32[3,40,128]{2,1,0:T(8,128)S(1)} %get-tuple-element.44), channel_id=1, source_target_pairs={{0,3},{1,2},{2,1},{3,0},{4,7},{5,6},{6,5},{7,4},{8,11},{9,10},{10,... | collective-permute-start | bytes 184328 | tf_op jit(solution)/shard_map/ppermute | solution.py:330
  47.9 3.0 %collective-permute-done.10.rest_1_ = f32[3,40,128]{2,1,0:T(8,128)S(1)} collective-permute-done((f32[3,40,128]{2,1,0:T(8,128)S(1)}, f32[3,40,128]{2,1,0:T(8,128)S(1)}, u32[]{:S(2)}, u32[]{:S(2)}) %collective-permute-start.10) | collective-permute-done | bytes 61472 | tf_op jit(solution)/shard_map/ppermute | solution.py:330
  50.9 0.4 collective-permute-done.11.rest_2_
  51.3 0.1 shard_map.92.own_ref
  51.5 3.7 %collective-permute-start.14 = (f32[16,128]{1,0:T(8,128)S(1)}, f32[16,128]{1,0:T(8,128)S(1)}, u32[]{:S(2)}, u32[]{:S(2)}) collective-permute-start(f32[16,128]{1,0:T(8,128)S(1)} %shard_map.92.own_ref), channel_id=1, source_target_pairs={{0,12},{4,8},{8,4},{12,0},{1,13},{5,9},{9,5},{13,1},{2,14},{6,10},... | collective-permute-start | bytes 24584 | tf_op jit(solution)/shard_map/ppermute | solution.py:372
  55.2 1.0 %collective-permute-start.13 = (f32[16,128]{1,0:T(8,128)S(1)}, f32[16,128]{1,0:T(8,128)S(1)}, u32[]{:S(2)}, u32[]{:S(2)}) collective-permute-start(f32[16,128]{1,0:T(8,128)S(1)} %shard_map.92.own_ref), channel_id=1, source_target_pairs={{0,8},{4,12},{8,0},{12,4},{1,9},{5,13},{9,1},{13,5},{2,10},{6,14},... | collective-permute-start | bytes 24584 | tf_op jit(solution)/shard_map/ppermute | solution.py:372
  56.2 0.5 collective-permute-start.12
  56.8 0.9 %shard_map.91 = f32[9,36,128]{2,1,0:T(8,128)} custom-call(f32[9,40,128]{2,1,0:T(8,128)S(1)} %get-tuple-element.41.e_ref, f32[3,40,128]{2,1,0:T(8,128)S(1)} %collective-permute-done.9.rest_0_, f32[3,40,128]{2,1,0:T(8,128)S(1)} %collective-permute-done.10.rest_1_, f32[3,40,128]{2,1,0:T(8,128)S(1)} %collective-permute-done.11.rest_2_), custom_call_target="tpu_custom_call" | custom-call | tf_op jit(solution)/shard_map/pallas_call | solution.py:311
  57.7 2.2 %collective-permute-done.13.rest_1_ = f32[16,128]{1,0:T(8,128)S(1)} collective-permute-done((f32[16,128]{1,0:T(8,128)S(1)}, f32[16,128]{1,0:T(8,128)S(1)}, u32[]{:S(2)}, u32[]{:S(2)}) %collective-permute-start.13) | collective-permute-done | bytes 8224 | tf_op jit(solution)/shard_map/ppermute | solution.py:372
  59.9 0.1 collective-permute-done.12.rest_0_
  60.0 0.7 %shard_map.93 = f32[12,128]{1,0:T(8,128)} custom-call(f32[16,128]{1,0:T(8,128)S(1)} %shard_map.92.own_ref, f32[16,128]{1,0:T(8,128)S(1)} %collective-permute-done.12.rest_0_, f32[16,128]{1,0:T(8,128)S(1)} %collective-permute-done.13.rest_1_, f32[16,128]{1,0:T(8,128)S(1)} %collective-permute-done.14.rest_2_), custom_call_target="tpu_custom_call" | custom-call | tf_op jit(solution)/shard_map/pallas_call | solution.py:311
  (19 shorter events, 0.1 us)
Async XLA Ops:
  0.6 0.7 %copy-start.1 = (s32[9,128]{1,0:T(8,128)S(1)}, s32[9,128]{1,0:T(8,128)}, u32[]{:S(2)}) copy-start(s32[9,128]{1,0:T(8,128)} %u_hbm.1) | copy-start | bytes 13828
  1.3 12.0 %copy-start = (f32[36,128]{1,0:T(8,128)S(1)}, f32[36,128]{1,0:T(8,128)}, u32[]{:S(2)}) copy-start(f32[36,128]{1,0:T(8,128)} %refs_7_.1) | copy-start | bytes 55300
  3.1 3.2 %collective-permute-start = (f32[7,40,128]{2,1,0:T(8,128)S(1)}, f32[7,40,128]{2,1,0:T(8,128)S(1)}, u32[]{:S(2)}, u32[]{:S(2)}) collective-permute-start(f32[7,40,128]{2,1,0:T(8,128)S(1)} %get-tuple-element.25), channel_id=1, source_target_pairs={{0,1},{1,0},{2,3},{3,2},{4,5},{5,4},{6,7},{7,6},{8,9},{9,8},{10,11... | collective-permute-start | bytes 430088 | tf_op jit(solution)/shard_map/ppermute | solution.py:330
  3.6 7.2 %collective-permute-start.1 = (f32[7,40,128]{2,1,0:T(8,128)S(1)}, f32[7,40,128]{2,1,0:T(8,128)S(1)}, u32[]{:S(2)}, u32[]{:S(2)}) collective-permute-start(f32[7,40,128]{2,1,0:T(8,128)S(1)} %get-tuple-element.26), channel_id=1, source_target_pairs={{0,2},{1,3},{2,0},{3,1},{4,6},{5,7},{6,4},{7,5},{8,10},{9,11},{10,... | collective-permute-start | bytes 430088 | tf_op jit(solution)/shard_map/ppermute | solution.py:330
  6.2 7.2 %collective-permute-start.2 = (f32[7,40,128]{2,1,0:T(8,128)S(1)}, f32[7,40,128]{2,1,0:T(8,128)S(1)}, u32[]{:S(2)}, u32[]{:S(2)}) collective-permute-start(f32[7,40,128]{2,1,0:T(8,128)S(1)} %get-tuple-element.27), channel_id=1, source_target_pairs={{0,3},{1,2},{2,1},{3,0},{4,7},{5,6},{6,5},{7,4},{8,11},{9,10},{10,... | collective-permute-start | bytes 430088 | tf_op jit(solution)/shard_map/ppermute | solution.py:330
  13.6 3.8 %copy-start.3 = (f32[36]{0:T(128)S(1)}, f32[36]{0:T(128)}, u32[]{:S(2)}) copy-start(f32[36]{0:T(128)} %param.11) | copy-start | bytes 436
  13.6 9.7 %collective-permute-start.4 = (f32[19,40,128]{2,1,0:T(8,128)S(1)}, f32[19,40,128]{2,1,0:T(8,128)S(1)}, u32[]{:S(2)}, u32[]{:S(2)}) collective-permute-start(f32[19,40,128]{2,1,0:T(8,128)S(1)} %get-tuple-element.30), channel_id=1, source_target_pairs={{0,12},{1,2},{2,1},{3,7},{4,8},{5,6},{6,5},{7,3},{8,4},{9,10},{10,... | collective-permute-start | bytes 1167368 | tf_op jit(solution)/shard_map/ppermute | solution.py:333
  17.4 1.7 %collective-permute-start.3 = (f32[18,40,128]{2,1,0:T(8,128)S(1)}, f32[18,40,128]{2,1,0:T(8,128)S(1)}, u32[]{:S(2)}, u32[]{:S(2)}) collective-permute-start(f32[18,40,128]{2,1,0:T(8,128)S(1)} %get-tuple-element.29), channel_id=1, source_target_pairs={{0,1},{1,0},{2,3},{3,2},{4,5},{5,4},{6,7},{7,6},{8,9},{9,8},{10,11... | collective-permute-start | bytes 1105928 | tf_op jit(solution)/shard_map/ppermute | solution.py:330
  27.1 7.4 %collective-permute-start.6 = (f32[9,40,128]{2,1,0:T(8,128)S(1)}, f32[9,40,128]{2,1,0:T(8,128)S(1)}, u32[]{:S(2)}, u32[]{:S(2)}) collective-permute-start(f32[9,40,128]{2,1,0:T(8,128)S(1)} %get-tuple-element.33.refs_0_), channel_id=1, source_target_pairs={{0,12},{1,2},{2,1},{3,7},{4,8},{5,6},{6,5},{7,3},{8,4},{9,10},{10,... | collective-permute-start | bytes 552968 | tf_op jit(solution)/shard_map/ppermute | solution.py:333
  30.8 3.7 %collective-permute-start.5 = (f32[9,40,128]{2,1,0:T(8,128)S(1)}, f32[9,40,128]{2,1,0:T(8,128)S(1)}, u32[]{:S(2)}, u32[]{:S(2)}) collective-permute-start(f32[9,40,128]{2,1,0:T(8,128)S(1)} %get-tuple-element.33.refs_0_), channel_id=1, source_target_pairs={{0,1},{1,0},{2,3},{3,2},{4,5},{5,4},{6,7},{7,6},{8,9},{9,8},{10,11... | collective-permute-start | bytes 552968 | tf_op jit(solution)/shard_map/ppermute | solution.py:330
  36.6 7.5 %collective-permute-start.8 = (f32[9,40,128]{2,1,0:T(8,128)S(1)}, f32[9,40,128]{2,1,0:T(8,128)S(1)}, u32[]{:S(2)}, u32[]{:S(2)}) collective-permute-start(f32[9,40,128]{2,1,0:T(8,128)S(1)} %get-tuple-element.39.refs_0_), channel_id=1, source_target_pairs={{0,12},{1,2},{2,1},{3,7},{4,8},{5,6},{6,5},{7,3},{8,4},{9,10},{10,... | collective-permute-start | bytes 552968 | tf_op jit(solution)/shard_map/ppermute | solution.py:333
  40.4 3.7 %collective-permute-start.7 = (f32[9,40,128]{2,1,0:T(8,128)S(1)}, f32[9,40,128]{2,1,0:T(8,128)S(1)}, u32[]{:S(2)}, u32[]{:S(2)}) collective-permute-start(f32[9,40,128]{2,1,0:T(8,128)S(1)} %get-tuple-element.39.refs_0_), channel_id=1, source_target_pairs={{0,1},{1,0},{2,3},{3,2},{4,5},{5,4},{6,7},{7,6},{8,9},{9,8},{10,11... | collective-permute-start | bytes 552968 | tf_op jit(solution)/shard_map/ppermute | solution.py:330
  46.0 1.9 %collective-permute-start.9 = (f32[3,40,128]{2,1,0:T(8,128)S(1)}, f32[3,40,128]{2,1,0:T(8,128)S(1)}, u32[]{:S(2)}, u32[]{:S(2)}) collective-permute-start(f32[3,40,128]{2,1,0:T(8,128)S(1)} %get-tuple-element.42), channel_id=1, source_target_pairs={{0,1},{1,0},{2,3},{3,2},{4,5},{5,4},{6,7},{7,6},{8,9},{9,8},{10,11... | collective-permute-start | bytes 184328 | tf_op jit(solution)/shard_map/ppermute | solution.py:330
  46.1 4.9 %collective-permute-start.10 = (f32[3,40,128]{2,1,0:T(8,128)S(1)}, f32[3,40,128]{2,1,0:T(8,128)S(1)}, u32[]{:S(2)}, u32[]{:S(2)}) collective-permute-start(f32[3,40,128]{2,1,0:T(8,128)S(1)} %get-tuple-element.43), channel_id=1, source_target_pairs={{0,2},{1,3},{2,0},{3,1},{4,6},{5,7},{6,4},{7,5},{8,10},{9,11},{10,... | collective-permute-start | bytes 184328 | tf_op jit(solution)/shard_map/ppermute | solution.py:330
  46.1 5.2 %copy-start.2 = (s32[128]{0:T(128)S(1)}, s32[128]{0:T(128)}, u32[]{:S(2)}) copy-start(s32[128]{0:T(128)} %order_ref.1) | copy-start | bytes 1540
  46.1 5.2 %collective-permute-start.11 = (f32[3,40,128]{2,1,0:T(8,128)S(1)}, f32[3,40,128]{2,1,0:T(8,128)S(1)}, u32[]{:S(2)}, u32[]{:S(2)}) collective-permute-start(f32[3,40,128]{2,1,0:T(8,128)S(1)} %get-tuple-element.44), channel_id=1, source_target_pairs={{0,3},{1,2},{2,1},{3,0},{4,7},{5,6},{6,5},{7,4},{8,11},{9,10},{10,... | collective-permute-start | bytes 184328 | tf_op jit(solution)/shard_map/ppermute | solution.py:330
  51.5 6.2 %collective-permute-start.14 = (f32[16,128]{1,0:T(8,128)S(1)}, f32[16,128]{1,0:T(8,128)S(1)}, u32[]{:S(2)}, u32[]{:S(2)}) collective-permute-start(f32[16,128]{1,0:T(8,128)S(1)} %shard_map.92.own_ref), channel_id=1, source_target_pairs={{0,12},{4,8},{8,4},{12,0},{1,13},{5,9},{9,5},{13,1},{2,14},{6,10},... | collective-permute-start | bytes 24584 | tf_op jit(solution)/shard_map/ppermute | solution.py:372
  55.2 4.6 %collective-permute-start.13 = (f32[16,128]{1,0:T(8,128)S(1)}, f32[16,128]{1,0:T(8,128)S(1)}, u32[]{:S(2)}, u32[]{:S(2)}) collective-permute-start(f32[16,128]{1,0:T(8,128)S(1)} %shard_map.92.own_ref), channel_id=1, source_target_pairs={{0,8},{4,12},{8,0},{12,4},{1,9},{5,13},{9,1},{13,5},{2,10},{6,14},... | collective-permute-start | bytes 24584 | tf_op jit(solution)/shard_map/ppermute | solution.py:372
  56.2 3.7 %collective-permute-start.12 = (f32[16,128]{1,0:T(8,128)S(1)}, f32[16,128]{1,0:T(8,128)S(1)}, u32[]{:S(2)}, u32[]{:S(2)}) collective-permute-start(f32[16,128]{1,0:T(8,128)S(1)} %shard_map.92.own_ref), channel_id=1, source_target_pairs={{0,4},{4,0},{8,12},{12,8},{1,5},{5,1},{9,13},{13,9},{2,6},{6,2},{1... | collective-permute-start | bytes 24584 | tf_op jit(solution)/shard_map/ppermute | solution.py:372

commit v3 on v2

--- a/solution.py
+++ b/solution.py
@@ -16,19 +16,35 @@
     return 0.035 * jnp.float32(1.1) ** jnp.arange(count, dtype=jnp.float32)
 
 
+def orders(tiles, n):
+    up = list(range(n))
+    if tiles == 4 and n == 4:
+        return [up, [3, 1, 0, 2], [2, 0, 1, 3], up[::-1]]
+    return [up if s % 2 == 0 else up[::-1] for s in range(tiles)]
+
+
 def subtile_of(s, k, n):
-    return jnp.where(s % 2 == 0, k, n - 1 - k)
-
-
-def far_route(tiles, n):
+    tiles = lax.axis_size("space")
+    table = orders(tiles, n)
+    if tiles != 4:
+        return jnp.where(s % 2 == 0, k, n - 1 - k)
+    q = k
+    for t in range(1, tiles):
+        here = n - 1
+        for i in range(n - 1):
+            here = jnp.where(k == table[t][i], i, here)
+        q = jnp.where(s == t, here, q)
+    return q
+
+
+def ring_route(tiles, n, far):
+    table = orders(tiles, n)
     route = []
     for s in range(tiles):
-        for k in range(n):
-            q = k if s % 2 == 0 else n - 1 - k
+        for q in range(n):
             at = s * n + q
-            to = (at - 1 if q % 2 == 0 else at + 1) % (tiles * n)
-            ts, tq = divmod(to, n)
-            route.append((s * n + k, ts * n + (tq if ts % 2 == 0 else n - 1 - tq)))
+            to = (at + (1 if (q % 2 == 0) != far else -1)) % (tiles * n)
+            route.append((s * n + table[s][q], to // n * n + table[to // n][to % n]))
     return route
 
 
@@ -37,10 +53,12 @@
 
 
 class Spot:
-    def __init__(self, n, npt):
+    def __init__(self, n, npt, q=None):
         self.n, self.sub, self.npt = n, npt // n, npt
-        self.s, self.k = lax.axis_index("space"), lax.axis_index("spec")
-        self.q = subtile_of(self.s, self.k, n)
+        if q is None:
+            self.s, self.k = lax.axis_index("space"), lax.axis_index("spec")
+            q = subtile_of(self.s, self.k, n)
+        self.q = q
         self.qn = self.q ^ 1
         self.qf = n - 1 - self.q
         self.even = self.q % 2 == 0
@@ -51,8 +69,14 @@
     def block(self, shape):
         return lanes(shape) // self.sub
 
+    def each(self, body):
+        for q in range(self.n):
+            pl.when(self.q == q)(functools.partial(body, Spot(self.n, self.npt, q)))
+
 
 def move(x, amount):
+    if isinstance(amount, int) and amount == 0:
+        return x
     return pltpu.roll(x, amount, 1)
 
 
@@ -124,26 +148,31 @@
             row = left if row is None else jnp.where(block == (b + a) % n, left, row)
         out[full * n] = move(row, npt - a * at.sub) if a else row
     slabs = full * n + 1
-    for out, first in ((near, jnp.logical_not(at.even)), (far, at.even)):
-        keep = jnp.logical_xor(low, jnp.logical_not(first))
-        amount = jnp.where(first, half, npt - half)
-        for g in range(slabs):
-            out[g] = pe[g]
-            out[slabs + g] = jnp.where(keep, pc[g], move(pr[g], amount))
+    def fill(even):
+        for out, first in ((near, not even), (far, even)):
+            for g in range(slabs):
+                out[g] = pe[g]
+                out[slabs + g] = jnp.where(low == first, pc[g], move(pr[g], half if first else npt - half))
+
+    pl.when(at.even)(functools.partial(fill, True))
+    pl.when(jnp.logical_not(at.even))(functools.partial(fill, False))
     far[2 * slabs, :nfreq, :] = g_ref[...]
     far[2 * slabs, nfreq:, :] = jnp.zeros((rows - nfreq, npt), F32)
 
 
-def window(at, own, near, far, base, nback, fback, out, where, block):
+def window(at, own, near, far, base, nback, fback, out, where, block, turned):
     dn, df = at.shift(at.qn, at.q), at.shift(at.qf, at.q)
     dn, df = (dn + nback) % at.npt, (df + fback) % at.npt
     step = (at.qn - at.q + at.n) % at.n
-    for g in range(own.shape[0]):
-        x, y, z = own[g], move(near[base + g], dn), move(far[base + g], df)
-        for d, (slab, i) in enumerate(where):
-            if slab == g:
-                both = jnp.where(block == i, x, jnp.where(block == (i + step) % at.n, y, z))
-                out[d] = move(both, at.shift(at.q, i))
+    slabs = own.shape[0]
+    for source, start, amount in ((near, 0, dn), (far, slabs, df)):
+        for g in range(slabs):
+            turned[start + g] = move(source[base + g], amount)
+    for i in range(at.n):
+        here, side = block == i, block == (i + step) % at.n
+        for d, (g, j) in enumerate(where):
+            if i == j:
+                out[d] = move(jnp.where(here, own[g], jnp.where(side, turned[g], turned[slabs + g])), at.shift(at.q, i))
 
 
 def hour(e, c, r, idx, out, m0s, grow1, dissip, freqs, bins, nfreq, factor):
@@ -215,12 +244,17 @@
     block = at.block(shape)
     where = pieces(dirs, n)
     slabs = own.shape[0]
-    window(at, own, near, far, 0, 0, 0, ew, where, block)
+
+    def unpack(at):
+        window(at, own, near, far, 0, 0, 0, ew, where, block, et)
+        if stage == 0:
+            half = at.sub // 2
+            nback, fback = (npt - half, half) if at.even else (half, npt - half)
+            window(at, pc, near, far, slabs, 0, 0, cw, where, block, et)
+            window(at, pr, near, far, slabs, nback, fback, rw, where, block, et)
+
+    at.each(unpack)
     if stage == 0:
-        half = at.sub // 2
-        nback, fback = jnp.where(at.even, npt - half, half), jnp.where(at.even, half, npt - half)
-        window(at, pc, near, far, slabs, 0, 0, cw, where, block)
-        window(at, pr, near, far, slabs, nback, fback, rw, where, block)
         m0s[...] = jnp.zeros(shape, F32)
         for d in range(ndir):
             m0s[d : d + 1, :] = ew[d, nfreq : nfreq + 1, :]
@@ -232,13 +266,17 @@
     fb, hb, pb = hour(et, cw, rw, idx, ew, m0s, grow1, dissip, freqs, bins, nfreq, fa)
     if stage < 2:
         fields[...] = jnp.concatenate([ha, hb, pa, pb], axis=0)
-        for g in range(slabs):
-            row = None
-            for d, (slab, i) in enumerate(where):
-                if slab == g:
-                    piece = move(ew[d] * fb, at.shift(i, at.q))
-                    row = piece if row is None else jnp.where(block == i, piece, row)
-            msg[g] = row
+
+        def pack(at):
+            for g in range(slabs):
+                row = None
+                for d, (slab, i) in enumerate(where):
+                    if slab == g:
+                        piece = move(ew[d] * fb, at.shift(i, at.q))
+                        row = piece if row is None else jnp.where(block == i, piece, row)
+                msg[g] = row
+
+        at.each(pack)
     else:
         h = [o[:2] for o in old] + [ha, hb]
         p = [o[2:] for o in old] + [pa, pb]
@@ -249,18 +287,23 @@
         m0s[...] = jnp.zeros(shape, F32)
         m0s[:16, :] = every
         tail = m0s[...]
-        for d in range(1, n):
-            b = at.k ^ d
-            for g in range(backs[0].shape[0]):
-                row = None
-                for i in range(n):
-                    j = n * g + i
-                    if j > dirs:
-                        continue
-                    x = ew[dirs * b + j] * fb if j < dirs else tail
-                    piece = move(x, at.shift(i, at.q))
-                    row = piece if row is None else jnp.where(block == i, piece, row)
-                backs[d - 1][g] = row
+        k = at.k
+
+        def pack(at):
+            for d in range(1, n):
+                b = k ^ d
+                for g in range(backs[0].shape[0]):
+                    row = None
+                    for i in range(n):
+                        j = n * g + i
+                        if j > dirs:
+                            continue
+                        x = ew[dirs * b + j] * fb if j < dirs else tail
+                        piece = move(x, at.shift(i, at.q))
+                        row = piece if row is None else jnp.where(block == i, piece, row)
+                    backs[d - 1][g] = row
+
+        at.each(pack)
 
 
 def order_kernel(n, dirs, f_ref, order_ref, *rest):
@@ -328,9 +371,8 @@
     slabs = full * n + 1
     peers = range(1, n)
     swap = lambda x, d: lax.ppermute(x, "spec", [(k, k ^ d) for k in range(n)])
-    near_to = lambda x: swap(x, 1)
-    route = far_route(tiles, n)
-    far_to = lambda x: lax.ppermute(x, ("space", "spec"), route)
+    near_to = lambda x: lax.ppermute(x, ("space", "spec"), ring_route(tiles, n, False))
+    far_to = lambda x: lax.ppermute(x, ("space", "spec"), ring_route(tiles, n, True))
     wide = lambda v: jnp.pad(jnp.broadcast_to(v[:, None], (nfreq, npt)), ((0, ROWS - nfreq), (0, 0)))
     freqs, dissip = wide(frequency_table(nfreq)), wide(dissip)
     field = (ROWS, npt)

time: 60.8 us -> 58.3 us (0.959)
  Pallas kernels: 11.3 us -> 8.87 us
    pallas_call x8, Pallas kernels: 11.3 us -> 8.87 us  [call(): pl.pallas_call(kernel, out_shape=[jax.ShapeDtypeStruct(shape, dtype) for...]
    ppermute x9 -> x6, waiting for transfers between devices: 12.2 us -> 10.5 us  [on_device(): swap = lambda x, d: lax.ppermute(x, 'spec', [(k, k ^ d) for k in range(n)])]
    ppermute x3 -> x6, waiting for transfers between devices: 11.7 us -> 12.9 us  [the longest x3 11.3 us: on_device(): lax.ppermute(x, ('space', 'spec'), ring_route(tiles, n, True))]
    ppermute x3 -> x6, starting transfers between devices: 11.3 us -> 11.5 us  [the longest x3 11.4 us: on_device(): lax.ppermute(x, ('space', 'spec'), ring_route(tiles, n, True))]
    ppermute x9 -> x6, starting transfers between devices: 5.07 us -> 5.07 us  [on_device(): swap = lambda x, d: lax.ppermute(x, 'spec', [(k, k ^ d) for k in range(n)])]
  transfers between devices with their start and end apart: 15 -> 15, of which waited for: 10 -> 10; matrix products, arithmetic and copies ran while one was open for 0% -> 0% of each run, Pallas kernels for 1% -> 2%
where the time goes in v3:
time: 58.3 us; the launch traced here: 58.1 us
  waiting for transfers between devices  26.1 us (45%)
  starting transfers between devices  21.5 us (37%)
  Pallas kernels  8.87 us (15%)
  local copies, waits for them, and re-layouts  0.85 us (1%)
  between operations  0.74 us (1%)
    ppermute x3, starting transfers between devices, on_device(): lax.ppermute(x, ('space', 'spec'), ring_route(tiles, n, True))  11.4 us
    ppermute x3, waiting for transfers between devices, on_device(): lax.ppermute(x, ('space', 'spec'), ring_route(tiles, n, True))  11.3 us
    ppermute x6, waiting for transfers between devices, on_device(): swap = lambda x, d: lax.ppermute(x, 'spec', [(k, k ^ d) for k in range(n)])  10.5 us
    pallas_call x8, Pallas kernels, call(): pl.pallas_call(kernel, out_shape=[jax.ShapeDtypeStruct(shape, dtype) for...  8.87 us
    ppermute x6, starting transfers between devices, on_device(): swap = lambda x, d: lax.ppermute(x, 'spec', [(k, k ^ d) for k in range(n)])  5.07 us
    ppermute x3, starting transfers between devices, on_device(): lax.ppermute(ordered, 'space', [(t, t ^ d) for t in range(tiles)])  4.93 us
    ppermute x3, waiting for transfers between devices, on_device(): lax.ppermute(ordered, 'space', [(t, t ^ d) for t in range(tiles)])  2.72 us
    ppermute x3, waiting for transfers between devices, on_device(): lax.ppermute(x, ('space', 'spec'), ring_route(tiles, n, False))  1.65 us
  transfers between devices with their start and end apart: 15, of which 10 were waited for; matrix products, arithmetic and copies ran while one was open for 0% of the time, Pallas kernels for 2%

profile of v3, /device:TPU:0, one launch (start us, length us, event | category | flops | bytes accessed | tf_op | source)
XLA Modules:
  0.0 58.1 jit_solution(13102126058938957352)
XLA Ops:
  0.6 0.7 %copy-done.1 = s32[9,128]{1,0:T(8,128)S(1)} copy-done((s32[9,128]{1,0:T(8,128)S(1)}, s32[9,128]{1,0:T(8,128)}, u32[]{:S(2)}) %copy-start.1) | copy-done | bytes 4632
  1.3 1.8 %shard_map.86 = (f32[7,40,128]{2,1,0:T(8,128)S(1)}, f32[7,40,128]{2,1,0:T(8,128)S(1)}, f32[7,40,128]{2,1,0:T(8,128)S(1)}, f32[7,40,128]{2,1,0:T(8,128)S(1)}) custom-call(f32[9,36,128]{2,1,0:T(8,128)} %e_hbm.1, f32[9,36,128]{2,1,0:T(8,128)} %c_hbm.1, f32[9,36,128]{2,1,0:T(8,128)} %r_hbm.1, s32[9,128]{1,0:T(8,128)S(1)} %copy-done.1), custom_call_target="tpu_custom_call" | custom-call | tf_op jit(solution)/shard_map/pallas_call | solution.py:354
  3.1 0.5 collective-permute-start
  3.6 2.6 %collective-permute-start.1 = (f32[7,40,128]{2,1,0:T(8,128)S(1)}, f32[7,40,128]{2,1,0:T(8,128)S(1)}, u32[]{:S(2)}, u32[]{:S(2)}) collective-permute-start(f32[7,40,128]{2,1,0:T(8,128)S(1)} %get-tuple-element.26), channel_id=1, source_target_pairs={{0,2},{1,3},{2,0},{3,1},{4,6},{5,7},{6,4},{7,5},{8,10},{9,11},{10,... | collective-permute-start | bytes 430088 | tf_op jit(solution)/shard_map/ppermute | solution.py:373
  6.2 0.1 collective-permute-start.2
  6.3 4.5 %collective-permute-done.1.rest_2_ = f32[7,40,128]{2,1,0:T(8,128)S(1)} collective-permute-done((f32[7,40,128]{2,1,0:T(8,128)S(1)}, f32[7,40,128]{2,1,0:T(8,128)S(1)}, u32[]{:S(2)}, u32[]{:S(2)}) %collective-permute-start.1) | collective-permute-done | bytes 143392 | tf_op jit(solution)/shard_map/ppermute | solution.py:373
  10.8 2.5 %collective-permute-done.2.rest_3_ = f32[7,40,128]{2,1,0:T(8,128)S(1)} collective-permute-done((f32[7,40,128]{2,1,0:T(8,128)S(1)}, f32[7,40,128]{2,1,0:T(8,128)S(1)}, u32[]{:S(2)}, u32[]{:S(2)}) %collective-permute-start.2) | collective-permute-done | bytes 143392 | tf_op jit(solution)/shard_map/ppermute | solution.py:373
  13.4 0.2 shard_map.87
  13.6 3.8 %collective-permute-start.4 = (f32[19,40,128]{2,1,0:T(8,128)S(1)}, f32[19,40,128]{2,1,0:T(8,128)S(1)}, u32[]{:S(2)}, u32[]{:S(2)}) collective-permute-start(f32[19,40,128]{2,1,0:T(8,128)S(1)} %get-tuple-element.30), channel_id=1, source_target_pairs={{0,12},{1,2},{2,1},{3,7},{7,3},{5,4},{4,5},{6,10},{10,6},{8,9},{9,... | collective-permute-start | bytes 1167368 | tf_op jit(solution)/shard_map/ppermute | solution.py:375
  17.4 1.6 %collective-permute-done.3.refs_1_ = f32[18,40,128]{2,1,0:T(8,128)S(1)} collective-permute-done((f32[18,40,128]{2,1,0:T(8,128)S(1)}, f32[18,40,128]{2,1,0:T(8,128)S(1)}, u32[]{:S(2)}, u32[]{:S(2)}) %collective-permute-start.3) | collective-permute-done | bytes 368672 | tf_op jit(solution)/shard_map/ppermute | solution.py:374
  19.1 4.1 %collective-permute-done.4.refs_2_ = f32[19,40,128]{2,1,0:T(8,128)S(1)} collective-permute-done((f32[19,40,128]{2,1,0:T(8,128)S(1)}, f32[19,40,128]{2,1,0:T(8,128)S(1)}, u32[]{:S(2)}, u32[]{:S(2)}) %collective-permute-start.4) | collective-permute-done | bytes 389152 | tf_op jit(solution)/shard_map/ppermute | solution.py:375
  23.2 0.1 pad.14.refs_4_
  23.3 0.1 pad.12.refs_3_
  23.4 2.1 %shard_map.88 = (f32[36,40,128]{2,1,0:T(8,128)S(1)}, f32[36,40,128]{2,1,0:T(8,128)S(1)}, s32[40,128]{1,0:T(8,128)S(1)}, f32[40,128]{1,0:T(8,128)S(1)}, f32[4,128]{1,0:T(4,128)S(1)}, /*index=5*/f32[9,40,128]{2,1,0:T(8,128)S(1)}) custom-call(f32[9,40,128]{2,1,0:T(8,128)S(1)} %get-tuple-element.28.refs_0_, f32[18,40,128]{2,1,0:T(8,128)S(1)} %collective-permute-done.3.refs_1_, ...), custom_call_target="tpu_custom_call" | custom-call | tf_op jit(solution)/shard_map/pallas_call | solution.py:354
  25.5 3.8 %collective-permute-start.6 = (f32[9,40,128]{2,1,0:T(8,128)S(1)}, f32[9,40,128]{2,1,0:T(8,128)S(1)}, u32[]{:S(2)}, u32[]{:S(2)}) collective-permute-start(f32[9,40,128]{2,1,0:T(8,128)S(1)} %get-tuple-element.33.refs_0_), channel_id=1, source_target_pairs={{0,12},{1,2},{2,1},{3,7},{7,3},{5,4},{4,5},{6,10},{10,6},{8,9},{9,... | collective-permute-start | bytes 552968 | tf_op jit(solution)/shard_map/ppermute | solution.py:375
  29.3 3.6 %collective-permute-done.6.refs_2_ = f32[9,40,128]{2,1,0:T(8,128)S(1)} collective-permute-done((f32[9,40,128]{2,1,0:T(8,128)S(1)}, f32[9,40,128]{2,1,0:T(8,128)S(1)}, u32[]{:S(2)}, u32[]{:S(2)}) %collective-permute-start.6) | collective-permute-done | bytes 184352 | tf_op jit(solution)/shard_map/ppermute | solution.py:375
  32.9 1.5 %shard_map.89 = (f32[4,128]{1,0:T(4,128)S(1)}, f32[9,40,128]{2,1,0:T(8,128)S(1)}) custom-call(f32[9,40,128]{2,1,0:T(8,128)S(1)} %get-tuple-element.33.refs_0_, f32[9,40,128]{2,1,0:T(8,128)S(1)} %collective-permute-done.5.refs_1_, f32[9,40,128]{2,1,0:T(8,128)S(1)} %collective-permute-done.6.refs_2_, f32[40,128]{1,0:T(8,128)S(1)} %pad.12.refs_3_, ...), custom_call_target="tpu_custom_call" | custom-call | tf_op jit(solution)/shard_map/pallas_call | solution.py:354
  34.4 3.8 %collective-permute-start.8 = (f32[9,40,128]{2,1,0:T(8,128)S(1)}, f32[9,40,128]{2,1,0:T(8,128)S(1)}, u32[]{:S(2)}, u32[]{:S(2)}) collective-permute-start(f32[9,40,128]{2,1,0:T(8,128)S(1)} %get-tuple-element.39.refs_0_), channel_id=1, source_target_pairs={{0,12},{1,2},{2,1},{3,7},{7,3},{5,4},{4,5},{6,10},{10,6},{8,9},{9,... | collective-permute-start | bytes 552968 | tf_op jit(solution)/shard_map/ppermute | solution.py:375
  38.3 3.6 %collective-permute-done.8.refs_2_ = f32[9,40,128]{2,1,0:T(8,128)S(1)} collective-permute-done((f32[9,40,128]{2,1,0:T(8,128)S(1)}, f32[9,40,128]{2,1,0:T(8,128)S(1)}, u32[]{:S(2)}, u32[]{:S(2)}) %collective-permute-start.8) | collective-permute-done | bytes 184352 | tf_op jit(solution)/shard_map/ppermute | solution.py:375
  41.8 1.5 %shard_map.90 = (f32[16,128]{1,0:T(8,128)S(1)}, f32[9,40,128]{2,1,0:T(8,128)S(1)}, f32[3,40,128]{2,1,0:T(8,128)S(1)}, f32[3,40,128]{2,1,0:T(8,128)S(1)}, f32[3,40,128]{2,1,0:T(8,128)S(1)}) custom-call(f32[9,40,128]{2,1,0:T(8,128)S(1)} %get-tuple-element.39.refs_0_, f32[9,40,128]{2,1,0:T(8,128)S(1)} %collective-permute-done.7.refs_1_, ...), custom_call_target="tpu_custom_call" | custom-call | tf_op jit(solution)/shard_map/pallas_call | solution.py:354
  43.3 0.1 collective-permute-start.9
  43.4 0.1 collective-permute-start.10
  43.5 1.8 %collective-permute-start.11 = (f32[3,40,128]{2,1,0:T(8,128)S(1)}, f32[3,40,128]{2,1,0:T(8,128)S(1)}, u32[]{:S(2)}, u32[]{:S(2)}) collective-permute-start(f32[3,40,128]{2,1,0:T(8,128)S(1)} %get-tuple-element.44), channel_id=1, source_target_pairs={{0,3},{1,2},{2,1},{3,0},{4,7},{5,6},{6,5},{7,4},{8,11},{9,10},{10,... | collective-permute-start | bytes 184328 | tf_op jit(solution)/shard_map/ppermute | solution.py:373
  45.3 3.0 %collective-permute-done.10.rest_1_ = f32[3,40,128]{2,1,0:T(8,128)S(1)} collective-permute-done((f32[3,40,128]{2,1,0:T(8,128)S(1)}, f32[3,40,128]{2,1,0:T(8,128)S(1)}, u32[]{:S(2)}, u32[]{:S(2)}) %collective-permute-start.10) | collective-permute-done | bytes 61472 | tf_op jit(solution)/shard_map/ppermute | solution.py:373
  48.3 0.4 collective-permute-done.11.rest_2_
  48.7 0.2 shard_map.92.own_ref
  48.8 3.8 %collective-permute-start.14 = (f32[16,128]{1,0:T(8,128)S(1)}, f32[16,128]{1,0:T(8,128)S(1)}, u32[]{:S(2)}, u32[]{:S(2)}) collective-permute-start(f32[16,128]{1,0:T(8,128)S(1)} %shard_map.92.own_ref), channel_id=1, source_target_pairs={{0,12},{4,8},{8,4},{12,0},{1,13},{5,9},{9,5},{13,1},{2,14},{6,10},... | collective-permute-start | bytes 24584 | tf_op jit(solution)/shard_map/ppermute | solution.py:414
  52.6 1.1 %collective-permute-start.13 = (f32[16,128]{1,0:T(8,128)S(1)}, f32[16,128]{1,0:T(8,128)S(1)}, u32[]{:S(2)}, u32[]{:S(2)}) collective-permute-start(f32[16,128]{1,0:T(8,128)S(1)} %shard_map.92.own_ref), channel_id=1, source_target_pairs={{0,8},{4,12},{8,0},{12,4},{1,9},{5,13},{9,1},{13,5},{2,10},{6,14},... | collective-permute-start | bytes 24584 | tf_op jit(solution)/shard_map/ppermute | solution.py:414
  53.8 0.9 %shard_map.91 = f32[9,36,128]{2,1,0:T(8,128)} custom-call(f32[9,40,128]{2,1,0:T(8,128)S(1)} %get-tuple-element.41.e_ref, f32[3,40,128]{2,1,0:T(8,128)S(1)} %collective-permute-done.9.rest_0_, f32[3,40,128]{2,1,0:T(8,128)S(1)} %collective-permute-done.10.rest_1_, f32[3,40,128]{2,1,0:T(8,128)S(1)} %collective-permute-done.11.rest_2_), custom_call_target="tpu_custom_call" | custom-call | tf_op jit(solution)/shard_map/pallas_call | solution.py:354
  54.7 2.5 %collective-permute-done.13.rest_1_ = f32[16,128]{1,0:T(8,128)S(1)} collective-permute-done((f32[16,128]{1,0:T(8,128)S(1)}, f32[16,128]{1,0:T(8,128)S(1)}, u32[]{:S(2)}, u32[]{:S(2)}) %collective-permute-start.13) | collective-permute-done | bytes 8224 | tf_op jit(solution)/shard_map/ppermute | solution.py:414
  57.2 0.2 collective-permute-done.12.rest_0_
  57.4 0.7 %shard_map.93 = f32[12,128]{1,0:T(8,128)} custom-call(f32[16,128]{1,0:T(8,128)S(1)} %shard_map.92.own_ref, f32[16,128]{1,0:T(8,128)S(1)} %collective-permute-done.12.rest_0_, f32[16,128]{1,0:T(8,128)S(1)} %collective-permute-done.13.rest_1_, f32[16,128]{1,0:T(8,128)S(1)} %collective-permute-done.14.rest_2_), custom_call_target="tpu_custom_call" | custom-call | tf_op jit(solution)/shard_map/pallas_call | solution.py:354
  (19 shorter events, 0.1 us)
Async XLA Ops:
  0.6 0.7 %copy-start.1 = (s32[9,128]{1,0:T(8,128)S(1)}, s32[9,128]{1,0:T(8,128)}, u32[]{:S(2)}) copy-start(s32[9,128]{1,0:T(8,128)} %u_hbm.1) | copy-start | bytes 13828
  1.3 12.0 %copy-start = (f32[36,128]{1,0:T(8,128)S(1)}, f32[36,128]{1,0:T(8,128)}, u32[]{:S(2)}) copy-start(f32[36,128]{1,0:T(8,128)} %refs_7_.1) | copy-start | bytes 55300
  3.1 3.2 %collective-permute-start = (f32[7,40,128]{2,1,0:T(8,128)S(1)}, f32[7,40,128]{2,1,0:T(8,128)S(1)}, u32[]{:S(2)}, u32[]{:S(2)}) collective-permute-start(f32[7,40,128]{2,1,0:T(8,128)S(1)} %get-tuple-element.25), channel_id=1, source_target_pairs={{0,1},{1,0},{2,3},{3,2},{4,5},{5,4},{6,7},{7,6},{8,9},{9,8},{10,11... | collective-permute-start | bytes 430088 | tf_op jit(solution)/shard_map/ppermute | solution.py:373
  3.6 7.2 %collective-permute-start.1 = (f32[7,40,128]{2,1,0:T(8,128)S(1)}, f32[7,40,128]{2,1,0:T(8,128)S(1)}, u32[]{:S(2)}, u32[]{:S(2)}) collective-permute-start(f32[7,40,128]{2,1,0:T(8,128)S(1)} %get-tuple-element.26), channel_id=1, source_target_pairs={{0,2},{1,3},{2,0},{3,1},{4,6},{5,7},{6,4},{7,5},{8,10},{9,11},{10,... | collective-permute-start | bytes 430088 | tf_op jit(solution)/shard_map/ppermute | solution.py:373
  6.2 7.2 %collective-permute-start.2 = (f32[7,40,128]{2,1,0:T(8,128)S(1)}, f32[7,40,128]{2,1,0:T(8,128)S(1)}, u32[]{:S(2)}, u32[]{:S(2)}) collective-permute-start(f32[7,40,128]{2,1,0:T(8,128)S(1)} %get-tuple-element.27), channel_id=1, source_target_pairs={{0,3},{1,2},{2,1},{3,0},{4,7},{5,6},{6,5},{7,4},{8,11},{9,10},{10,... | collective-permute-start | bytes 430088 | tf_op jit(solution)/shard_map/ppermute | solution.py:373
  13.6 3.8 %copy-start.3 = (f32[36]{0:T(128)S(1)}, f32[36]{0:T(128)}, u32[]{:S(2)}) copy-start(f32[36]{0:T(128)} %param.11) | copy-start | bytes 436
  13.6 9.6 %collective-permute-start.4 = (f32[19,40,128]{2,1,0:T(8,128)S(1)}, f32[19,40,128]{2,1,0:T(8,128)S(1)}, u32[]{:S(2)}, u32[]{:S(2)}) collective-permute-start(f32[19,40,128]{2,1,0:T(8,128)S(1)} %get-tuple-element.30), channel_id=1, source_target_pairs={{0,12},{1,2},{2,1},{3,7},{7,3},{5,4},{4,5},{6,10},{10,6},{8,9},{9,... | collective-permute-start | bytes 1167368 | tf_op jit(solution)/shard_map/ppermute | solution.py:375
  17.4 1.7 %collective-permute-start.3 = (f32[18,40,128]{2,1,0:T(8,128)S(1)}, f32[18,40,128]{2,1,0:T(8,128)S(1)}, u32[]{:S(2)}, u32[]{:S(2)}) collective-permute-start(f32[18,40,128]{2,1,0:T(8,128)S(1)} %get-tuple-element.29), channel_id=1, source_target_pairs={{0,1},{1,0},{2,3},{3,2},{7,5},{5,7},{4,6},{6,4},{10,8},{8,10},{9,1... | collective-permute-start | bytes 1105928 | tf_op jit(solution)/shard_map/ppermute | solution.py:374
  25.5 7.4 %collective-permute-start.6 = (f32[9,40,128]{2,1,0:T(8,128)S(1)}, f32[9,40,128]{2,1,0:T(8,128)S(1)}, u32[]{:S(2)}, u32[]{:S(2)}) collective-permute-start(f32[9,40,128]{2,1,0:T(8,128)S(1)} %get-tuple-element.33.refs_0_), channel_id=1, source_target_pairs={{0,12},{1,2},{2,1},{3,7},{7,3},{5,4},{4,5},{6,10},{10,6},{8,9},{9,... | collective-permute-start | bytes 552968 | tf_op jit(solution)/shard_map/ppermute | solution.py:375
  29.3 3.6 %collective-permute-start.5 = (f32[9,40,128]{2,1,0:T(8,128)S(1)}, f32[9,40,128]{2,1,0:T(8,128)S(1)}, u32[]{:S(2)}, u32[]{:S(2)}) collective-permute-start(f32[9,40,128]{2,1,0:T(8,128)S(1)} %get-tuple-element.33.refs_0_), channel_id=1, source_target_pairs={{0,1},{1,0},{2,3},{3,2},{7,5},{5,7},{4,6},{6,4},{10,8},{8,10},{9,1... | collective-permute-start | bytes 552968 | tf_op jit(solution)/shard_map/ppermute | solution.py:374
  34.4 7.4 %collective-permute-start.8 = (f32[9,40,128]{2,1,0:T(8,128)S(1)}, f32[9,40,128]{2,1,0:T(8,128)S(1)}, u32[]{:S(2)}, u32[]{:S(2)}) collective-permute-start(f32[9,40,128]{2,1,0:T(8,128)S(1)} %get-tuple-element.39.refs_0_), channel_id=1, source_target_pairs={{0,12},{1,2},{2,1},{3,7},{7,3},{5,4},{4,5},{6,10},{10,6},{8,9},{9,... | collective-permute-start | bytes 552968 | tf_op jit(solution)/shard_map/ppermute | solution.py:375
  38.3 3.6 %collective-permute-start.7 = (f32[9,40,128]{2,1,0:T(8,128)S(1)}, f32[9,40,128]{2,1,0:T(8,128)S(1)}, u32[]{:S(2)}, u32[]{:S(2)}) collective-permute-start(f32[9,40,128]{2,1,0:T(8,128)S(1)} %get-tuple-element.39.refs_0_), channel_id=1, source_target_pairs={{0,1},{1,0},{2,3},{3,2},{7,5},{5,7},{4,6},{6,4},{10,8},{8,10},{9,1... | collective-permute-start | bytes 552968 | tf_op jit(solution)/shard_map/ppermute | solution.py:374
  43.3 1.9 %collective-permute-start.9 = (f32[3,40,128]{2,1,0:T(8,128)S(1)}, f32[3,40,128]{2,1,0:T(8,128)S(1)}, u32[]{:S(2)}, u32[]{:S(2)}) collective-permute-start(f32[3,40,128]{2,1,0:T(8,128)S(1)} %get-tuple-element.42), channel_id=1, source_target_pairs={{0,1},{1,0},{2,3},{3,2},{4,5},{5,4},{6,7},{7,6},{8,9},{9,8},{10,11... | collective-permute-start | bytes 184328 | tf_op jit(solution)/shard_map/ppermute | solution.py:373
  43.4 4.9 %collective-permute-start.10 = (f32[3,40,128]{2,1,0:T(8,128)S(1)}, f32[3,40,128]{2,1,0:T(8,128)S(1)}, u32[]{:S(2)}, u32[]{:S(2)}) collective-permute-start(f32[3,40,128]{2,1,0:T(8,128)S(1)} %get-tuple-element.43), channel_id=1, source_target_pairs={{0,2},{1,3},{2,0},{3,1},{4,6},{5,7},{6,4},{7,5},{8,10},{9,11},{10,... | collective-permute-start | bytes 184328 | tf_op jit(solution)/shard_map/ppermute | solution.py:373
  43.5 5.2 %copy-start.2 = (s32[128]{0:T(128)S(1)}, s32[128]{0:T(128)}, u32[]{:S(2)}) copy-start(s32[128]{0:T(128)} %order_ref.1) | copy-start | bytes 1540
  43.5 5.2 %collective-permute-start.11 = (f32[3,40,128]{2,1,0:T(8,128)S(1)}, f32[3,40,128]{2,1,0:T(8,128)S(1)}, u32[]{:S(2)}, u32[]{:S(2)}) collective-permute-start(f32[3,40,128]{2,1,0:T(8,128)S(1)} %get-tuple-element.44), channel_id=1, source_target_pairs={{0,3},{1,2},{2,1},{3,0},{4,7},{5,6},{6,5},{7,4},{8,11},{9,10},{10,... | collective-permute-start | bytes 184328 | tf_op jit(solution)/shard_map/ppermute | solution.py:373
  48.8 5.8 %collective-permute-start.14 = (f32[16,128]{1,0:T(8,128)S(1)}, f32[16,128]{1,0:T(8,128)S(1)}, u32[]{:S(2)}, u32[]{:S(2)}) collective-permute-start(f32[16,128]{1,0:T(8,128)S(1)} %shard_map.92.own_ref), channel_id=1, source_target_pairs={{0,12},{4,8},{8,4},{12,0},{1,13},{5,9},{9,5},{13,1},{2,14},{6,10},... | collective-permute-start | bytes 24584 | tf_op jit(solution)/shard_map/ppermute | solution.py:414
  52.6 4.5 %collective-permute-start.13 = (f32[16,128]{1,0:T(8,128)S(1)}, f32[16,128]{1,0:T(8,128)S(1)}, u32[]{:S(2)}, u32[]{:S(2)}) collective-permute-start(f32[16,128]{1,0:T(8,128)S(1)} %shard_map.92.own_ref), channel_id=1, source_target_pairs={{0,8},{4,12},{8,0},{12,4},{1,9},{5,13},{9,1},{13,5},{2,10},{6,14},... | collective-permute-start | bytes 24584 | tf_op jit(solution)/shard_map/ppermute | solution.py:414
  53.7 3.7 %collective-permute-start.12 = (f32[16,128]{1,0:T(8,128)S(1)}, f32[16,128]{1,0:T(8,128)S(1)}, u32[]{:S(2)}, u32[]{:S(2)}) collective-permute-start(f32[16,128]{1,0:T(8,128)S(1)} %shard_map.92.own_ref), channel_id=1, source_target_pairs={{0,4},{4,0},{8,12},{12,8},{1,5},{5,1},{9,13},{13,9},{2,6},{6,2},{1... | collective-permute-start | bytes 24584 | tf_op jit(solution)/shard_map/ppermute | solution.py:414

commit v4 on v3

--- a/solution.py
+++ b/solution.py
@@ -93,40 +93,54 @@
     return where
 
 
-def pack_kernel(n, total, reach, e_hbm, c_hbm, r_hbm, u_hbm, *rest):
-    outs, (e_ref, c_ref, r_ref, u_ref, v, sem) = rest[:n], rest[n:]
+def pack_kernel(n, e_hbm, c_hbm, r_hbm, *rest):
+    outs, (e_ref, c_ref, r_ref, sem) = rest[:n], rest[n:]
     dirs, nfreq, npt = e_ref.shape
     copies = [
         pltpu.make_async_copy(x, y, sem.at[i])
-        for i, (x, y) in enumerate(((e_hbm, e_ref), (c_hbm, c_ref), (r_hbm, r_ref), (u_hbm, u_ref)))
+        for i, (x, y) in enumerate(((e_hbm, e_ref), (c_hbm, c_ref), (r_hbm, r_ref)))
     ]
     for copy in copies:
         copy.start()
     for copy in copies:
         copy.wait()
     at = Spot(n, npt)
-    off = offsets(u_ref[...], at.s, npt, total, reach)
-    for a, ref in enumerate((e_ref, c_ref, r_ref)):
-        for j in range(dirs):
-            v[a * dirs + j, :nfreq, :] = ref[j]
-            v[a * dirs + j, nfreq:, :] = jnp.broadcast_to(off[j : j + 1], (ROWS - nfreq, npt))
-    block = at.block((ROWS, npt))
+    block = at.block((nfreq, npt))
     full = (dirs - 1) // n
     last = [(at.k + a) % n for a in range(3)]
     for d in range(n):
         to = subtile_of(at.s, at.k ^ d, n)
-        for a in range(3):
+        for a, ref in enumerate((e_ref, c_ref, r_ref)):
             for h in range(full):
                 row = None
                 for i in range(n):
-                    piece = move(v[a * dirs + n * h + i], at.shift(i, to))
+                    piece = move(ref[n * h + i], at.shift(i, to))
                     row = piece if row is None else jnp.where(block == i, piece, row)
-                outs[d][full * a + h] = row
+                outs[d][full * a + h, :nfreq, :] = row
         row = None
-        for a in range(3):
-            piece = move(v[(a + 1) * dirs - 1], at.shift(last[a], to))
+        for a, ref in enumerate((e_ref, c_ref, r_ref)):
+            piece = move(ref[dirs - 1], at.shift(last[a], to))
             row = piece if row is None else jnp.where(block == last[a], piece, row)
-        outs[d][3 * full] = row
+        outs[d][3 * full, :nfreq, :] = row
+
+
+def offset_kernel(n, nfreq, total, reach, u_ref, *refs):
+    outs = refs[n:]
+    dirs, npt = u_ref.shape
+    at = Spot(n, npt)
+    off = offsets(u_ref[...], at.s, npt, total, reach)
+    block = at.block((1, npt))
+    full = (dirs - 1) // n
+    for d in range(n):
+        to = subtile_of(at.s, at.k ^ d, n)
+        turned = [move(off, at.shift(i, to)) for i in range(n)]
+        for h in range(full):
+            row = turned[0][n * h : n * h + 1]
+            for i in range(1, n):
+                row = jnp.where(block == i, turned[i][n * h + i : n * h + i + 1], row)
+            outs[d][h, nfreq : nfreq + 1, :] = row
+        row = move(off, at.shift(at.k, to))[dirs - 1 : dirs]
+        outs[d][3 * full, nfreq : nfreq + 1, :] = row
 
 
 def spread_kernel(n, g_ref, *rest):
@@ -222,7 +236,7 @@
 def phase_kernel(n, stage, bins, nfreq, fields_before, *refs):
     refs = list(refs)
     take = lambda count: [refs.pop(0) for _ in range(count)]
-    own, near, far, dissip_ref, freqs_ref = take(5)
+    own, near, far, table_ref = take(4)
     if stage == 0:
         pc, pr, g_ref = take(3)
     else:
@@ -261,7 +275,7 @@
         idx[...] = (lanes(shape) + m0s[...].astype(jnp.int32)) & (npt - 1)
         gw[:nfreq, :] = 1.0 + jnp.where(block[:nfreq] == at.qf, far[2 * slabs, :nfreq, :], g_ref[...])
         gw[nfreq:, :] = jnp.ones((rows - nfreq, npt), F32)
-    grow1, dissip, freqs = gw[...], dissip_ref[...], freqs_ref[...]
+    grow1, dissip, freqs = gw[...], table_ref[0], table_ref[1]
     fa, ha, pa = hour(ew, cw, rw, idx, et, m0s, grow1, dissip, freqs, bins, nfreq, None)
     fb, hb, pb = hour(et, cw, rw, idx, ew, m0s, grow1, dissip, freqs, bins, nfreq, fa)
     if stage < 2:
@@ -349,7 +363,7 @@
     out[...] = x[:rows]
 
 
-def call(kernel, outs, scratch, *args, hbm=0):
+def call(kernel, outs, scratch, *args, hbm=0, alias=None):
     vm = pl.BlockSpec(memory_space=pltpu.VMEM)
     return pl.pallas_call(
         kernel,
@@ -357,6 +371,7 @@
         in_specs=[pl.BlockSpec(memory_space=pltpu.HBM)] * hbm + [vm] * (len(args) - hbm),
         out_specs=[vm] * len(outs),
         scratch_shapes=scratch,
+        input_output_aliases=alias or {},
         compiler_params=pltpu.CompilerParams(vmem_limit_bytes=(54600 if hbm else 40960) * 1024),
     )(*args)
 
@@ -373,17 +388,23 @@
     swap = lambda x, d: lax.ppermute(x, "spec", [(k, k ^ d) for k in range(n)])
     near_to = lambda x: lax.ppermute(x, ("space", "spec"), ring_route(tiles, n, False))
     far_to = lambda x: lax.ppermute(x, ("space", "spec"), ring_route(tiles, n, True))
-    wide = lambda v: jnp.pad(jnp.broadcast_to(v[:, None], (nfreq, npt)), ((0, ROWS - nfreq), (0, 0)))
-    freqs, dissip = wide(frequency_table(nfreq)), wide(dissip)
+    table = jnp.stack([dissip, frequency_table(nfreq)])
+    table = jnp.broadcast_to(jnp.pad(table, ((0, 0), (0, ROWS - nfreq)))[:, :, None], (2, ROWS, npt))
     field = (ROWS, npt)
     state, packed = ((ndir, *field), F32), ((slabs, *field), F32)
 
     part = pltpu.VMEM(spectrum.shape, F32)
     sent = call(
-        functools.partial(pack_kernel, n, total, reach),
+        functools.partial(pack_kernel, n),
         [((3 * full + 1, *field), F32)] * n,
-        [part, part, part, pltpu.VMEM(upwind.shape, jnp.int32), pltpu.VMEM((3 * dirs, *field), F32), pltpu.SemaphoreType.DMA((4,))],
-        spectrum, courant, refraction, upwind, hbm=4,
+        [part, part, part, pltpu.SemaphoreType.DMA((3,))],
+        spectrum, courant, refraction, hbm=3,
+    )
+    sent = call(
+        functools.partial(offset_kernel, n, nfreq, total, reach),
+        [((3 * full + 1, *field), F32)] * n,
+        [],
+        upwind, *sent, alias={1 + d: d for d in range(n)},
     )
     got = [sent[0]] + [swap(sent[d], d) for d in peers]
     e, c, r, near, far = call(
@@ -399,13 +420,13 @@
     some = ((4, npt), F32)
     c, r, idx, gw, f0, e = phase(
         0, 0, [state, state, (field, jnp.int32), (field, F32), some, packed],
-        e, near_to(near), far_to(far), dissip, freqs, c, r, growth,
-    )
-    f1, e = phase(1, 1, [some, packed], e, near_to(e), far_to(e), dissip, freqs, c, r, idx, gw, f0)
+        e, near_to(near), far_to(far), table, c, r, growth,
+    )
+    f1, e = phase(1, 1, [some, packed], e, near_to(e), far_to(e), table, c, r, idx, gw, f0)
     back = ((-(-(dirs + 1) // n), *field), F32)
     fields, own, *backs = phase(
         2, 2, [((16, npt), F32), ((dirs, *field), F32)] + [back] * (n - 1),
-        e, near_to(e), far_to(e), dissip, freqs, c, r, idx, gw, f0, f1,
+        e, near_to(e), far_to(e), table, c, r, idx, gw, f0, f1,
     )
     backs = [swap(x, d) for d, x in zip(peers, backs)]
     (ordered,) = call(functools.partial(order_kernel, n, dirs), [((16, npt), F32)], [], fields, send_order, *backs)

time: 58.3 us -> 57.6 us (0.988)
  waiting for transfers between devices: 26.1 us -> 25.5 us
    ppermute x3, waiting for transfers between devices: 1.65 us -> 1.01 us  [on_device(): lax.ppermute(x, ('space', 'spec'), ring_route(tiles, n, False))]
    pallas_call x8 -> x9, Pallas kernels: 8.87 us -> 9.01 us  [call(): pl.pallas_call(kernel, out_shape=[jax.ShapeDtypeStruct(shape, dtype) for...]
where the time goes in v4:
time: 57.6 us; the launch traced here: 57.5 us
  waiting for transfers between devices  25.5 us (44%)
  starting transfers between devices  21.4 us (37%)
  Pallas kernels  9.01 us (16%)
  local copies, waits for them, and re-layouts  0.74 us (1%)
  between operations  0.74 us (1%)
    ppermute x3, starting transfers between devices, on_device(): lax.ppermute(x, ('space', 'spec'), ring_route(tiles, n, True))  11.4 us
    ppermute x3, waiting for transfers between devices, on_device(): lax.ppermute(x, ('space', 'spec'), ring_route(tiles, n, True))  11.3 us
    ppermute x6, waiting for transfers between devices, on_device(): swap = lambda x, d: lax.ppermute(x, 'spec', [(k, k ^ d) for k in range(n)])  10.5 us
    pallas_call x9, Pallas kernels, call(): pl.pallas_call(kernel, out_shape=[jax.ShapeDtypeStruct(shape, dtype) for...  9.01 us
    ppermute x6, starting transfers between devices, on_device(): swap = lambda x, d: lax.ppermute(x, 'spec', [(k, k ^ d) for k in range(n)])  5.06 us
    ppermute x3, starting transfers between devices, on_device(): lax.ppermute(ordered, 'space', [(t, t ^ d) for t in range(tiles)])  4.93 us
    ppermute x3, waiting for transfers between devices, on_device(): lax.ppermute(ordered, 'space', [(t, t ^ d) for t in range(tiles)])  2.73 us
  transfers between devices with their start and end apart: 15, of which 10 were waited for; matrix products, arithmetic and copies ran while one was open for 0% of the time, Pallas kernels for 2%

profile of v4, /device:TPU:0, one launch (start us, length us, event | category | flops | bytes accessed | tf_op | source)
XLA Modules:
  0.0 57.5 jit_solution(13899787969850479746)
XLA Ops:
  0.6 1.8 %shard_map.86 = (f32[7,40,128]{2,1,0:T(8,128)S(1)}, f32[7,40,128]{2,1,0:T(8,128)S(1)}, f32[7,40,128]{2,1,0:T(8,128)S(1)}, f32[7,40,128]{2,1,0:T(8,128)S(1)}) custom-call(f32[9,36,128]{2,1,0:T(8,128)} %e_hbm.1, f32[9,36,128]{2,1,0:T(8,128)} %c_hbm.1, f32[9,36,128]{2,1,0:T(8,128)} %r_hbm.1), custom_call_target="tpu_custom_call" | custom-call | tf_op jit(solution)/shard_map/pallas_call | solution.py:368
  2.4 0.2 shard_map.87
  2.6 0.5 collective-permute-start
  3.1 2.6 %collective-permute-start.1 = (f32[7,40,128]{2,1,0:T(8,128)S(1)}, f32[7,40,128]{2,1,0:T(8,128)S(1)}, u32[]{:S(2)}, u32[]{:S(2)}) collective-permute-start(f32[7,40,128]{2,1,0:T(8,128)S(1)} %get-tuple-element.34), channel_id=1, source_target_pairs={{0,2},{1,3},{2,0},{3,1},{4,6},{5,7},{6,4},{7,5},{8,10},{9,11},{10,... | collective-permute-start | bytes 430088 | tf_op jit(solution)/shard_map/ppermute | solution.py:388
  5.7 0.1 collective-permute-start.2
  5.7 4.5 %collective-permute-done.1.rest_2_ = f32[7,40,128]{2,1,0:T(8,128)S(1)} collective-permute-done((f32[7,40,128]{2,1,0:T(8,128)S(1)}, f32[7,40,128]{2,1,0:T(8,128)S(1)}, u32[]{:S(2)}, u32[]{:S(2)}) %collective-permute-start.1) | collective-permute-done | bytes 143392 | tf_op jit(solution)/shard_map/ppermute | solution.py:388
  10.3 2.5 %collective-permute-done.2.rest_3_ = f32[7,40,128]{2,1,0:T(8,128)S(1)} collective-permute-done((f32[7,40,128]{2,1,0:T(8,128)S(1)}, f32[7,40,128]{2,1,0:T(8,128)S(1)}, u32[]{:S(2)}, u32[]{:S(2)}) %collective-permute-start.2) | collective-permute-done | bytes 143392 | tf_op jit(solution)/shard_map/ppermute | solution.py:388
  12.8 0.2 shard_map.88
  13.1 3.8 %collective-permute-start.4 = (f32[19,40,128]{2,1,0:T(8,128)S(1)}, f32[19,40,128]{2,1,0:T(8,128)S(1)}, u32[]{:S(2)}, u32[]{:S(2)}) collective-permute-start(f32[19,40,128]{2,1,0:T(8,128)S(1)} %get-tuple-element.38), channel_id=1, source_target_pairs={{0,12},{1,2},{2,1},{3,7},{7,3},{5,4},{4,5},{6,10},{10,6},{8,9},{9,... | collective-permute-start | bytes 1167368 | tf_op jit(solution)/shard_map/ppermute | solution.py:390
  16.9 0.7 %copy-done.3 = f32[36]{0:T(128)S(1)} copy-done((f32[36]{0:T(128)S(1)}, f32[36]{0:T(128)}, u32[]{:S(2)}) %copy-start.3) | copy-done | bytes 168
  17.5 1.0 %collective-permute-done.3.refs_1_ = f32[18,40,128]{2,1,0:T(8,128)S(1)} collective-permute-done((f32[18,40,128]{2,1,0:T(8,128)S(1)}, f32[18,40,128]{2,1,0:T(8,128)S(1)}, u32[]{:S(2)}, u32[]{:S(2)}) %collective-permute-start.3) | collective-permute-done | bytes 368672 | tf_op jit(solution)/shard_map/ppermute | solution.py:389
  18.5 4.1 %collective-permute-done.4.refs_2_ = f32[19,40,128]{2,1,0:T(8,128)S(1)} collective-permute-done((f32[19,40,128]{2,1,0:T(8,128)S(1)}, f32[19,40,128]{2,1,0:T(8,128)S(1)}, u32[]{:S(2)}, u32[]{:S(2)}) %collective-permute-start.4) | collective-permute-done | bytes 389152 | tf_op jit(solution)/shard_map/ppermute | solution.py:390
  22.7 0.1 broadcast_in_dim.2.refs_3_
  22.7 2.1 %shard_map.89 = (f32[36,40,128]{2,1,0:T(8,128)S(1)}, f32[36,40,128]{2,1,0:T(8,128)S(1)}, s32[40,128]{1,0:T(8,128)S(1)}, f32[40,128]{1,0:T(8,128)S(1)}, f32[4,128]{1,0:T(4,128)S(1)}, /*index=5*/f32[9,40,128]{2,1,0:T(8,128)S(1)}) custom-call(f32[9,40,128]{2,1,0:T(8,128)S(1)} %get-tuple-element.36.refs_0_, f32[18,40,128]{2,1,0:T(8,128)S(1)} %collective-permute-done.3.refs_1_, ...), custom_call_target="tpu_custom_call" | custom-call | tf_op jit(solution)/shard_map/pallas_call | solution.py:368
  24.9 3.8 %collective-permute-start.6 = (f32[9,40,128]{2,1,0:T(8,128)S(1)}, f32[9,40,128]{2,1,0:T(8,128)S(1)}, u32[]{:S(2)}, u32[]{:S(2)}) collective-permute-start(f32[9,40,128]{2,1,0:T(8,128)S(1)} %get-tuple-element.41.refs_0_), channel_id=1, source_target_pairs={{0,12},{1,2},{2,1},{3,7},{7,3},{5,4},{4,5},{6,10},{10,6},{8,9},{9,... | collective-permute-start | bytes 552968 | tf_op jit(solution)/shard_map/ppermute | solution.py:390
  28.7 3.6 %collective-permute-done.6.refs_2_ = f32[9,40,128]{2,1,0:T(8,128)S(1)} collective-permute-done((f32[9,40,128]{2,1,0:T(8,128)S(1)}, f32[9,40,128]{2,1,0:T(8,128)S(1)}, u32[]{:S(2)}, u32[]{:S(2)}) %collective-permute-start.6) | collective-permute-done | bytes 184352 | tf_op jit(solution)/shard_map/ppermute | solution.py:390
  32.3 1.5 %shard_map.90 = (f32[4,128]{1,0:T(4,128)S(1)}, f32[9,40,128]{2,1,0:T(8,128)S(1)}) custom-call(f32[9,40,128]{2,1,0:T(8,128)S(1)} %get-tuple-element.41.refs_0_, f32[9,40,128]{2,1,0:T(8,128)S(1)} %collective-permute-done.5.refs_1_, f32[9,40,128]{2,1,0:T(8,128)S(1)} %collective-permute-done.6.refs_2_, f32[2,40,128]{2,1,0:T(8,128)S(1)} %broadcast_in_dim.2.refs_3_, ...), custom_call_target="tpu_custom_call" | custom-call | tf_op jit(solution)/shard_map/pallas_call | solution.py:368
  33.8 3.8 %collective-permute-start.8 = (f32[9,40,128]{2,1,0:T(8,128)S(1)}, f32[9,40,128]{2,1,0:T(8,128)S(1)}, u32[]{:S(2)}, u32[]{:S(2)}) collective-permute-start(f32[9,40,128]{2,1,0:T(8,128)S(1)} %get-tuple-element.47.refs_0_), channel_id=1, source_target_pairs={{0,12},{1,2},{2,1},{3,7},{7,3},{5,4},{4,5},{6,10},{10,6},{8,9},{9,... | collective-permute-start | bytes 552968 | tf_op jit(solution)/shard_map/ppermute | solution.py:390
  37.7 3.6 %collective-permute-done.8.refs_2_ = f32[9,40,128]{2,1,0:T(8,128)S(1)} collective-permute-done((f32[9,40,128]{2,1,0:T(8,128)S(1)}, f32[9,40,128]{2,1,0:T(8,128)S(1)}, u32[]{:S(2)}, u32[]{:S(2)}) %collective-permute-start.8) | collective-permute-done | bytes 184352 | tf_op jit(solution)/shard_map/ppermute | solution.py:390
  41.2 1.5 %shard_map.91 = (f32[16,128]{1,0:T(8,128)S(1)}, f32[9,40,128]{2,1,0:T(8,128)S(1)}, f32[3,40,128]{2,1,0:T(8,128)S(1)}, f32[3,40,128]{2,1,0:T(8,128)S(1)}, f32[3,40,128]{2,1,0:T(8,128)S(1)}) custom-call(f32[9,40,128]{2,1,0:T(8,128)S(1)} %get-tuple-element.47.refs_0_, f32[9,40,128]{2,1,0:T(8,128)S(1)} %collective-permute-done.7.refs_1_, ...), custom_call_target="tpu_custom_call" | custom-call | tf_op jit(solution)/shard_map/pallas_call | solution.py:368
  42.7 0.1 collective-permute-start.9
  42.8 0.1 collective-permute-start.10
  42.9 1.8 %collective-permute-start.11 = (f32[3,40,128]{2,1,0:T(8,128)S(1)}, f32[3,40,128]{2,1,0:T(8,128)S(1)}, u32[]{:S(2)}, u32[]{:S(2)}) collective-permute-start(f32[3,40,128]{2,1,0:T(8,128)S(1)} %get-tuple-element.52), channel_id=1, source_target_pairs={{0,3},{1,2},{2,1},{3,0},{4,7},{5,6},{6,5},{7,4},{8,11},{9,10},{10,... | collective-permute-start | bytes 184328 | tf_op jit(solution)/shard_map/ppermute | solution.py:388
  44.6 3.0 %collective-permute-done.10.rest_1_ = f32[3,40,128]{2,1,0:T(8,128)S(1)} collective-permute-done((f32[3,40,128]{2,1,0:T(8,128)S(1)}, f32[3,40,128]{2,1,0:T(8,128)S(1)}, u32[]{:S(2)}, u32[]{:S(2)}) %collective-permute-start.10) | collective-permute-done | bytes 61472 | tf_op jit(solution)/shard_map/ppermute | solution.py:388
  47.6 0.4 collective-permute-done.11.rest_2_
  48.1 0.2 shard_map.93.own_ref
  48.2 3.8 %collective-permute-start.14 = (f32[16,128]{1,0:T(8,128)S(1)}, f32[16,128]{1,0:T(8,128)S(1)}, u32[]{:S(2)}, u32[]{:S(2)}) collective-permute-start(f32[16,128]{1,0:T(8,128)S(1)} %shard_map.93.own_ref), channel_id=1, source_target_pairs={{0,12},{4,8},{8,4},{12,0},{1,13},{5,9},{9,5},{13,1},{2,14},{6,10},... | collective-permute-start | bytes 24584 | tf_op jit(solution)/shard_map/ppermute | solution.py:435
  52.0 1.1 %collective-permute-start.13 = (f32[16,128]{1,0:T(8,128)S(1)}, f32[16,128]{1,0:T(8,128)S(1)}, u32[]{:S(2)}, u32[]{:S(2)}) collective-permute-start(f32[16,128]{1,0:T(8,128)S(1)} %shard_map.93.own_ref), channel_id=1, source_target_pairs={{0,8},{4,12},{8,0},{12,4},{1,9},{5,13},{9,1},{13,5},{2,10},{6,14},... | collective-permute-start | bytes 24584 | tf_op jit(solution)/shard_map/ppermute | solution.py:435
  53.1 0.9 %shard_map.92 = f32[9,36,128]{2,1,0:T(8,128)} custom-call(f32[9,40,128]{2,1,0:T(8,128)S(1)} %get-tuple-element.49.e_ref, f32[3,40,128]{2,1,0:T(8,128)S(1)} %collective-permute-done.9.rest_0_, f32[3,40,128]{2,1,0:T(8,128)S(1)} %collective-permute-done.10.rest_1_, f32[3,40,128]{2,1,0:T(8,128)S(1)} %collective-permute-done.11.rest_2_), custom_call_target="tpu_custom_call" | custom-call | tf_op jit(solution)/shard_map/pallas_call | solution.py:368
  54.0 2.5 %collective-permute-done.13.rest_1_ = f32[16,128]{1,0:T(8,128)S(1)} collective-permute-done((f32[16,128]{1,0:T(8,128)S(1)}, f32[16,128]{1,0:T(8,128)S(1)}, u32[]{:S(2)}, u32[]{:S(2)}) %collective-permute-start.13) | collective-permute-done | bytes 8224 | tf_op jit(solution)/shard_map/ppermute | solution.py:435
  56.6 0.2 collective-permute-done.12.rest_0_
  56.8 0.7 %shard_map.94 = f32[12,128]{1,0:T(8,128)} custom-call(f32[16,128]{1,0:T(8,128)S(1)} %shard_map.93.own_ref, f32[16,128]{1,0:T(8,128)S(1)} %collective-permute-done.12.rest_0_, f32[16,128]{1,0:T(8,128)S(1)} %collective-permute-done.13.rest_1_, f32[16,128]{1,0:T(8,128)S(1)} %collective-permute-done.14.rest_2_), custom_call_target="tpu_custom_call" | custom-call | tf_op jit(solution)/shard_map/pallas_call | solution.py:368
  (18 shorter events, 0.1 us)
Async XLA Ops:
  0.6 1.8 %copy-start.1 = (s32[9,128]{1,0:T(8,128)S(1)}, s32[9,128]{1,0:T(8,128)}, u32[]{:S(2)}) copy-start(s32[9,128]{1,0:T(8,128)} %u_ref.1) | copy-start | bytes 13828
  2.4 10.4 %copy-start = (f32[36,128]{1,0:T(8,128)S(1)}, f32[36,128]{1,0:T(8,128)}, u32[]{:S(2)}) copy-start(f32[36,128]{1,0:T(8,128)} %refs_6_.1) | copy-start | bytes 55300
  2.6 3.1 %collective-permute-start = (f32[7,40,128]{2,1,0:T(8,128)S(1)}, f32[7,40,128]{2,1,0:T(8,128)S(1)}, u32[]{:S(2)}, u32[]{:S(2)}) collective-permute-start(f32[7,40,128]{2,1,0:T(8,128)S(1)} %get-tuple-element.33), channel_id=1, source_target_pairs={{0,1},{1,0},{2,3},{3,2},{4,5},{5,4},{6,7},{7,6},{8,9},{9,8},{10,11... | collective-permute-start | bytes 430088 | tf_op jit(solution)/shard_map/ppermute | solution.py:388
  3.1 7.2 %collective-permute-start.1 = (f32[7,40,128]{2,1,0:T(8,128)S(1)}, f32[7,40,128]{2,1,0:T(8,128)S(1)}, u32[]{:S(2)}, u32[]{:S(2)}) collective-permute-start(f32[7,40,128]{2,1,0:T(8,128)S(1)} %get-tuple-element.34), channel_id=1, source_target_pairs={{0,2},{1,3},{2,0},{3,1},{4,6},{5,7},{6,4},{7,5},{8,10},{9,11},{10,... | collective-permute-start | bytes 430088 | tf_op jit(solution)/shard_map/ppermute | solution.py:388
  5.7 7.2 %collective-permute-start.2 = (f32[7,40,128]{2,1,0:T(8,128)S(1)}, f32[7,40,128]{2,1,0:T(8,128)S(1)}, u32[]{:S(2)}, u32[]{:S(2)}) collective-permute-start(f32[7,40,128]{2,1,0:T(8,128)S(1)} %get-tuple-element.35), channel_id=1, source_target_pairs={{0,3},{1,2},{2,1},{3,0},{4,7},{5,6},{6,5},{7,4},{8,11},{9,10},{10,... | collective-permute-start | bytes 430088 | tf_op jit(solution)/shard_map/ppermute | solution.py:388
  13.1 9.6 %collective-permute-start.4 = (f32[19,40,128]{2,1,0:T(8,128)S(1)}, f32[19,40,128]{2,1,0:T(8,128)S(1)}, u32[]{:S(2)}, u32[]{:S(2)}) collective-permute-start(f32[19,40,128]{2,1,0:T(8,128)S(1)} %get-tuple-element.38), channel_id=1, source_target_pairs={{0,12},{1,2},{2,1},{3,7},{7,3},{5,4},{4,5},{6,10},{10,6},{8,9},{9,... | collective-permute-start | bytes 1167368 | tf_op jit(solution)/shard_map/ppermute | solution.py:390
  16.9 1.7 %collective-permute-start.3 = (f32[18,40,128]{2,1,0:T(8,128)S(1)}, f32[18,40,128]{2,1,0:T(8,128)S(1)}, u32[]{:S(2)}, u32[]{:S(2)}) collective-permute-start(f32[18,40,128]{2,1,0:T(8,128)S(1)} %get-tuple-element.37), channel_id=1, source_target_pairs={{0,1},{1,0},{2,3},{3,2},{7,5},{5,7},{4,6},{6,4},{10,8},{8,10},{9,1... | collective-permute-start | bytes 1105928 | tf_op jit(solution)/shard_map/ppermute | solution.py:389
  16.9 0.7 %copy-start.3 = (f32[36]{0:T(128)S(1)}, f32[36]{0:T(128)}, u32[]{:S(2)}) copy-start(f32[36]{0:T(128)} %param.11) | copy-start | bytes 436
  24.9 7.4 %collective-permute-start.6 = (f32[9,40,128]{2,1,0:T(8,128)S(1)}, f32[9,40,128]{2,1,0:T(8,128)S(1)}, u32[]{:S(2)}, u32[]{:S(2)}) collective-permute-start(f32[9,40,128]{2,1,0:T(8,128)S(1)} %get-tuple-element.41.refs_0_), channel_id=1, source_target_pairs={{0,12},{1,2},{2,1},{3,7},{7,3},{5,4},{4,5},{6,10},{10,6},{8,9},{9,... | collective-permute-start | bytes 552968 | tf_op jit(solution)/shard_map/ppermute | solution.py:390
  28.7 3.6 %collective-permute-start.5 = (f32[9,40,128]{2,1,0:T(8,128)S(1)}, f32[9,40,128]{2,1,0:T(8,128)S(1)}, u32[]{:S(2)}, u32[]{:S(2)}) collective-permute-start(f32[9,40,128]{2,1,0:T(8,128)S(1)} %get-tuple-element.41.refs_0_), channel_id=1, source_target_pairs={{0,1},{1,0},{2,3},{3,2},{7,5},{5,7},{4,6},{6,4},{10,8},{8,10},{9,1... | collective-permute-start | bytes 552968 | tf_op jit(solution)/shard_map/ppermute | solution.py:389
  33.8 7.4 %collective-permute-start.8 = (f32[9,40,128]{2,1,0:T(8,128)S(1)}, f32[9,40,128]{2,1,0:T(8,128)S(1)}, u32[]{:S(2)}, u32[]{:S(2)}) collective-permute-start(f32[9,40,128]{2,1,0:T(8,128)S(1)} %get-tuple-element.47.refs_0_), channel_id=1, source_target_pairs={{0,12},{1,2},{2,1},{3,7},{7,3},{5,4},{4,5},{6,10},{10,6},{8,9},{9,... | collective-permute-start | bytes 552968 | tf_op jit(solution)/shard_map/ppermute | solution.py:390
  37.7 3.6 %collective-permute-start.7 = (f32[9,40,128]{2,1,0:T(8,128)S(1)}, f32[9,40,128]{2,1,0:T(8,128)S(1)}, u32[]{:S(2)}, u32[]{:S(2)}) collective-permute-start(f32[9,40,128]{2,1,0:T(8,128)S(1)} %get-tuple-element.47.refs_0_), channel_id=1, source_target_pairs={{0,1},{1,0},{2,3},{3,2},{7,5},{5,7},{4,6},{6,4},{10,8},{8,10},{9,1... | collective-permute-start | bytes 552968 | tf_op jit(solution)/shard_map/ppermute | solution.py:389
  42.7 1.9 %collective-permute-start.9 = (f32[3,40,128]{2,1,0:T(8,128)S(1)}, f32[3,40,128]{2,1,0:T(8,128)S(1)}, u32[]{:S(2)}, u32[]{:S(2)}) collective-permute-start(f32[3,40,128]{2,1,0:T(8,128)S(1)} %get-tuple-element.50), channel_id=1, source_target_pairs={{0,1},{1,0},{2,3},{3,2},{4,5},{5,4},{6,7},{7,6},{8,9},{9,8},{10,11... | collective-permute-start | bytes 184328 | tf_op jit(solution)/shard_map/ppermute | solution.py:388
  42.8 4.9 %collective-permute-start.10 = (f32[3,40,128]{2,1,0:T(8,128)S(1)}, f32[3,40,128]{2,1,0:T(8,128)S(1)}, u32[]{:S(2)}, u32[]{:S(2)}) collective-permute-start(f32[3,40,128]{2,1,0:T(8,128)S(1)} %get-tuple-element.51), channel_id=1, source_target_pairs={{0,2},{1,3},{2,0},{3,1},{4,6},{5,7},{6,4},{7,5},{8,10},{9,11},{10,... | collective-permute-start | bytes 184328 | tf_op jit(solution)/shard_map/ppermute | solution.py:388
  42.9 5.2 %copy-start.2 = (s32[128]{0:T(128)S(1)}, s32[128]{0:T(128)}, u32[]{:S(2)}) copy-start(s32[128]{0:T(128)} %order_ref.1) | copy-start | bytes 1540
  42.9 5.2 %collective-permute-start.11 = (f32[3,40,128]{2,1,0:T(8,128)S(1)}, f32[3,40,128]{2,1,0:T(8,128)S(1)}, u32[]{:S(2)}, u32[]{:S(2)}) collective-permute-start(f32[3,40,128]{2,1,0:T(8,128)S(1)} %get-tuple-element.52), channel_id=1, source_target_pairs={{0,3},{1,2},{2,1},{3,0},{4,7},{5,6},{6,5},{7,4},{8,11},{9,10},{10,... | collective-permute-start | bytes 184328 | tf_op jit(solution)/shard_map/ppermute | solution.py:388
  48.2 5.8 %collective-permute-start.14 = (f32[16,128]{1,0:T(8,128)S(1)}, f32[16,128]{1,0:T(8,128)S(1)}, u32[]{:S(2)}, u32[]{:S(2)}) collective-permute-start(f32[16,128]{1,0:T(8,128)S(1)} %shard_map.93.own_ref), channel_id=1, source_target_pairs={{0,12},{4,8},{8,4},{12,0},{1,13},{5,9},{9,5},{13,1},{2,14},{6,10},... | collective-permute-start | bytes 24584 | tf_op jit(solution)/shard_map/ppermute | solution.py:435
  52.0 4.5 %collective-permute-start.13 = (f32[16,128]{1,0:T(8,128)S(1)}, f32[16,128]{1,0:T(8,128)S(1)}, u32[]{:S(2)}, u32[]{:S(2)}) collective-permute-start(f32[16,128]{1,0:T(8,128)S(1)} %shard_map.93.own_ref), channel_id=1, source_target_pairs={{0,8},{4,12},{8,0},{12,4},{1,9},{5,13},{9,1},{13,5},{2,10},{6,14},... | collective-permute-start | bytes 24584 | tf_op jit(solution)/shard_map/ppermute | solution.py:435
  53.1 3.7 %collective-permute-start.12 = (f32[16,128]{1,0:T(8,128)S(1)}, f32[16,128]{1,0:T(8,128)S(1)}, u32[]{:S(2)}, u32[]{:S(2)}) collective-permute-start(f32[16,128]{1,0:T(8,128)S(1)} %shard_map.93.own_ref), channel_id=1, source_target_pairs={{0,4},{4,0},{8,12},{12,8},{1,5},{5,1},{9,13},{13,9},{2,6},{6,2},{1... | collective-permute-start | bytes 24584 | tf_op jit(solution)/shard_map/ppermute | solution.py:435

commit v5 on v4

--- a/solution.py
+++ b/solution.py
@@ -19,7 +19,7 @@
 def orders(tiles, n):
     up = list(range(n))
     if tiles == 4 and n == 4:
-        return [up, [3, 1, 0, 2], [2, 0, 1, 3], up[::-1]]
+        return [up, [3, 0, 1, 2], [2, 1, 0, 3], up[::-1]]
     return [up if s % 2 == 0 else up[::-1] for s in range(tiles)]
 
 
@@ -236,7 +236,7 @@
 def phase_kernel(n, stage, bins, nfreq, fields_before, *refs):
     refs = list(refs)
     take = lambda count: [refs.pop(0) for _ in range(count)]
-    own, near, far, table_ref = take(4)
+    own, far, near, table_ref = take(4)
     if stage == 0:
         pc, pr, g_ref = take(3)
     else:
@@ -420,13 +420,13 @@
     some = ((4, npt), F32)
     c, r, idx, gw, f0, e = phase(
         0, 0, [state, state, (field, jnp.int32), (field, F32), some, packed],
-        e, near_to(near), far_to(far), table, c, r, growth,
-    )
-    f1, e = phase(1, 1, [some, packed], e, near_to(e), far_to(e), table, c, r, idx, gw, f0)
+        e, far_to(far), near_to(near), table, c, r, growth,
+    )
+    f1, e = phase(1, 1, [some, packed], e, far_to(e), near_to(e), table, c, r, idx, gw, f0)
     back = ((-(-(dirs + 1) // n), *field), F32)
     fields, own, *backs = phase(
         2, 2, [((16, npt), F32), ((dirs, *field), F32)] + [back] * (n - 1),
-        e, near_to(e), far_to(e), table, c, r, idx, gw, f0, f1,
+        e, far_to(e), near_to(e), table, c, r, idx, gw, f0, f1,
     )
     backs = [swap(x, d) for d, x in zip(peers, backs)]
     (ordered,) = call(functools.partial(order_kernel, n, dirs), [((16, npt), F32)], [], fields, send_order, *backs)

time: 57.6 us -> 57.6 us (level)
  no operation moved by 1% of the time
where the time goes in v5:
time: 57.6 us; the launch traced here: 57.4 us
  waiting for transfers between devices  25.8 us (45%)
  starting transfers between devices  21 us (36%)
  Pallas kernels  9.02 us (16%)
  between operations  0.76 us (1%)
  local copies, waits for them, and re-layouts  0.74 us (1%)
    ppermute x3, starting transfers between devices, on_device(): lax.ppermute(x, ('space', 'spec'), ring_route(tiles, n, True))  11.4 us
    ppermute x3, waiting for transfers between devices, on_device(): lax.ppermute(x, ('space', 'spec'), ring_route(tiles, n, True))  11.3 us
    ppermute x6, waiting for transfers between devices, on_device(): swap = lambda x, d: lax.ppermute(x, 'spec', [(k, k ^ d) for k in range(n)])  10.5 us
    pallas_call x9, Pallas kernels, call(): pl.pallas_call(kernel, out_shape=[jax.ShapeDtypeStruct(shape, dtype) for...  9.02 us
    ppermute x6, starting transfers between devices, on_device(): swap = lambda x, d: lax.ppermute(x, 'spec', [(k, k ^ d) for k in range(n)])  5.06 us
    ppermute x3, starting transfers between devices, on_device(): lax.ppermute(ordered, 'space', [(t, t ^ d) for t in range(tiles)])  4.39 us
    ppermute x3, waiting for transfers between devices, on_device(): lax.ppermute(ordered, 'space', [(t, t ^ d) for t in range(tiles)])  3.06 us
  transfers between devices with their start and end apart: 15, of which 10 were waited for; matrix products, arithmetic and copies ran while one was open for 0% of the time, Pallas kernels for 2%

profile of v5, /device:TPU:0, one launch (start us, length us, event | category | flops | bytes accessed | tf_op | source)
XLA Modules:
  0.0 57.4 jit_solution(1272808755090486241)
XLA Ops:
  0.6 1.8 %shard_map.86 = (f32[7,40,128]{2,1,0:T(8,128)S(1)}, f32[7,40,128]{2,1,0:T(8,128)S(1)}, f32[7,40,128]{2,1,0:T(8,128)S(1)}, f32[7,40,128]{2,1,0:T(8,128)S(1)}) custom-call(f32[9,36,128]{2,1,0:T(8,128)} %e_hbm.1, f32[9,36,128]{2,1,0:T(8,128)} %c_hbm.1, f32[9,36,128]{2,1,0:T(8,128)} %r_hbm.1), custom_call_target="tpu_custom_call" | custom-call | tf_op jit(solution)/shard_map/pallas_call | solution.py:368
  2.4 0.2 shard_map.87
  2.6 0.5 collective-permute-start
  3.1 2.6 %collective-permute-start.1 = (f32[7,40,128]{2,1,0:T(8,128)S(1)}, f32[7,40,128]{2,1,0:T(8,128)S(1)}, u32[]{:S(2)}, u32[]{:S(2)}) collective-permute-start(f32[7,40,128]{2,1,0:T(8,128)S(1)} %get-tuple-element.34), channel_id=1, source_target_pairs={{0,2},{1,3},{2,0},{3,1},{4,6},{5,7},{6,4},{7,5},{8,10},{9,11},{10,... | collective-permute-start | bytes 430088 | tf_op jit(solution)/shard_map/ppermute | solution.py:388
  5.7 4.5 %collective-permute-done.1.rest_2_ = f32[7,40,128]{2,1,0:T(8,128)S(1)} collective-permute-done((f32[7,40,128]{2,1,0:T(8,128)S(1)}, f32[7,40,128]{2,1,0:T(8,128)S(1)}, u32[]{:S(2)}, u32[]{:S(2)}) %collective-permute-start.1) | collective-permute-done | bytes 143392 | tf_op jit(solution)/shard_map/ppermute | solution.py:388
  10.3 2.5 %collective-permute-done.2.rest_3_ = f32[7,40,128]{2,1,0:T(8,128)S(1)} collective-permute-done((f32[7,40,128]{2,1,0:T(8,128)S(1)}, f32[7,40,128]{2,1,0:T(8,128)S(1)}, u32[]{:S(2)}, u32[]{:S(2)}) %collective-permute-start.2) | collective-permute-done | bytes 143392 | tf_op jit(solution)/shard_map/ppermute | solution.py:388
  12.8 0.2 shard_map.88
  13.1 3.8 %collective-permute-start.3 = (f32[19,40,128]{2,1,0:T(8,128)S(1)}, f32[19,40,128]{2,1,0:T(8,128)S(1)}, u32[]{:S(2)}, u32[]{:S(2)}) collective-permute-start(f32[19,40,128]{2,1,0:T(8,128)S(1)} %get-tuple-element.37), channel_id=1, source_target_pairs={{0,12},{1,2},{2,1},{3,7},{7,3},{4,5},{5,4},{6,10},{10,6},{9,8},{8,... | collective-permute-start | bytes 1167368 | tf_op jit(solution)/shard_map/ppermute | solution.py:390
  16.9 0.7 %copy-done.3 = f32[36]{0:T(128)S(1)} copy-done((f32[36]{0:T(128)S(1)}, f32[36]{0:T(128)}, u32[]{:S(2)}) %copy-start.3) | copy-done | bytes 168
  17.5 1.0 %collective-permute-done.4.refs_2_ = f32[18,40,128]{2,1,0:T(8,128)S(1)} collective-permute-done((f32[18,40,128]{2,1,0:T(8,128)S(1)}, f32[18,40,128]{2,1,0:T(8,128)S(1)}, u32[]{:S(2)}, u32[]{:S(2)}) %collective-permute-start.4) | collective-permute-done | bytes 368672 | tf_op jit(solution)/shard_map/ppermute | solution.py:389
  18.5 4.1 %collective-permute-done.3.refs_1_ = f32[19,40,128]{2,1,0:T(8,128)S(1)} collective-permute-done((f32[19,40,128]{2,1,0:T(8,128)S(1)}, f32[19,40,128]{2,1,0:T(8,128)S(1)}, u32[]{:S(2)}, u32[]{:S(2)}) %collective-permute-start.3) | collective-permute-done | bytes 389152 | tf_op jit(solution)/shard_map/ppermute | solution.py:390
  22.7 0.1 broadcast_in_dim.2.refs_3_
  22.7 2.1 %shard_map.89 = (f32[36,40,128]{2,1,0:T(8,128)S(1)}, f32[36,40,128]{2,1,0:T(8,128)S(1)}, s32[40,128]{1,0:T(8,128)S(1)}, f32[40,128]{1,0:T(8,128)S(1)}, f32[4,128]{1,0:T(4,128)S(1)}, /*index=5*/f32[9,40,128]{2,1,0:T(8,128)S(1)}) custom-call(f32[9,40,128]{2,1,0:T(8,128)S(1)} %get-tuple-element.36.refs_0_, f32[19,40,128]{2,1,0:T(8,128)S(1)} %collective-permute-done.3.refs_1_, ...), custom_call_target="tpu_custom_call" | custom-call | tf_op jit(solution)/shard_map/pallas_call | solution.py:368
  25.0 3.8 %collective-permute-start.5 = (f32[9,40,128]{2,1,0:T(8,128)S(1)}, f32[9,40,128]{2,1,0:T(8,128)S(1)}, u32[]{:S(2)}, u32[]{:S(2)}) collective-permute-start(f32[9,40,128]{2,1,0:T(8,128)S(1)} %get-tuple-element.41.refs_0_), channel_id=1, source_target_pairs={{0,12},{1,2},{2,1},{3,7},{7,3},{4,5},{5,4},{6,10},{10,6},{9,8},{8,... | collective-permute-start | bytes 552968 | tf_op jit(solution)/shard_map/ppermute | solution.py:390
  28.8 3.6 %collective-permute-done.5.refs_1_ = f32[9,40,128]{2,1,0:T(8,128)S(1)} collective-permute-done((f32[9,40,128]{2,1,0:T(8,128)S(1)}, f32[9,40,128]{2,1,0:T(8,128)S(1)}, u32[]{:S(2)}, u32[]{:S(2)}) %collective-permute-start.5) | collective-permute-done | bytes 184352 | tf_op jit(solution)/shard_map/ppermute | solution.py:390
  32.4 1.5 %shard_map.90 = (f32[4,128]{1,0:T(4,128)S(1)}, f32[9,40,128]{2,1,0:T(8,128)S(1)}) custom-call(f32[9,40,128]{2,1,0:T(8,128)S(1)} %get-tuple-element.41.refs_0_, f32[9,40,128]{2,1,0:T(8,128)S(1)} %collective-permute-done.5.refs_1_, f32[9,40,128]{2,1,0:T(8,128)S(1)} %collective-permute-done.6.refs_2_, f32[2,40,128]{2,1,0:T(8,128)S(1)} %broadcast_in_dim.2.refs_3_, ...), custom_call_target="tpu_custom_call" | custom-call | tf_op jit(solution)/shard_map/pallas_call | solution.py:368
  33.9 0.1 collective-permute-start.8
  34.0 3.8 %collective-permute-start.7 = (f32[9,40,128]{2,1,0:T(8,128)S(1)}, f32[9,40,128]{2,1,0:T(8,128)S(1)}, u32[]{:S(2)}, u32[]{:S(2)}) collective-permute-start(f32[9,40,128]{2,1,0:T(8,128)S(1)} %get-tuple-element.47.refs_0_), channel_id=1, source_target_pairs={{0,12},{1,2},{2,1},{3,7},{7,3},{4,5},{5,4},{6,10},{10,6},{9,8},{8,... | collective-permute-start | bytes 552968 | tf_op jit(solution)/shard_map/ppermute | solution.py:390
  37.8 3.6 %collective-permute-done.7.refs_1_ = f32[9,40,128]{2,1,0:T(8,128)S(1)} collective-permute-done((f32[9,40,128]{2,1,0:T(8,128)S(1)}, f32[9,40,128]{2,1,0:T(8,128)S(1)}, u32[]{:S(2)}, u32[]{:S(2)}) %collective-permute-start.7) | collective-permute-done | bytes 184352 | tf_op jit(solution)/shard_map/ppermute | solution.py:390
  41.4 1.5 %shard_map.91 = (f32[16,128]{1,0:T(8,128)S(1)}, f32[9,40,128]{2,1,0:T(8,128)S(1)}, f32[3,40,128]{2,1,0:T(8,128)S(1)}, f32[3,40,128]{2,1,0:T(8,128)S(1)}, f32[3,40,128]{2,1,0:T(8,128)S(1)}) custom-call(f32[9,40,128]{2,1,0:T(8,128)S(1)} %get-tuple-element.47.refs_0_, f32[9,40,128]{2,1,0:T(8,128)S(1)} %collective-permute-done.7.refs_1_, ...), custom_call_target="tpu_custom_call" | custom-call | tf_op jit(solution)/shard_map/pallas_call | solution.py:368
  42.9 0.1 collective-permute-start.9
  42.9 0.1 collective-permute-start.10
  43.0 1.8 %collective-permute-start.11 = (f32[3,40,128]{2,1,0:T(8,128)S(1)}, f32[3,40,128]{2,1,0:T(8,128)S(1)}, u32[]{:S(2)}, u32[]{:S(2)}) collective-permute-start(f32[3,40,128]{2,1,0:T(8,128)S(1)} %get-tuple-element.52), channel_id=1, source_target_pairs={{0,3},{1,2},{2,1},{3,0},{4,7},{5,6},{6,5},{7,4},{8,11},{9,10},{10,... | collective-permute-start | bytes 184328 | tf_op jit(solution)/shard_map/ppermute | solution.py:388
  44.8 3.0 %collective-permute-done.10.rest_1_ = f32[3,40,128]{2,1,0:T(8,128)S(1)} collective-permute-done((f32[3,40,128]{2,1,0:T(8,128)S(1)}, f32[3,40,128]{2,1,0:T(8,128)S(1)}, u32[]{:S(2)}, u32[]{:S(2)}) %collective-permute-start.10) | collective-permute-done | bytes 61472 | tf_op jit(solution)/shard_map/ppermute | solution.py:388
  47.8 0.4 collective-permute-done.11.rest_2_
  48.2 0.2 shard_map.93.own_ref
  48.4 3.8 %collective-permute-start.14 = (f32[16,128]{1,0:T(8,128)S(1)}, f32[16,128]{1,0:T(8,128)S(1)}, u32[]{:S(2)}, u32[]{:S(2)}) collective-permute-start(f32[16,128]{1,0:T(8,128)S(1)} %shard_map.93.own_ref), channel_id=1, source_target_pairs={{0,12},{4,8},{8,4},{12,0},{1,13},{5,9},{9,5},{13,1},{2,14},{6,10},... | collective-permute-start | bytes 24584 | tf_op jit(solution)/shard_map/ppermute | solution.py:435
  52.2 0.6 %collective-permute-start.12 = (f32[16,128]{1,0:T(8,128)S(1)}, f32[16,128]{1,0:T(8,128)S(1)}, u32[]{:S(2)}, u32[]{:S(2)}) collective-permute-start(f32[16,128]{1,0:T(8,128)S(1)} %shard_map.93.own_ref), channel_id=1, source_target_pairs={{0,4},{4,0},{8,12},{12,8},{1,5},{5,1},{9,13},{13,9},{2,6},{6,2},{1... | collective-permute-start | bytes 24584 | tf_op jit(solution)/shard_map/ppermute | solution.py:435
  52.8 0.9 %shard_map.92 = f32[9,36,128]{2,1,0:T(8,128)} custom-call(f32[9,40,128]{2,1,0:T(8,128)S(1)} %get-tuple-element.49.e_ref, f32[3,40,128]{2,1,0:T(8,128)S(1)} %collective-permute-done.9.rest_0_, f32[3,40,128]{2,1,0:T(8,128)S(1)} %collective-permute-done.10.rest_1_, f32[3,40,128]{2,1,0:T(8,128)S(1)} %collective-permute-done.11.rest_2_), custom_call_target="tpu_custom_call" | custom-call | tf_op jit(solution)/shard_map/pallas_call | solution.py:368
  53.7 0.2 collective-permute-done.14.rest_2_
  53.8 2.9 %collective-permute-done.13.rest_1_ = f32[16,128]{1,0:T(8,128)S(1)} collective-permute-done((f32[16,128]{1,0:T(8,128)S(1)}, f32[16,128]{1,0:T(8,128)S(1)}, u32[]{:S(2)}, u32[]{:S(2)}) %collective-permute-start.13) | collective-permute-done | bytes 8224 | tf_op jit(solution)/shard_map/ppermute | solution.py:435
  56.7 0.7 %shard_map.94 = f32[12,128]{1,0:T(8,128)} custom-call(f32[16,128]{1,0:T(8,128)S(1)} %shard_map.93.own_ref, f32[16,128]{1,0:T(8,128)S(1)} %collective-permute-done.12.rest_0_, f32[16,128]{1,0:T(8,128)S(1)} %collective-permute-done.13.rest_1_, f32[16,128]{1,0:T(8,128)S(1)} %collective-permute-done.14.rest_2_), custom_call_target="tpu_custom_call" | custom-call | tf_op jit(solution)/shard_map/pallas_call | solution.py:368
  (18 shorter events, 0.2 us)
Async XLA Ops:
  0.6 1.8 %copy-start.1 = (s32[9,128]{1,0:T(8,128)S(1)}, s32[9,128]{1,0:T(8,128)}, u32[]{:S(2)}) copy-start(s32[9,128]{1,0:T(8,128)} %u_ref.1) | copy-start | bytes 13828
  2.4 10.4 %copy-start = (f32[36,128]{1,0:T(8,128)S(1)}, f32[36,128]{1,0:T(8,128)}, u32[]{:S(2)}) copy-start(f32[36,128]{1,0:T(8,128)} %refs_6_.1) | copy-start | bytes 55300
  2.6 3.1 %collective-permute-start = (f32[7,40,128]{2,1,0:T(8,128)S(1)}, f32[7,40,128]{2,1,0:T(8,128)S(1)}, u32[]{:S(2)}, u32[]{:S(2)}) collective-permute-start(f32[7,40,128]{2,1,0:T(8,128)S(1)} %get-tuple-element.33), channel_id=1, source_target_pairs={{0,1},{1,0},{2,3},{3,2},{4,5},{5,4},{6,7},{7,6},{8,9},{9,8},{10,11... | collective-permute-start | bytes 430088 | tf_op jit(solution)/shard_map/ppermute | solution.py:388
  3.1 7.2 %collective-permute-start.1 = (f32[7,40,128]{2,1,0:T(8,128)S(1)}, f32[7,40,128]{2,1,0:T(8,128)S(1)}, u32[]{:S(2)}, u32[]{:S(2)}) collective-permute-start(f32[7,40,128]{2,1,0:T(8,128)S(1)} %get-tuple-element.34), channel_id=1, source_target_pairs={{0,2},{1,3},{2,0},{3,1},{4,6},{5,7},{6,4},{7,5},{8,10},{9,11},{10,... | collective-permute-start | bytes 430088 | tf_op jit(solution)/shard_map/ppermute | solution.py:388
  5.7 7.2 %collective-permute-start.2 = (f32[7,40,128]{2,1,0:T(8,128)S(1)}, f32[7,40,128]{2,1,0:T(8,128)S(1)}, u32[]{:S(2)}, u32[]{:S(2)}) collective-permute-start(f32[7,40,128]{2,1,0:T(8,128)S(1)} %get-tuple-element.35), channel_id=1, source_target_pairs={{0,3},{1,2},{2,1},{3,0},{4,7},{5,6},{6,5},{7,4},{8,11},{9,10},{10,... | collective-permute-start | bytes 430088 | tf_op jit(solution)/shard_map/ppermute | solution.py:388
  13.1 9.6 %collective-permute-start.3 = (f32[19,40,128]{2,1,0:T(8,128)S(1)}, f32[19,40,128]{2,1,0:T(8,128)S(1)}, u32[]{:S(2)}, u32[]{:S(2)}) collective-permute-start(f32[19,40,128]{2,1,0:T(8,128)S(1)} %get-tuple-element.37), channel_id=1, source_target_pairs={{0,12},{1,2},{2,1},{3,7},{7,3},{4,5},{5,4},{6,10},{10,6},{9,8},{8,... | collective-permute-start | bytes 1167368 | tf_op jit(solution)/shard_map/ppermute | solution.py:390
  16.9 1.7 %collective-permute-start.4 = (f32[18,40,128]{2,1,0:T(8,128)S(1)}, f32[18,40,128]{2,1,0:T(8,128)S(1)}, u32[]{:S(2)}, u32[]{:S(2)}) collective-permute-start(f32[18,40,128]{2,1,0:T(8,128)S(1)} %get-tuple-element.38), channel_id=1, source_target_pairs={{0,1},{1,0},{2,3},{3,2},{7,4},{4,7},{5,6},{6,5},{10,9},{9,10},{8,1... | collective-permute-start | bytes 1105928 | tf_op jit(solution)/shard_map/ppermute | solution.py:389
  16.9 0.7 %copy-start.3 = (f32[36]{0:T(128)S(1)}, f32[36]{0:T(128)}, u32[]{:S(2)}) copy-start(f32[36]{0:T(128)} %param.11) | copy-start | bytes 436
  24.9 3.9 %collective-permute-start.6 = (f32[9,40,128]{2,1,0:T(8,128)S(1)}, f32[9,40,128]{2,1,0:T(8,128)S(1)}, u32[]{:S(2)}, u32[]{:S(2)}) collective-permute-start(f32[9,40,128]{2,1,0:T(8,128)S(1)} %get-tuple-element.41.refs_0_), channel_id=1, source_target_pairs={{0,1},{1,0},{2,3},{3,2},{7,4},{4,7},{5,6},{6,5},{10,9},{9,10},{8,1... | collective-permute-start | bytes 552968 | tf_op jit(solution)/shard_map/ppermute | solution.py:389
  25.0 7.4 %collective-permute-start.5 = (f32[9,40,128]{2,1,0:T(8,128)S(1)}, f32[9,40,128]{2,1,0:T(8,128)S(1)}, u32[]{:S(2)}, u32[]{:S(2)}) collective-permute-start(f32[9,40,128]{2,1,0:T(8,128)S(1)} %get-tuple-element.41.refs_0_), channel_id=1, source_target_pairs={{0,12},{1,2},{2,1},{3,7},{7,3},{4,5},{5,4},{6,10},{10,6},{9,8},{8,... | collective-permute-start | bytes 552968 | tf_op jit(solution)/shard_map/ppermute | solution.py:390
  33.9 3.9 %collective-permute-start.8 = (f32[9,40,128]{2,1,0:T(8,128)S(1)}, f32[9,40,128]{2,1,0:T(8,128)S(1)}, u32[]{:S(2)}, u32[]{:S(2)}) collective-permute-start(f32[9,40,128]{2,1,0:T(8,128)S(1)} %get-tuple-element.47.refs_0_), channel_id=1, source_target_pairs={{0,1},{1,0},{2,3},{3,2},{7,4},{4,7},{5,6},{6,5},{10,9},{9,10},{8,1... | collective-permute-start | bytes 552968 | tf_op jit(solution)/shard_map/ppermute | solution.py:389
  34.0 7.4 %collective-permute-start.7 = (f32[9,40,128]{2,1,0:T(8,128)S(1)}, f32[9,40,128]{2,1,0:T(8,128)S(1)}, u32[]{:S(2)}, u32[]{:S(2)}) collective-permute-start(f32[9,40,128]{2,1,0:T(8,128)S(1)} %get-tuple-element.47.refs_0_), channel_id=1, source_target_pairs={{0,12},{1,2},{2,1},{3,7},{7,3},{4,5},{5,4},{6,10},{10,6},{9,8},{8,... | collective-permute-start | bytes 552968 | tf_op jit(solution)/shard_map/ppermute | solution.py:390
  42.9 1.9 %collective-permute-start.9 = (f32[3,40,128]{2,1,0:T(8,128)S(1)}, f32[3,40,128]{2,1,0:T(8,128)S(1)}, u32[]{:S(2)}, u32[]{:S(2)}) collective-permute-start(f32[3,40,128]{2,1,0:T(8,128)S(1)} %get-tuple-element.50), channel_id=1, source_target_pairs={{0,1},{1,0},{2,3},{3,2},{4,5},{5,4},{6,7},{7,6},{8,9},{9,8},{10,11... | collective-permute-start | bytes 184328 | tf_op jit(solution)/shard_map/ppermute | solution.py:388
  42.9 4.9 %collective-permute-start.10 = (f32[3,40,128]{2,1,0:T(8,128)S(1)}, f32[3,40,128]{2,1,0:T(8,128)S(1)}, u32[]{:S(2)}, u32[]{:S(2)}) collective-permute-start(f32[3,40,128]{2,1,0:T(8,128)S(1)} %get-tuple-element.51), channel_id=1, source_target_pairs={{0,2},{1,3},{2,0},{3,1},{4,6},{5,7},{6,4},{7,5},{8,10},{9,11},{10,... | collective-permute-start | bytes 184328 | tf_op jit(solution)/shard_map/ppermute | solution.py:388
  43.0 5.2 %copy-start.2 = (s32[128]{0:T(128)S(1)}, s32[128]{0:T(128)}, u32[]{:S(2)}) copy-start(s32[128]{0:T(128)} %order_ref.1) | copy-start | bytes 1540
  43.0 5.2 %collective-permute-start.11 = (f32[3,40,128]{2,1,0:T(8,128)S(1)}, f32[3,40,128]{2,1,0:T(8,128)S(1)}, u32[]{:S(2)}, u32[]{:S(2)}) collective-permute-start(f32[3,40,128]{2,1,0:T(8,128)S(1)} %get-tuple-element.52), channel_id=1, source_target_pairs={{0,3},{1,2},{2,1},{3,0},{4,7},{5,6},{6,5},{7,4},{8,11},{9,10},{10,... | collective-permute-start | bytes 184328 | tf_op jit(solution)/shard_map/ppermute | solution.py:388
  48.4 5.5 %collective-permute-start.14 = (f32[16,128]{1,0:T(8,128)S(1)}, f32[16,128]{1,0:T(8,128)S(1)}, u32[]{:S(2)}, u32[]{:S(2)}) collective-permute-start(f32[16,128]{1,0:T(8,128)S(1)} %shard_map.93.own_ref), channel_id=1, source_target_pairs={{0,12},{4,8},{8,4},{12,0},{1,13},{5,9},{9,5},{13,1},{2,14},{6,10},... | collective-permute-start | bytes 24584 | tf_op jit(solution)/shard_map/ppermute | solution.py:435
  52.2 4.5 %collective-permute-start.13 = (f32[16,128]{1,0:T(8,128)S(1)}, f32[16,128]{1,0:T(8,128)S(1)}, u32[]{:S(2)}, u32[]{:S(2)}) collective-permute-start(f32[16,128]{1,0:T(8,128)S(1)} %shard_map.93.own_ref), channel_id=1, source_target_pairs={{0,8},{4,12},{8,0},{12,4},{1,9},{5,13},{9,1},{13,5},{2,10},{6,14},... | collective-permute-start | bytes 24584 | tf_op jit(solution)/shard_map/ppermute | solution.py:435
  52.2 4.5 %collective-permute-start.12 = (f32[16,128]{1,0:T(8,128)S(1)}, f32[16,128]{1,0:T(8,128)S(1)}, u32[]{:S(2)}, u32[]{:S(2)}) collective-permute-start(f32[16,128]{1,0:T(8,128)S(1)} %shard_map.93.own_ref), channel_id=1, source_target_pairs={{0,4},{4,0},{8,12},{12,8},{1,5},{5,1},{9,13},{13,9},{2,6},{6,2},{1... | collective-permute-start | bytes 24584 | tf_op jit(solution)/shard_map/ppermute | solution.py:435

commit v6 on v4

--- a/solution.py
+++ b/solution.py
@@ -102,21 +102,21 @@
     ]
     for copy in copies:
         copy.start()
-    for copy in copies:
-        copy.wait()
     at = Spot(n, npt)
     block = at.block((nfreq, npt))
     full = (dirs - 1) // n
     last = [(at.k + a) % n for a in range(3)]
-    for d in range(n):
-        to = subtile_of(at.s, at.k ^ d, n)
-        for a, ref in enumerate((e_ref, c_ref, r_ref)):
+    tos = [subtile_of(at.s, at.k ^ d, n) for d in range(n)]
+    for a, ref in enumerate((e_ref, c_ref, r_ref)):
+        copies[a].wait()
+        for d, to in enumerate(tos):
             for h in range(full):
                 row = None
                 for i in range(n):
                     piece = move(ref[n * h + i], at.shift(i, to))
                     row = piece if row is None else jnp.where(block == i, piece, row)
                 outs[d][full * a + h, :nfreq, :] = row
+    for d, to in enumerate(tos):
         row = None
         for a, ref in enumerate((e_ref, c_ref, r_ref)):
             piece = move(ref[dirs - 1], at.shift(last[a], to))

time: 57.6 us -> 57.6 us (level)
  no operation moved by 1% of the time
where the time goes in v6:
time: 57.6 us; the launch traced here: 57.4 us
  waiting for transfers between devices  25.5 us (44%)
  starting transfers between devices  21.4 us (37%)
  Pallas kernels  8.97 us (16%)
  local copies, waits for them, and re-layouts  0.74 us (1%)
  between operations  0.74 us (1%)
    ppermute x3, starting transfers between devices, on_device(): lax.ppermute(x, ('space', 'spec'), ring_route(tiles, n, True))  11.4 us
    ppermute x3, waiting for transfers between devices, on_device(): lax.ppermute(x, ('space', 'spec'), ring_route(tiles, n, True))  11.3 us
    ppermute x6, waiting for transfers between devices, on_device(): swap = lambda x, d: lax.ppermute(x, 'spec', [(k, k ^ d) for k in range(n)])  10.5 us
    pallas_call x9, Pallas kernels, call(): pl.pallas_call(kernel, out_shape=[jax.ShapeDtypeStruct(shape, dtype) for...  8.97 us
    ppermute x6, starting transfers between devices, on_device(): swap = lambda x, d: lax.ppermute(x, 'spec', [(k, k ^ d) for k in range(n)])  5.06 us
    ppermute x3, starting transfers between devices, on_device(): lax.ppermute(ordered, 'space', [(t, t ^ d) for t in range(tiles)])  4.93 us
    ppermute x3, waiting for transfers between devices, on_device(): lax.ppermute(ordered, 'space', [(t, t ^ d) for t in range(tiles)])  2.73 us
  transfers between devices with their start and end apart: 15, of which 10 were waited for; matrix products, arithmetic and copies ran while one was open for 0% of the time, Pallas kernels for 2%

profile of v6, /device:TPU:0, one launch (start us, length us, event | category | flops | bytes accessed | tf_op | source)
XLA Modules:
  0.0 57.4 jit_solution(2170354273456871852)
XLA Ops:
  0.6 1.7 %shard_map.86 = (f32[7,40,128]{2,1,0:T(8,128)S(1)}, f32[7,40,128]{2,1,0:T(8,128)S(1)}, f32[7,40,128]{2,1,0:T(8,128)S(1)}, f32[7,40,128]{2,1,0:T(8,128)S(1)}) custom-call(f32[9,36,128]{2,1,0:T(8,128)} %e_hbm.1, f32[9,36,128]{2,1,0:T(8,128)} %c_hbm.1, f32[9,36,128]{2,1,0:T(8,128)} %r_hbm.1), custom_call_target="tpu_custom_call" | custom-call | tf_op jit(solution)/shard_map/pallas_call | solution.py:368
  2.4 0.2 shard_map.87
  2.6 0.5 collective-permute-start
  3.1 2.6 %collective-permute-start.1 = (f32[7,40,128]{2,1,0:T(8,128)S(1)}, f32[7,40,128]{2,1,0:T(8,128)S(1)}, u32[]{:S(2)}, u32[]{:S(2)}) collective-permute-start(f32[7,40,128]{2,1,0:T(8,128)S(1)} %get-tuple-element.34), channel_id=1, source_target_pairs={{0,2},{1,3},{2,0},{3,1},{4,6},{5,7},{6,4},{7,5},{8,10},{9,11},{10,... | collective-permute-start | bytes 430088 | tf_op jit(solution)/shard_map/ppermute | solution.py:388
  5.6 0.1 collective-permute-start.2
  5.7 4.5 %collective-permute-done.1.rest_2_ = f32[7,40,128]{2,1,0:T(8,128)S(1)} collective-permute-done((f32[7,40,128]{2,1,0:T(8,128)S(1)}, f32[7,40,128]{2,1,0:T(8,128)S(1)}, u32[]{:S(2)}, u32[]{:S(2)}) %collective-permute-start.1) | collective-permute-done | bytes 143392 | tf_op jit(solution)/shard_map/ppermute | solution.py:388
  10.2 2.5 %collective-permute-done.2.rest_3_ = f32[7,40,128]{2,1,0:T(8,128)S(1)} collective-permute-done((f32[7,40,128]{2,1,0:T(8,128)S(1)}, f32[7,40,128]{2,1,0:T(8,128)S(1)}, u32[]{:S(2)}, u32[]{:S(2)}) %collective-permute-start.2) | collective-permute-done | bytes 143392 | tf_op jit(solution)/shard_map/ppermute | solution.py:388
  12.8 0.2 shard_map.88
  13.0 3.8 %collective-permute-start.4 = (f32[19,40,128]{2,1,0:T(8,128)S(1)}, f32[19,40,128]{2,1,0:T(8,128)S(1)}, u32[]{:S(2)}, u32[]{:S(2)}) collective-permute-start(f32[19,40,128]{2,1,0:T(8,128)S(1)} %get-tuple-element.38), channel_id=1, source_target_pairs={{0,12},{1,2},{2,1},{3,7},{7,3},{5,4},{4,5},{6,10},{10,6},{8,9},{9,... | collective-permute-start | bytes 1167368 | tf_op jit(solution)/shard_map/ppermute | solution.py:390
  16.9 0.7 %copy-done.3 = f32[36]{0:T(128)S(1)} copy-done((f32[36]{0:T(128)S(1)}, f32[36]{0:T(128)}, u32[]{:S(2)}) %copy-start.3) | copy-done | bytes 168
  17.5 1.0 %collective-permute-done.3.refs_1_ = f32[18,40,128]{2,1,0:T(8,128)S(1)} collective-permute-done((f32[18,40,128]{2,1,0:T(8,128)S(1)}, f32[18,40,128]{2,1,0:T(8,128)S(1)}, u32[]{:S(2)}, u32[]{:S(2)}) %collective-permute-start.3) | collective-permute-done | bytes 368672 | tf_op jit(solution)/shard_map/ppermute | solution.py:389
  18.5 4.1 %collective-permute-done.4.refs_2_ = f32[19,40,128]{2,1,0:T(8,128)S(1)} collective-permute-done((f32[19,40,128]{2,1,0:T(8,128)S(1)}, f32[19,40,128]{2,1,0:T(8,128)S(1)}, u32[]{:S(2)}, u32[]{:S(2)}) %collective-permute-start.4) | collective-permute-done | bytes 389152 | tf_op jit(solution)/shard_map/ppermute | solution.py:390
  22.6 0.1 broadcast_in_dim.2.refs_3_
  22.7 2.1 %shard_map.89 = (f32[36,40,128]{2,1,0:T(8,128)S(1)}, f32[36,40,128]{2,1,0:T(8,128)S(1)}, s32[40,128]{1,0:T(8,128)S(1)}, f32[40,128]{1,0:T(8,128)S(1)}, f32[4,128]{1,0:T(4,128)S(1)}, /*index=5*/f32[9,40,128]{2,1,0:T(8,128)S(1)}) custom-call(f32[9,40,128]{2,1,0:T(8,128)S(1)} %get-tuple-element.36.refs_0_, f32[18,40,128]{2,1,0:T(8,128)S(1)} %collective-permute-done.3.refs_1_, ...), custom_call_target="tpu_custom_call" | custom-call | tf_op jit(solution)/shard_map/pallas_call | solution.py:368
  24.9 3.8 %collective-permute-start.6 = (f32[9,40,128]{2,1,0:T(8,128)S(1)}, f32[9,40,128]{2,1,0:T(8,128)S(1)}, u32[]{:S(2)}, u32[]{:S(2)}) collective-permute-start(f32[9,40,128]{2,1,0:T(8,128)S(1)} %get-tuple-element.41.refs_0_), channel_id=1, source_target_pairs={{0,12},{1,2},{2,1},{3,7},{7,3},{5,4},{4,5},{6,10},{10,6},{8,9},{9,... | collective-permute-start | bytes 552968 | tf_op jit(solution)/shard_map/ppermute | solution.py:390
  28.7 3.6 %collective-permute-done.6.refs_2_ = f32[9,40,128]{2,1,0:T(8,128)S(1)} collective-permute-done((f32[9,40,128]{2,1,0:T(8,128)S(1)}, f32[9,40,128]{2,1,0:T(8,128)S(1)}, u32[]{:S(2)}, u32[]{:S(2)}) %collective-permute-start.6) | collective-permute-done | bytes 184352 | tf_op jit(solution)/shard_map/ppermute | solution.py:390
  32.3 1.5 %shard_map.90 = (f32[4,128]{1,0:T(4,128)S(1)}, f32[9,40,128]{2,1,0:T(8,128)S(1)}) custom-call(f32[9,40,128]{2,1,0:T(8,128)S(1)} %get-tuple-element.41.refs_0_, f32[9,40,128]{2,1,0:T(8,128)S(1)} %collective-permute-done.5.refs_1_, f32[9,40,128]{2,1,0:T(8,128)S(1)} %collective-permute-done.6.refs_2_, f32[2,40,128]{2,1,0:T(8,128)S(1)} %broadcast_in_dim.2.refs_3_, ...), custom_call_target="tpu_custom_call" | custom-call | tf_op jit(solution)/shard_map/pallas_call | solution.py:368
  33.8 3.8 %collective-permute-start.8 = (f32[9,40,128]{2,1,0:T(8,128)S(1)}, f32[9,40,128]{2,1,0:T(8,128)S(1)}, u32[]{:S(2)}, u32[]{:S(2)}) collective-permute-start(f32[9,40,128]{2,1,0:T(8,128)S(1)} %get-tuple-element.47.refs_0_), channel_id=1, source_target_pairs={{0,12},{1,2},{2,1},{3,7},{7,3},{5,4},{4,5},{6,10},{10,6},{8,9},{9,... | collective-permute-start | bytes 552968 | tf_op jit(solution)/shard_map/ppermute | solution.py:390
  37.6 3.6 %collective-permute-done.8.refs_2_ = f32[9,40,128]{2,1,0:T(8,128)S(1)} collective-permute-done((f32[9,40,128]{2,1,0:T(8,128)S(1)}, f32[9,40,128]{2,1,0:T(8,128)S(1)}, u32[]{:S(2)}, u32[]{:S(2)}) %collective-permute-start.8) | collective-permute-done | bytes 184352 | tf_op jit(solution)/shard_map/ppermute | solution.py:390
  41.2 1.5 %shard_map.91 = (f32[16,128]{1,0:T(8,128)S(1)}, f32[9,40,128]{2,1,0:T(8,128)S(1)}, f32[3,40,128]{2,1,0:T(8,128)S(1)}, f32[3,40,128]{2,1,0:T(8,128)S(1)}, f32[3,40,128]{2,1,0:T(8,128)S(1)}) custom-call(f32[9,40,128]{2,1,0:T(8,128)S(1)} %get-tuple-element.47.refs_0_, f32[9,40,128]{2,1,0:T(8,128)S(1)} %collective-permute-done.7.refs_1_, ...), custom_call_target="tpu_custom_call" | custom-call | tf_op jit(solution)/shard_map/pallas_call | solution.py:368
  42.7 0.1 collective-permute-start.9
  42.7 0.1 collective-permute-start.10
  42.8 1.8 %collective-permute-start.11 = (f32[3,40,128]{2,1,0:T(8,128)S(1)}, f32[3,40,128]{2,1,0:T(8,128)S(1)}, u32[]{:S(2)}, u32[]{:S(2)}) collective-permute-start(f32[3,40,128]{2,1,0:T(8,128)S(1)} %get-tuple-element.52), channel_id=1, source_target_pairs={{0,3},{1,2},{2,1},{3,0},{4,7},{5,6},{6,5},{7,4},{8,11},{9,10},{10,... | collective-permute-start | bytes 184328 | tf_op jit(solution)/shard_map/ppermute | solution.py:388
  44.6 3.0 %collective-permute-done.10.rest_1_ = f32[3,40,128]{2,1,0:T(8,128)S(1)} collective-permute-done((f32[3,40,128]{2,1,0:T(8,128)S(1)}, f32[3,40,128]{2,1,0:T(8,128)S(1)}, u32[]{:S(2)}, u32[]{:S(2)}) %collective-permute-start.10) | collective-permute-done | bytes 61472 | tf_op jit(solution)/shard_map/ppermute | solution.py:388
  47.6 0.4 collective-permute-done.11.rest_2_
  48.0 0.2 shard_map.93.own_ref
  48.2 3.8 %collective-permute-start.14 = (f32[16,128]{1,0:T(8,128)S(1)}, f32[16,128]{1,0:T(8,128)S(1)}, u32[]{:S(2)}, u32[]{:S(2)}) collective-permute-start(f32[16,128]{1,0:T(8,128)S(1)} %shard_map.93.own_ref), channel_id=1, source_target_pairs={{0,12},{4,8},{8,4},{12,0},{1,13},{5,9},{9,5},{13,1},{2,14},{6,10},... | collective-permute-start | bytes 24584 | tf_op jit(solution)/shard_map/ppermute | solution.py:435
  52.0 1.1 %collective-permute-start.13 = (f32[16,128]{1,0:T(8,128)S(1)}, f32[16,128]{1,0:T(8,128)S(1)}, u32[]{:S(2)}, u32[]{:S(2)}) collective-permute-start(f32[16,128]{1,0:T(8,128)S(1)} %shard_map.93.own_ref), channel_id=1, source_target_pairs={{0,8},{4,12},{8,0},{12,4},{1,9},{5,13},{9,1},{13,5},{2,10},{6,14},... | collective-permute-start | bytes 24584 | tf_op jit(solution)/shard_map/ppermute | solution.py:435
  53.1 0.9 %shard_map.92 = f32[9,36,128]{2,1,0:T(8,128)} custom-call(f32[9,40,128]{2,1,0:T(8,128)S(1)} %get-tuple-element.49.e_ref, f32[3,40,128]{2,1,0:T(8,128)S(1)} %collective-permute-done.9.rest_0_, f32[3,40,128]{2,1,0:T(8,128)S(1)} %collective-permute-done.10.rest_1_, f32[3,40,128]{2,1,0:T(8,128)S(1)} %collective-permute-done.11.rest_2_), custom_call_target="tpu_custom_call" | custom-call | tf_op jit(solution)/shard_map/pallas_call | solution.py:368
  54.0 2.5 %collective-permute-done.13.rest_1_ = f32[16,128]{1,0:T(8,128)S(1)} collective-permute-done((f32[16,128]{1,0:T(8,128)S(1)}, f32[16,128]{1,0:T(8,128)S(1)}, u32[]{:S(2)}, u32[]{:S(2)}) %collective-permute-start.13) | collective-permute-done | bytes 8224 | tf_op jit(solution)/shard_map/ppermute | solution.py:435
  56.5 0.2 collective-permute-done.12.rest_0_
  56.7 0.7 %shard_map.94 = f32[12,128]{1,0:T(8,128)} custom-call(f32[16,128]{1,0:T(8,128)S(1)} %shard_map.93.own_ref, f32[16,128]{1,0:T(8,128)S(1)} %collective-permute-done.12.rest_0_, f32[16,128]{1,0:T(8,128)S(1)} %collective-permute-done.13.rest_1_, f32[16,128]{1,0:T(8,128)S(1)} %collective-permute-done.14.rest_2_), custom_call_target="tpu_custom_call" | custom-call | tf_op jit(solution)/shard_map/pallas_call | solution.py:368
  (18 shorter events, 0.1 us)
Async XLA Ops:
  0.6 1.7 %copy-start.1 = (s32[9,128]{1,0:T(8,128)S(1)}, s32[9,128]{1,0:T(8,128)}, u32[]{:S(2)}) copy-start(s32[9,128]{1,0:T(8,128)} %u_ref.1) | copy-start | bytes 13828
  2.4 10.4 %copy-start = (f32[36,128]{1,0:T(8,128)S(1)}, f32[36,128]{1,0:T(8,128)}, u32[]{:S(2)}) copy-start(f32[36,128]{1,0:T(8,128)} %refs_6_.1) | copy-start | bytes 55300
  2.6 3.1 %collective-permute-start = (f32[7,40,128]{2,1,0:T(8,128)S(1)}, f32[7,40,128]{2,1,0:T(8,128)S(1)}, u32[]{:S(2)}, u32[]{:S(2)}) collective-permute-start(f32[7,40,128]{2,1,0:T(8,128)S(1)} %get-tuple-element.33), channel_id=1, source_target_pairs={{0,1},{1,0},{2,3},{3,2},{4,5},{5,4},{6,7},{7,6},{8,9},{9,8},{10,11... | collective-permute-start | bytes 430088 | tf_op jit(solution)/shard_map/ppermute | solution.py:388
  3.1 7.2 %collective-permute-start.1 = (f32[7,40,128]{2,1,0:T(8,128)S(1)}, f32[7,40,128]{2,1,0:T(8,128)S(1)}, u32[]{:S(2)}, u32[]{:S(2)}) collective-permute-start(f32[7,40,128]{2,1,0:T(8,128)S(1)} %get-tuple-element.34), channel_id=1, source_target_pairs={{0,2},{1,3},{2,0},{3,1},{4,6},{5,7},{6,4},{7,5},{8,10},{9,11},{10,... | collective-permute-start | bytes 430088 | tf_op jit(solution)/shard_map/ppermute | solution.py:388
  5.6 7.2 %collective-permute-start.2 = (f32[7,40,128]{2,1,0:T(8,128)S(1)}, f32[7,40,128]{2,1,0:T(8,128)S(1)}, u32[]{:S(2)}, u32[]{:S(2)}) collective-permute-start(f32[7,40,128]{2,1,0:T(8,128)S(1)} %get-tuple-element.35), channel_id=1, source_target_pairs={{0,3},{1,2},{2,1},{3,0},{4,7},{5,6},{6,5},{7,4},{8,11},{9,10},{10,... | collective-permute-start | bytes 430088 | tf_op jit(solution)/shard_map/ppermute | solution.py:388
  13.0 9.6 %collective-permute-start.4 = (f32[19,40,128]{2,1,0:T(8,128)S(1)}, f32[19,40,128]{2,1,0:T(8,128)S(1)}, u32[]{:S(2)}, u32[]{:S(2)}) collective-permute-start(f32[19,40,128]{2,1,0:T(8,128)S(1)} %get-tuple-element.38), channel_id=1, source_target_pairs={{0,12},{1,2},{2,1},{3,7},{7,3},{5,4},{4,5},{6,10},{10,6},{8,9},{9,... | collective-permute-start | bytes 1167368 | tf_op jit(solution)/shard_map/ppermute | solution.py:390
  16.8 1.7 %collective-permute-start.3 = (f32[18,40,128]{2,1,0:T(8,128)S(1)}, f32[18,40,128]{2,1,0:T(8,128)S(1)}, u32[]{:S(2)}, u32[]{:S(2)}) collective-permute-start(f32[18,40,128]{2,1,0:T(8,128)S(1)} %get-tuple-element.37), channel_id=1, source_target_pairs={{0,1},{1,0},{2,3},{3,2},{7,5},{5,7},{4,6},{6,4},{10,8},{8,10},{9,1... | collective-permute-start | bytes 1105928 | tf_op jit(solution)/shard_map/ppermute | solution.py:389
  16.8 0.7 %copy-start.3 = (f32[36]{0:T(128)S(1)}, f32[36]{0:T(128)}, u32[]{:S(2)}) copy-start(f32[36]{0:T(128)} %param.11) | copy-start | bytes 436
  24.9 7.4 %collective-permute-start.6 = (f32[9,40,128]{2,1,0:T(8,128)S(1)}, f32[9,40,128]{2,1,0:T(8,128)S(1)}, u32[]{:S(2)}, u32[]{:S(2)}) collective-permute-start(f32[9,40,128]{2,1,0:T(8,128)S(1)} %get-tuple-element.41.refs_0_), channel_id=1, source_target_pairs={{0,12},{1,2},{2,1},{3,7},{7,3},{5,4},{4,5},{6,10},{10,6},{8,9},{9,... | collective-permute-start | bytes 552968 | tf_op jit(solution)/shard_map/ppermute | solution.py:390
  28.7 3.6 %collective-permute-start.5 = (f32[9,40,128]{2,1,0:T(8,128)S(1)}, f32[9,40,128]{2,1,0:T(8,128)S(1)}, u32[]{:S(2)}, u32[]{:S(2)}) collective-permute-start(f32[9,40,128]{2,1,0:T(8,128)S(1)} %get-tuple-element.41.refs_0_), channel_id=1, source_target_pairs={{0,1},{1,0},{2,3},{3,2},{7,5},{5,7},{4,6},{6,4},{10,8},{8,10},{9,1... | collective-permute-start | bytes 552968 | tf_op jit(solution)/shard_map/ppermute | solution.py:389
  33.8 7.4 %collective-permute-start.8 = (f32[9,40,128]{2,1,0:T(8,128)S(1)}, f32[9,40,128]{2,1,0:T(8,128)S(1)}, u32[]{:S(2)}, u32[]{:S(2)}) collective-permute-start(f32[9,40,128]{2,1,0:T(8,128)S(1)} %get-tuple-element.47.refs_0_), channel_id=1, source_target_pairs={{0,12},{1,2},{2,1},{3,7},{7,3},{5,4},{4,5},{6,10},{10,6},{8,9},{9,... | collective-permute-start | bytes 552968 | tf_op jit(solution)/shard_map/ppermute | solution.py:390
  37.6 3.6 %collective-permute-start.7 = (f32[9,40,128]{2,1,0:T(8,128)S(1)}, f32[9,40,128]{2,1,0:T(8,128)S(1)}, u32[]{:S(2)}, u32[]{:S(2)}) collective-permute-start(f32[9,40,128]{2,1,0:T(8,128)S(1)} %get-tuple-element.47.refs_0_), channel_id=1, source_target_pairs={{0,1},{1,0},{2,3},{3,2},{7,5},{5,7},{4,6},{6,4},{10,8},{8,10},{9,1... | collective-permute-start | bytes 552968 | tf_op jit(solution)/shard_map/ppermute | solution.py:389
  42.7 1.9 %collective-permute-start.9 = (f32[3,40,128]{2,1,0:T(8,128)S(1)}, f32[3,40,128]{2,1,0:T(8,128)S(1)}, u32[]{:S(2)}, u32[]{:S(2)}) collective-permute-start(f32[3,40,128]{2,1,0:T(8,128)S(1)} %get-tuple-element.50), channel_id=1, source_target_pairs={{0,1},{1,0},{2,3},{3,2},{4,5},{5,4},{6,7},{7,6},{8,9},{9,8},{10,11... | collective-permute-start | bytes 184328 | tf_op jit(solution)/shard_map/ppermute | solution.py:388
  42.7 4.9 %collective-permute-start.10 = (f32[3,40,128]{2,1,0:T(8,128)S(1)}, f32[3,40,128]{2,1,0:T(8,128)S(1)}, u32[]{:S(2)}, u32[]{:S(2)}) collective-permute-start(f32[3,40,128]{2,1,0:T(8,128)S(1)} %get-tuple-element.51), channel_id=1, source_target_pairs={{0,2},{1,3},{2,0},{3,1},{4,6},{5,7},{6,4},{7,5},{8,10},{9,11},{10,... | collective-permute-start | bytes 184328 | tf_op jit(solution)/shard_map/ppermute | solution.py:388
  42.8 5.2 %copy-start.2 = (s32[128]{0:T(128)S(1)}, s32[128]{0:T(128)}, u32[]{:S(2)}) copy-start(s32[128]{0:T(128)} %order_ref.1) | copy-start | bytes 1540
  42.8 5.2 %collective-permute-start.11 = (f32[3,40,128]{2,1,0:T(8,128)S(1)}, f32[3,40,128]{2,1,0:T(8,128)S(1)}, u32[]{:S(2)}, u32[]{:S(2)}) collective-permute-start(f32[3,40,128]{2,1,0:T(8,128)S(1)} %get-tuple-element.52), channel_id=1, source_target_pairs={{0,3},{1,2},{2,1},{3,0},{4,7},{5,6},{6,5},{7,4},{8,11},{9,10},{10,... | collective-permute-start | bytes 184328 | tf_op jit(solution)/shard_map/ppermute | solution.py:388
  48.2 5.8 %collective-permute-start.14 = (f32[16,128]{1,0:T(8,128)S(1)}, f32[16,128]{1,0:T(8,128)S(1)}, u32[]{:S(2)}, u32[]{:S(2)}) collective-permute-start(f32[16,128]{1,0:T(8,128)S(1)} %shard_map.93.own_ref), channel_id=1, source_target_pairs={{0,12},{4,8},{8,4},{12,0},{1,13},{5,9},{9,5},{13,1},{2,14},{6,10},... | collective-permute-start | bytes 24584 | tf_op jit(solution)/shard_map/ppermute | solution.py:435
  52.0 4.5 %collective-permute-start.13 = (f32[16,128]{1,0:T(8,128)S(1)}, f32[16,128]{1,0:T(8,128)S(1)}, u32[]{:S(2)}, u32[]{:S(2)}) collective-permute-start(f32[16,128]{1,0:T(8,128)S(1)} %shard_map.93.own_ref), channel_id=1, source_target_pairs={{0,8},{4,12},{8,0},{12,4},{1,9},{5,13},{9,1},{13,5},{2,10},{6,14},... | collective-permute-start | bytes 24584 | tf_op jit(solution)/shard_map/ppermute | solution.py:435
  53.1 3.7 %collective-permute-start.12 = (f32[16,128]{1,0:T(8,128)S(1)}, f32[16,128]{1,0:T(8,128)S(1)}, u32[]{:S(2)}, u32[]{:S(2)}) collective-permute-start(f32[16,128]{1,0:T(8,128)S(1)} %shard_map.93.own_ref), channel_id=1, source_target_pairs={{0,4},{4,0},{8,12},{12,8},{1,5},{5,1},{9,13},{13,9},{2,6},{6,2},{1... | collective-permute-start | bytes 24584 | tf_op jit(solution)/shard_map/ppermute | solution.py:435
